TPU v7x, 32 devices: a whole 2x2x4 slice. The times are simulated.
32 devices in a mesh: seq: 16 (over z, y, x), tp: 2 (over core).
Axes of the slice: x: 2, y: 2, z: 4, core: 2. Of those that a mesh axis runs over, the one named last changes fastest.
Arguments:
- tokens: bfloat16 [96, 2048], P('seq', 'tp'), may hold values from -6 to 6
- norm_gain: float32 [2048], replicated, may hold values from 0.25 to 4
- w_query: bfloat16 [2048, 2048], P(None, 'tp'), may hold values from -0.125 to 0.125
- w_key_value: bfloat16 [2, 2048, 1024], P(None, None, 'tp'), may hold values from -0.125 to 0.125
- w_out: bfloat16 [2048, 2048], P('tp'), may hold values from -0.125 to 0.125
- kv_pool: bfloat16 [2, 1792, 16, 1024], P(None, 'seq', None, 'tp'), may hold values from -256 to 256
- slot_owner: int32 [1792, 2], P('seq'), may hold values from -1 to 447, as said below
- slot_dest: int32 [1792], P('seq'), may hold values from -1 to 1791, as said below
- lengths: int32 [24], replicated, may hold values from 1 to 7164, as said below
Outputs:
- attn_out: bfloat16 [96, 2048], P('seq', 'tp')
- kv_moved: bfloat16 [2, 1792, 16, 1024], P(None, 'seq', None, 'tp')
Inputs may be any that keep to these rules, and one draw needn't show every extreme that they name: `lengths`: two requests are long, at least 5731 and one of them exactly 7164; the others hold at most 444. `slot_owner`: pages 0 to (lengths[r] + 3) // 16 of every request r are held by exactly one slot each, no other pages by any; a free slot holds (-1, -1). `slot_dest`: -1 where the page stays. Destinations are distinct, each a free slot or a slot whose own page moves. At most 7 slots of one index of seq move to slots of one index of seq, and exactly 7 do for some pair in every draw.
All inputs are finite; a program needn't handle non-finite values.
Results may differ from a plain program's by a relative error of at most 0.024.
The roundings to bfloat16 on the way count: a program that leaves them out, or rounds other values in their place, can miss the bound.
Values may be sent and summed in bfloat16 or wider, within the bound.
No kernel may reach another device: no remote copies, remote signals or barrier semaphores. Data moves between devices by JAX's collectives and lax.ppermute only.
A program may use at most 128 MiB of HBM per device.

v0:
```python
import jax
import jax.numpy as jnp
from jax import lax
from jax.sharding import PartitionSpec as P

HD = 128
STEPS = 4


ROPE_BASE = 1000000.0
NEG_FILL = -1e30
NORM_EPS = 1e-06


def rotate(projected, positions, head_count):
    row_count = projected.shape[0]
    width = projected.shape[1] // head_count
    half_width = width // 2
    heads_view = projected.reshape(row_count, head_count, width)
    frequency = ROPE_BASE ** (-jnp.arange(half_width, dtype=jnp.float32) * 2.0 / width)
    angles = positions.astype(jnp.float32)[:, None] * frequency[None, :]
    cosine = jnp.cos(angles)[:, None, :]
    sine_part = jnp.sin(angles)[:, None, :]
    lower_half = heads_view[:, :, :half_width]
    upper_half = heads_view[:, :, half_width:]
    turned = jnp.concatenate(
        [
            lower_half * cosine - upper_half * sine_part,
            upper_half * cosine + lower_half * sine_part,
        ],
        axis=2,
    )
    return turned.reshape(row_count, head_count * width)


def project_rows(token_block, norm_gain, w_query, w_key_value, lengths):
    row_count = token_block.shape[0]
    row_index = jnp.arange(row_count, dtype=jnp.int32)
    positions = lengths[row_index // STEPS] + row_index % STEPS
    widened = token_block.astype(jnp.float32)
    mean_square = jnp.mean(widened * widened, axis=1, keepdims=True)
    normed = (widened * lax.rsqrt(mean_square + NORM_EPS) * norm_gain[None, :]).astype(jnp.bfloat16)
    queries = jnp.dot(normed, w_query, preferred_element_type=jnp.float32)
    keyval = jnp.einsum("rd,cde->cre", normed, w_key_value, preferred_element_type=jnp.float32)
    queries = rotate(queries, positions, w_query.shape[1] // HD).astype(jnp.bfloat16)
    fresh_key = rotate(keyval[0], positions, w_key_value.shape[2] // HD).astype(jnp.bfloat16)
    fresh_value = keyval[1].astype(jnp.bfloat16)
    return jnp.concatenate([queries, fresh_key, fresh_value], axis=1)


def local(tokens, norm_gain, w_query, w_key_value, w_out, kv_pool, slot_owner, slot_dest, lengths):
    seq_count = lax.axis_size("seq")
    my_index = lax.axis_index("seq")
    row_count = tokens.shape[0]
    slot_count = kv_pool.shape[1]
    page_size = kv_pool.shape[2]
    kv_width = kv_pool.shape[3]
    kv_count = kv_width // HD
    q_width = w_query.shape[1]
    q_count = q_width // HD
    group_size = q_count // kv_count
    request_count = lengths.shape[0]
    own_tokens = lax.all_gather(tokens, "tp", axis=1, tiled=True)
    packed = project_rows(
        lax.all_gather(own_tokens, "seq", axis=0, tiled=True),
        norm_gain,
        w_query,
        w_key_value,
        lengths,
    )
    query_all = packed[:, :q_width]
    key_new = packed[:, q_width : q_width + kv_width]
    value_new = packed[:, q_width + kv_width :]
    owner_req = slot_owner[:, 0]
    owner_page = slot_owner[:, 1]
    occupied = owner_req >= 0
    safe_req = jnp.where(occupied, owner_req, 0)
    base_len = lengths[safe_req]
    offset = jnp.arange(page_size, dtype=jnp.int32)
    position = owner_page[:, None] * page_size + offset[None, :]
    step_of = position - base_len[:, None]
    is_new = occupied[:, None] & (step_of >= 0) & (step_of < STEPS)
    source_row = jnp.where(is_new, safe_req[:, None] * STEPS + step_of, 0)
    fresh_rows = jnp.stack([key_new[source_row], value_new[source_row]])
    written = jnp.where(is_new[None, :, :, None], fresh_rows, kv_pool)
    slot_queries = query_all.reshape(request_count, STEPS, q_width)[safe_req]
    slot_queries = slot_queries.reshape(slot_count, STEPS, kv_count, group_size, HD)
    page_keys = written[0].reshape(slot_count, page_size, kv_count, HD)
    page_values = written[1].reshape(slot_count, page_size, kv_count, HD)
    scores = jnp.einsum(
        "stkgd,spkd->stkgp", slot_queries, page_keys, preferred_element_type=jnp.float32
    ) * HD ** (-0.5)
    step_ids = jnp.arange(STEPS, dtype=jnp.int32)
    visible = occupied[:, None, None] & (
        position[:, None, :] <= base_len[:, None, None] + step_ids[None, :, None]
    )
    visible = visible[:, :, None, None, :]
    scores = jnp.where(visible, scores, NEG_FILL)
    slot_top = jnp.max(scores, axis=4).reshape(slot_count, -1)
    member = owner_req[None, :] == jnp.arange(request_count, dtype=jnp.int32)[:, None]
    req_top = jnp.max(jnp.where(member[:, :, None], slot_top[None, :, :], NEG_FILL), axis=1)
    slot_ref = req_top[safe_req].reshape(slot_count, STEPS, kv_count, group_size, 1)
    weights = jnp.where(visible, jnp.exp(scores - slot_ref), 0.0)
    slot_sum = jnp.sum(weights, axis=4).reshape(slot_count, -1)
    slot_out = jnp.einsum(
        "stkgp,spkd->stkgd",
        weights.astype(jnp.bfloat16),
        page_values,
        preferred_element_type=jnp.float32,
    ).reshape(slot_count, -1)
    member_float = member.astype(jnp.float32)
    req_sum = jnp.dot(member_float, slot_sum, precision=lax.Precision.HIGHEST)
    req_out = jnp.dot(member_float, slot_out, precision=lax.Precision.HIGHEST)
    row_top = req_top.reshape(request_count * STEPS, q_count)
    row_sum = req_sum.reshape(request_count * STEPS, q_count)
    row_out = req_out.reshape(request_count * STEPS, q_width)
    first_own = my_index * row_count
    row_peak = lax.pmax(row_top, "seq")
    rescale = jnp.exp(row_top - row_peak)
    total_all, summed_all = lax.psum(
        (row_sum * rescale, row_out * jnp.repeat(rescale, HD, axis=1)), "seq"
    )
    row_total = lax.dynamic_slice_in_dim(total_all, first_own, row_count, 0)
    row_summed = lax.dynamic_slice_in_dim(summed_all, first_own, row_count, 0)
    attended = (row_summed / jnp.repeat(row_total, HD, axis=1)).astype(jnp.bfloat16)
    partial_out = jnp.dot(attended, w_out, preferred_element_type=jnp.float32)
    attn_out = lax.psum_scatter(
        partial_out.astype(jnp.bfloat16), "tp", scatter_dimension=1, tiled=True
    )
    moving = slot_dest >= 0
    capacity = -(-slot_count // seq_count)
    target_dev = jnp.where(moving, slot_dest // slot_count, -1)
    dev_hot = (target_dev[:, None] == jnp.arange(seq_count, dtype=jnp.int32)[None, :]).astype(
        jnp.int32
    )
    send_rank = jnp.sum((jnp.cumsum(dev_hot, axis=0) - 1) * dev_hot, axis=1)
    buffer_slot = jnp.where(moving, target_dev * capacity + send_rank, -1)
    picker = (
        buffer_slot[None, :] == jnp.arange(seq_count * capacity, dtype=jnp.int32)[:, None]
    ).astype(jnp.bfloat16)
    outgoing = jnp.einsum(
        "bs,cspw->cbpw", picker, written, preferred_element_type=jnp.float32
    ).astype(jnp.bfloat16)
    arrived = lax.all_to_all(outgoing, "seq", split_axis=1, concat_axis=1, tiled=True)
    every_dest = lax.all_gather(slot_dest, "seq", axis=0, tiled=True).reshape(seq_count, slot_count)
    to_me = (every_dest >= 0) & (every_dest // slot_count == my_index)
    arrival_rank = jnp.cumsum(to_me.astype(jnp.int32), axis=1) - 1
    local_slot = every_dest % slot_count
    matches = to_me[:, None, :] & (
        arrival_rank[:, None, :] == jnp.arange(capacity, dtype=jnp.int32)[None, :, None]
    )
    landing = jnp.sum(jnp.where(matches, local_slot[:, None, :], 0), axis=2).reshape(-1)
    filled = jnp.any(matches, axis=2).reshape(-1)
    placer = filled[None, :] & (
        landing[None, :] == jnp.arange(slot_count, dtype=jnp.int32)[:, None]
    )
    incoming = jnp.einsum(
        "lb,cbpw->clpw", placer.astype(jnp.bfloat16), arrived, preferred_element_type=jnp.float32
    ).astype(jnp.bfloat16)
    landed = jnp.any(placer, axis=1)
    kv_moved = jnp.where(
        landed[None, :, None, None],
        incoming,
        jnp.where(moving[None, :, None, None], jnp.zeros_like(written), written),
    )
    return (attn_out, kv_moved)


def solution(mesh):
    in_specs = (
        P("seq", "tp"),
        P(),
        P(None, "tp"),
        P(None, None, "tp"),
        P("tp", None),
        P(None, "seq", None, "tp"),
        P("seq", None),
        P("seq"),
        P(),
    )
    out_specs = (P("seq", "tp"), P(None, "seq", None, "tp"))
    return jax.shard_map(local, mesh=mesh, in_specs=in_specs, out_specs=out_specs, check_vma=False)
```

profile of v0, /device:TPU:5, one launch (start us, length us, event | category | flops | bytes accessed | tf_op | source)
XLA Modules:
  0.0 350.0 jit_solution(8746316704760175440)
XLA Ops:
  7.2 0.8 slice_bitcast_fusion
  8.0 0.7 compare_bitcast_fusion
  8.7 2.4 all_gather.9
  11.0 33.4 %all-gather = bf16[16,6,2048]{2,1,0:T(8,128)(2,1)S(1)} all-gather(bf16[1,6,2048]{2,1,0:T(8,128)(2,1)S(1)} %bitcast.91), channel_id=1, replica_groups=mesh['seq'=16,'tp'=2] {'seq'}, dimensions={0}, use_global_device_ids=true | all-gather | bytes 417792 | tf_op jit(solution)/shard_map/all_gather | solution.py:65
  44.7 3.1 convolution_bitcast_fusion.1
  47.8 1.2 gather_fusion.1
  49.1 1.2 gather_fusion
  50.6 5.5 %gather_fusion.3 = bf16[1792,512]{1,0:T(8,128)(2,1)S(1)} fusion(bf16[96,512]{1,0:T(8,128)(2,1)S(1)} %fusion.20, s32[2048]{0:T(1024)S(1)} %pad_clamp_fusion), kind=kCustom, calls=%fused_computation.3 | custom fusion | bytes 3677184 | tf_op jit(solution)/shard_map/gather | solution.py:84
  56.2 2.2 copy.64
  58.5 0.2 multiply_cosine_fusion
  58.7 0.2 subtract_convert_fusion.1
  59.1 5.5 %gather_fusion.2 = bf16[1792,512]{1,0:T(8,128)(2,1)S(1)} fusion(bf16[96,512]{1,0:T(8,128)(2,1)S(1)} %bitcast.82, s32[2048]{0:T(1024)S(1)} %pad_clamp_fusion), kind=kCustom, calls=%fused_computation.2 | custom fusion | bytes 3677184 | tf_op jit(solution)/shard_map/gather | solution.py:84
  64.7 2.3 copy.63
  67.3 6.2 %maximum_select_fusion = bf16[2,112,16,512]{3,1,2,0:T(8,128)(2,1)S(1)} fusion(bf16[1,112,16,512]{3,1,2,0:T(8,128)(2,1)} %copy.64, bf16[1,112,16,512]{3,1,2,0:T(8,128)(2,1)} %copy.63, bf16[2,112,16,512]{3,2,1,0:T(8,128)(2,1)} %param.14, pred[112,16]{0,1:T(8,128)(4,1)S(1)} %compare_and_fusion.1), kind=kLoop, calls=%fused_computation.6 | loop fusion | flops 3670016 | bytes 11011840 | tf_op jit(solution)/shard_map/jit(_where)/select_n | solution.py:85
  73.6 1.8 copy-done.2
  75.4 1.1 convert_bitcast_fusion
  76.5 3.9 %copy.80 = bf16[2,112,16,512]{3,2,0,1:T(8,128)(2,1)} copy(bf16[2,112,16,512]{3,1,2,0:T(8,128)(2,1)S(1)} %convert_bitcast_fusion) | data formatting | bytes 7340032 | tf_op jit(solution)/shard_map/convert_element_type | solution.py:143
  80.4 8.1 %all-to-all-start = ((bf16[2,112,16,512]{3,2,0,1:T(8,128)(2,1)}), bf16[2,112,16,512]{3,2,0,1:T(8,128)(2,1)}, u32[]{:S(2)}, u32[]{:S(2)}) async-start(bf16[2,112,16,512]{3,2,0,1:T(8,128)(2,1)} %copy.80), calls=%async_computation.1 | async-start | bytes 7340032 | tf_op jit(solution)/shard_map/all_to_all | solution.py:144
  88.5 0.2 all-reduce.3.cloned.1.call-start
  88.8 3.8 %fusion.55 = (bf16[1,112,16,512]{3,1,2,0:T(8,128)(2,1)S(1)}, bf16[1,112,16,512]{3,1,2,0:T(8,128)(2,1)}) fusion(bf16[2,112,16,512]{3,1,2,0:T(8,128)(2,1)} %copy-done.2), kind=kLoop, calls=%fused_computation.118 | loop fusion | bytes 7340032 | tf_op jit(solution)/shard_map/slice | solution.py:89
  92.5 0.9 convolution_bitcast_fusion
  93.5 0.2 subtract_convert_fusion
  93.9 1.5 gather_fusion.4
  95.4 4.2 %reshape.572 = bf16[112,16,4,128]{3,2,0,1:T(4,128)(2,1)} reshape(bf16[1,112,16,512]{3,1,2,0:T(8,128)(2,1)} %get-tuple-element.17) | data formatting | bytes 3670016 | tf_op jit(solution)/shard_map/reshape;squeeze | solution.py:88
  99.8 0.3 compare_and_fusion
  100.1 5.2 %fusion.56 = (f32[112,4,4,2]{1,3,2,0:T(2,128)S(1)}, f32[112,4,4,2,16]{4,1,3,2,0:T(4,128)}) fusion(bf16[112,4,4,2,128]{4,1,3,2,0:T(4,128)(2,1)S(1)} %bitcast.89, bf16[112,16,4,128,1]{3,2,0,1,4:T(4,128)(2,1)} %bitcast.86, pred[112,4,16]{2,1,0:T(4,128)(4,1)S(1)} %compare_and_fusion), kind=kOutput, calls=%fused_computation.119 | convolution fusion | flops 14848512 | bytes 3003392 | tf_op jit(solution)/shard_map/stkgd,spkd->stkgp/dot_general | solution.py:90
  105.3 0.3 copy.70
  105.8 0.8 gather_fusion.5
  106.7 0.4 copy.72
  107.0 3.5 %fusion.13 = f32[112,4,4,2]{1,3,2,0:T(2,128)S(1)} fusion(f32[112,4,4,2,16]{4,1,3,2,0:T(4,128)} %get-tuple-element.33, f32[112,4,4,2]{1,3,2,0:T(2,128)S(1)} %copy.72, pred[112,4,16]{2,1,0:T(4,128)(4,1)S(1)} %compare_and_fusion), kind=kLoop, calls=%fused_computation.21 | loop fusion | flops 168448 | bytes 265216 | tf_op jit(solution)/shard_map/reduce_sum | solution.py:104
  110.6 0.3 copy.75
  111.1 1.6 reshape.571
  112.7 4.1 %fusion.10 = f32[112,4,4,2,128]{4,1,3,2,0:T(4,128)S(1)} fusion(bf16[112,16,4,128,1]{3,2,0,1,4:T(4,128)(2,1)} %bitcast.87, f32[112,4,4,2,16]{4,1,3,2,0:T(4,128)} %get-tuple-element.33, f32[112,4,4,2]{1,3,2,0:T(2,128)S(1)} %copy.72, pred[112,4,16]{2,1,0:T(4,128)(4,1)S(1)} %compare_and_fusion), kind=kOutput, calls=%fused_computation.18 | convolution fusion | flops 14852096 | bytes 3920896 | tf_op jit(solution)/shard_map/stkgp,spkd->stkgd/dot_general | solution.py:105
  116.7 2.3 copy.74
  119.0 2.7 reshape.499
  121.8 0.7 fusion.42
  122.6 86.5 %pmax.7 = f32[96,8]{1,0:T(8,128)S(1)} all-reduce(f32[96,8]{1,0:T(8,128)S(1)} %reshape.501), channel_id=1, replica_groups=mesh['seq'=16,'tp'=2] {'seq'}, use_global_device_ids=true, to_apply=%region_3.4 | all-reduce | flops 768 | bytes 6144 | tf_op jit(solution)/shard_map/pmax | solution.py:118
  209.3 0.8 bitcast_multiply_fusion
  210.3 0.6 dynamic-slice
  211.5 0.3 dynamic-update-slice
  211.8 9.0 %all-reduce = s32[1792]{0:T(1024)S(1)} all-reduce(s32[1792]{0:T(1024)S(1)} %dynamic-update-slice), channel_id=1, replica_groups=mesh['seq'=16,'tp'=2] {'seq'}, use_global_device_ids=true, to_apply=%add | all-reduce | flops 1792 | bytes 14336
  221.2 0.3 reduce_window_sum.22
  221.4 59.8 %psum.15 = f32[96,8]{1,0:T(8,128)S(1)} all-reduce(f32[96,8]{1,0:T(8,128)S(1)} %get-tuple-element.14), channel_id=1, replica_groups=mesh['seq'=16,'tp'=2] {'seq'}, use_global_device_ids=true, to_apply=%region_6.7 | all-reduce | flops 768 | bytes 6144 | tf_op jit(solution)/shard_map/psum | solution.py:120
  281.3 0.2 fusion.26
  282.3 47.2 %all-reduce.3.cloned.1.call-done = f32[96,1024]{1,0:T(8,128)} async-done(((f32[96,1024]{1,0:T(8,128)}), f32[96,1024]{1,0:T(8,128)}) %all-reduce.3.cloned.1.call-update) | async-done | bytes 393232 | tf_op jit(solution)/shard_map/psum | solution.py:120
  329.5 3.5 convolution_convert_fusion
  333.0 6.2 %bitcast_select_fusion = bf16[2,112,16,512]{3,1,2,0:T(8,128)(2,1)S(1)} fusion(bf16[2,112,16,512]{3,1,2,0:T(8,128)(2,1)} %copy-done.2, pred[112]{0:T(512)(128)(4,1)S(1)} %broadcast_compare_fusion.2, pred[112]{0:T(512)(128)(4,1)S(1)} %fusion.29, bf16[2,112,16,512]{3,2,0,1:T(8,128)(2,1)} %all-to-all-done, s32[112]{0:T(128)S(1)} %eq.98, pred[112]{0:T(512)(128)(4,1)S(1)} %and.153), kind=kOutput, calls=%fused_computation.7 | convolution fusion | flops 416571904 | bytes 11010832 | tf_op jit(solution)/shard_map/lb,cbpw->clpw/dot_general | solution.py:157
  339.3 3.9 %copy.82 = bf16[2,112,16,512]{3,2,1,0:T(8,128)(2,1)} copy(bf16[2,112,16,512]{3,1,2,0:T(8,128)(2,1)S(1)} %bitcast_select_fusion) | data formatting | bytes 7340032
  (86 shorter events, 3.7 us)
Async XLA Ops:
  7.2 40.7 %copy-start = (s32[24]{0:T(128)S(1)}, s32[24]{0:T(128)}, u32[]{:S(2)}) copy-start(s32[24]{0:T(128)} %param.17) | copy-start | bytes 292
  7.2 37.5 %copy-start.5 = (f32[2048]{0:T(1024)S(1)}, f32[2048]{0:T(1024)}, u32[]{:S(2)}) copy-start(f32[2048]{0:T(1024)} %param.10) | copy-start | bytes 24580
  47.8 8.4 %copy-start.4 = (f32[2,96,512]{2,1,0:T(8,128)}, f32[2,96,512]{2,1,0:T(8,128)S(1)}, u32[]{:S(2)}) copy-start(f32[2,96,512]{2,1,0:T(8,128)S(1)} %convolution_bitcast_fusion.1) | copy-start | bytes 1179652
  49.1 1.4 copy-start.6
  56.1 2.3 slice-start
  64.7 2.3 copy-start.8
  73.6 1.8 copy-start.2
  80.4 252.6 %all-to-all-start = ((bf16[2,112,16,512]{3,2,0,1:T(8,128)(2,1)}), bf16[2,112,16,512]{3,2,0,1:T(8,128)(2,1)}, u32[]{:S(2)}, u32[]{:S(2)}) async-start(bf16[2,112,16,512]{3,2,0,1:T(8,128)(2,1)} %copy.80), calls=%async_computation.1 | async-start | bytes 7340032 | tf_op jit(solution)/shard_map/all_to_all | solution.py:144
  88.5 241.0 %all-reduce.3.cloned.1.call-start = ((), (), s32[]{:S(2)}) async-start(), calls=%async_computation.2 | async-start | bytes 786432 | tf_op jit(solution)/shard_map/psum | solution.py:120
  88.8 3.8 %copy-start.3 = (bf16[2048,1024]{1,0:T(8,128)(2,1)S(1)}, bf16[2048,1024]{1,0:T(8,128)(2,1)}, u32[]{:S(2)}) copy-start(bf16[2048,1024]{1,0:T(8,128)(2,1)} %param.11) | copy-start | bytes 12582916
  95.4 4.3 %copy-start.7 = (s32[112,2]{0,1:T(2,128)S(1)}, s32[112,2]{0,1:T(2,128)}, u32[]{:S(2)}) copy-start(s32[112,2]{0,1:T(2,128)} %param.15) | copy-start | bytes 2692
  122.5 87.8 %copy-start.10 = (u32[32]{0:T(128)S(1)}, u32[32]{0:T(128)}, u32[]{:S(2)}) copy-start(u32[32]{0:T(128)} %constant.117) | copy-start | bytes 388
  122.5 89.0 %copy-start.9 = (s32[112]{0:T(128)S(1)}, s32[112]{0:T(128)}, u32[]{:S(2)}) copy-start(s32[112]{0:T(128)} %param.16) | copy-start | bytes 1348
  210.2 133.0 %reduce-scatter.2.cloned.1.call-start = ((), (), s32[]{:S(2)}) async-start(), calls=%async_computation.3 | async-start | bytes 49152 | tf_op jit(solution)/shard_map/reduce_scatter | solution.py:127
  339.3 3.9 %copy-start.1 = (s32[24]{0:T(128)S(1)}, s32[24]{0:T(128)}, u32[]{:S(2)}) copy-start(s32[24]{0:T(128)} %param.17) | copy-start | bytes 292
Sparse Core Ops, SparseCore 0:
  210.3 119.1 all-reduce.2
  333.2 9.0 reduce-scatter.1
where the time goes:
time: 354 us; the launch traced here: 350 us
  blocking collectives  191 us (54%)
  local copies, waits for them, and re-layouts  48.2 us (14%)
  waiting for transfers between devices  47.2 us (13%)
  matrix products  24.8 us (7%)
  between operations  15.2 us (4%)
  other arithmetic  15 us (4%)
  starting transfers between devices  8.37 us (2%)
    pmax x1, blocking collectives, local(): row_peak = lax.pmax(row_top, 'seq')  86.5 us
    psum x1, blocking collectives, local(): lax.psum((row_sum * rescale, row_out * jnp.repeat(rescale, HD, axis=1)),...  59.8 us
    psum x1, waiting for transfers between devices, local(): lax.psum((row_sum * rescale, row_out * jnp.repeat(rescale, HD, axis=1)),...  47.2 us
    all_gather x1, blocking collectives, local(): lax.all_gather(own_tokens, 'seq', axis=0, tiled=True)  33.4 us
    gather x2, local copies, waits for them, and re-layouts, local(): fresh_rows = jnp.stack([key_new[source_row], value_new[source_row]])  11 us
    unnamed x1, blocking collectives  8.99 us
    all_to_all x1, starting transfers between devices, local(): lax.all_to_all(outgoing, 'seq', split_axis=1, concat_axis=1, tiled=True)  8.11 us
  transfers between devices with their start and end apart: 3, of which 1 were waited for; matrix products, arithmetic and copies ran while one was open for 15% of the time, Pallas kernels for 0%

commit v1 on v0

v1 whole, which is shorter than its diff:
```python
import functools

import jax
import jax.numpy as jnp
from jax import lax
from jax.experimental import pallas as pl
from jax.experimental.pallas import tpu as pltpu
from jax.sharding import PartitionSpec as P

HD = 128
STEPS = 4
STAT_PARTS = 3

ROPE_BASE = 1000000.0
NEG_FILL = -1e30
NORM_EPS = 1e-06


def rotate(projected, positions, head_count):
    row_count = projected.shape[0]
    width = projected.shape[1] // head_count
    half_width = width // 2
    heads_view = projected.reshape(row_count, head_count, width)
    frequency = ROPE_BASE ** (-jnp.arange(half_width, dtype=jnp.float32) * 2.0 / width)
    angles = positions.astype(jnp.float32)[:, None] * frequency[None, :]
    cosine = jnp.cos(angles)[:, None, :]
    sine_part = jnp.sin(angles)[:, None, :]
    lower_half = heads_view[:, :, :half_width]
    upper_half = heads_view[:, :, half_width:]
    turned = jnp.concatenate(
        [
            lower_half * cosine - upper_half * sine_part,
            upper_half * cosine + lower_half * sine_part,
        ],
        axis=2,
    )
    return turned.reshape(row_count, head_count * width)


def project_rows(token_block, norm_gain, w_query, w_key_value, lengths):
    row_count = token_block.shape[0]
    row_index = jnp.arange(row_count, dtype=jnp.int32)
    positions = lengths[row_index // STEPS] + row_index % STEPS
    widened = token_block.astype(jnp.float32)
    mean_square = jnp.mean(widened * widened, axis=1, keepdims=True)
    normed = (widened * lax.rsqrt(mean_square + NORM_EPS) * norm_gain[None, :]).astype(jnp.bfloat16)
    queries = jnp.dot(normed, w_query, preferred_element_type=jnp.float32)
    keyval = jnp.einsum("rd,cde->cre", normed, w_key_value, preferred_element_type=jnp.float32)
    queries = rotate(queries, positions, w_query.shape[1] // HD).astype(jnp.bfloat16)
    fresh_key = rotate(keyval[0], positions, w_key_value.shape[2] // HD).astype(jnp.bfloat16)
    fresh_value = keyval[1].astype(jnp.bfloat16)
    return queries, fresh_key, fresh_value


def pack_body(slot_count, seq_count, capacity, dest_ref, owner_ref, pool_ref, out_ref, meta_ref, count_ref, sem):
    def clear(i, carry):
        meta_ref[0, i] = -1
        meta_ref[1, i] = -1
        meta_ref[2, i] = 0
        return carry

    lax.fori_loop(0, seq_count * capacity, clear, 0)

    def reset(i, carry):
        count_ref[i] = 0
        return carry

    lax.fori_loop(0, seq_count, reset, 0)

    def send(slot, total):
        dest = dest_ref[slot]
        moving = dest >= 0

        @pl.when(moving)
        def _():
            target = dest // slot_count
            rank = count_ref[target]
            count_ref[target] = rank + 1
            place = target * capacity + rank
            meta_ref[0, place] = dest - target * slot_count
            meta_ref[1, place] = owner_ref[slot * 2]
            meta_ref[2, place] = owner_ref[slot * 2 + 1]
            pltpu.make_async_copy(pool_ref.at[:, slot], out_ref.at[place], sem).start()

        return total + moving.astype(jnp.int32)

    total = lax.fori_loop(0, slot_count, send, 0)

    def finish(i, carry):
        pltpu.make_async_copy(pool_ref.at[:, 0], out_ref.at[0], sem).wait()
        return carry

    lax.fori_loop(0, total, finish, 0)


def pack_pages(kv_pool, slot_dest, slot_owner, seq_count):
    slot_count, page_size, width = kv_pool.shape[1:]
    capacity = -(-slot_count // seq_count)
    places = seq_count * capacity
    return pl.pallas_call(
        functools.partial(pack_body, slot_count, seq_count, capacity),
        out_shape=(
            jax.ShapeDtypeStruct((places, 2, page_size, width), kv_pool.dtype),
            jax.ShapeDtypeStruct((3, places), jnp.int32),
        ),
        in_specs=[
            pl.BlockSpec(memory_space=pltpu.SMEM),
            pl.BlockSpec(memory_space=pltpu.SMEM),
            pl.BlockSpec(memory_space=pl.ANY),
        ],
        out_specs=(
            pl.BlockSpec(memory_space=pl.ANY),
            pl.BlockSpec(memory_space=pltpu.SMEM),
        ),
        scratch_shapes=[pltpu.SMEM((seq_count,), jnp.int32), pltpu.SemaphoreType.DMA],
        name="pack_pages",
    )(slot_dest, slot_owner.reshape(-1), kv_pool)


def place_body(
    slot_count, places, page_size,
    dest_ref, owner_ref, meta_ref, length_ref, pool_ref, arrived_ref, key_ref, value_ref,
    out_ref, landed_ref, patch_ref, zero_ref, sem,
):
    zero_ref[...] = jnp.zeros_like(zero_ref)

    def reset(i, carry):
        landed_ref[i] = 0
        return carry

    lax.fori_loop(0, slot_count, reset, 0)

    def note_patch(count, slot, req, page):
        first = length_ref[jnp.maximum(req, 0)] - page * page_size
        hit = (req >= 0) & (first > -STEPS) & (first < page_size)

        @pl.when(hit)
        def _():
            patch_ref[0, count] = slot
            patch_ref[1, count] = req
            patch_ref[2, count] = first

        return count + hit.astype(jnp.int32)

    def land(place, count):
        slot = meta_ref[0, place]

        @pl.when(slot >= 0)
        def _():
            landed_ref[slot] = 1
            pltpu.make_async_copy(arrived_ref.at[place], out_ref.at[:, slot], sem).start()

        return note_patch(count, slot, jnp.where(slot >= 0, meta_ref[1, place], -1), meta_ref[2, place])

    count = lax.fori_loop(0, places, land, 0)

    def keep(slot, count):
        vacant = landed_ref[slot] == 0
        stays = (dest_ref[slot] < 0) & vacant

        @pl.when(stays)
        def _():
            pltpu.make_async_copy(pool_ref.at[:, slot], out_ref.at[:, slot], sem).start()

        @pl.when((dest_ref[slot] >= 0) & vacant)
        def _():
            pltpu.make_async_copy(zero_ref, out_ref.at[:, slot], sem).start()

        return note_patch(
            count, slot, jnp.where(stays, owner_ref[slot * 2], -1), owner_ref[slot * 2 + 1]
        )

    count = lax.fori_loop(0, slot_count, keep, count)
    pltpu.make_async_copy(pool_ref, out_ref, sem).wait()
    entry = lax.broadcasted_iota(jnp.int32, (page_size, out_ref.shape[3]), 0)

    def patch(i, carry):
        slot = patch_ref[0, i]
        req = patch_ref[1, i]
        first = patch_ref[2, i]
        for which, fresh_ref in ((0, key_ref), (1, value_ref)):
            page = out_ref[which, slot].astype(jnp.float32)
            for step in range(STEPS):
                fresh = fresh_ref[pl.ds(req * STEPS + step, 1), :]
                page = jnp.where(entry == first + step, fresh, page)
            out_ref[which, slot] = page.astype(out_ref.dtype)
        return carry

    lax.fori_loop(0, count, patch, 0)


def place_pages(kv_pool, arrived, meta, slot_dest, slot_owner, lengths, key_new, value_new):
    slot_count, page_size, width = kv_pool.shape[1:]
    places = arrived.shape[0]
    smem = pl.BlockSpec(memory_space=pltpu.SMEM)
    hbm = pl.BlockSpec(memory_space=pl.ANY)
    vmem = pl.BlockSpec(memory_space=pltpu.VMEM)
    return pl.pallas_call(
        functools.partial(place_body, slot_count, places, page_size),
        out_shape=jax.ShapeDtypeStruct(kv_pool.shape, kv_pool.dtype),
        in_specs=[smem, smem, smem, smem, hbm, hbm, vmem, vmem],
        out_specs=vmem,
        scratch_shapes=[
            pltpu.SMEM((slot_count,), jnp.int32),
            pltpu.SMEM((3, slot_count), jnp.int32),
            pltpu.VMEM((2, page_size, width), kv_pool.dtype),
            pltpu.SemaphoreType.DMA,
        ],
        compiler_params=pltpu.CompilerParams(vmem_limit_bytes=32 * 2**20),
        name="place_pages",
    )(
        slot_dest, slot_owner.reshape(-1), meta, lengths, kv_pool, arrived,
        key_new.astype(jnp.float32), value_new.astype(jnp.float32),
    )


def split_parts(value):
    parts = []
    for _ in range(STAT_PARTS):
        part = value.astype(jnp.bfloat16).astype(jnp.float32)
        parts.append(part)
        value = value - part
    return parts


def attend_body(
    kv_count, group_size, seq_count,
    index_ref, query_ref, key_new_ref, value_new_ref, key_req_ref, pool_ref, out_ref,
):
    rows = query_ref.shape[0]
    entries = key_req_ref.shape[1]
    q_count = kv_count * group_size
    stack = rows * group_size
    row = lax.broadcasted_iota(jnp.int32, (stack, 1), 0) % rows
    row_req = row // STEPS
    new_row = lax.broadcasted_iota(jnp.int32, (stack, rows), 1)
    mine = (row_req % seq_count) == index_ref[0]
    new_mask = (new_row // STEPS == row_req) & (new_row <= row) & mine
    lane = lax.broadcasted_iota(jnp.int32, (rows, HD), 1)
    stats = jnp.zeros((rows, HD), jnp.float32)
    for head in range(kv_count):
        cols = slice(head * HD, (head + 1) * HD)
        query = jnp.concatenate(
            [
                query_ref[:, (head * group_size + g) * HD : (head * group_size + g + 1) * HD]
                for g in range(group_size)
            ],
            axis=0,
        )
        contract = (((1,), (1,)), ((), ()))
        old = lax.dot_general(
            query, pool_ref[0, :, cols], contract, preferred_element_type=jnp.float32
        ) * HD ** (-0.5)
        fresh = lax.dot_general(
            query, key_new_ref[:, cols], contract, preferred_element_type=jnp.float32
        ) * HD ** (-0.5)
        old_mask = key_req_ref[...] == row_req
        old = jnp.where(old_mask, old, NEG_FILL)
        fresh = jnp.where(new_mask, fresh, NEG_FILL)
        top = jnp.maximum(
            jnp.max(old, axis=1, keepdims=True), jnp.max(fresh, axis=1, keepdims=True)
        )
        old = jnp.where(old_mask, jnp.exp(old - top), 0.0)
        fresh = jnp.where(new_mask, jnp.exp(fresh - top), 0.0)
        total = jnp.sum(old, axis=1, keepdims=True) + jnp.sum(fresh, axis=1, keepdims=True)
        summed = jnp.dot(
            old.astype(jnp.bfloat16), pool_ref[1, :, cols], preferred_element_type=jnp.float32
        ) + jnp.dot(
            fresh.astype(jnp.bfloat16), value_new_ref[:, cols], preferred_element_type=jnp.float32
        )
        summed = summed / jnp.where(total > 0.0, total, 1.0)
        parts = split_parts(top) + split_parts(total)
        for g in range(group_size):
            at = head * group_size + g
            own = slice(g * rows, (g + 1) * rows)
            out_ref[:, at * HD : (at + 1) * HD] = summed[own].astype(out_ref.dtype)
            for k, part in enumerate(parts):
                stats = jnp.where(lane == k * q_count + at, part[own], stats)
    out_ref[:, q_count * HD :] = stats.astype(out_ref.dtype)


def attend(my_index, seq_count, queries, key_new, value_new, key_req, kv_pool):
    slot_count, page_size, width = kv_pool.shape[1:]
    kv_count = width // HD
    rows, q_width = queries.shape
    vmem = pl.BlockSpec(memory_space=pltpu.VMEM)
    return pl.pallas_call(
        functools.partial(attend_body, kv_count, q_width // width, seq_count),
        out_shape=jax.ShapeDtypeStruct((rows, q_width + HD), jnp.bfloat16),
        in_specs=[pl.BlockSpec(memory_space=pltpu.SMEM)] + [vmem] * 5,
        out_specs=vmem,
        compiler_params=pltpu.CompilerParams(vmem_limit_bytes=40 * 2**20),
        name="attend",
    )(
        my_index.reshape(1).astype(jnp.int32), queries, key_new, value_new, key_req,
        kv_pool.reshape(2, slot_count * page_size, width),
    )


def local(tokens, norm_gain, w_query, w_key_value, w_out, kv_pool, slot_owner, slot_dest, lengths):
    seq_count = lax.axis_size("seq")
    my_index = lax.axis_index("seq")
    row_count = tokens.shape[0]
    page_size = kv_pool.shape[2]
    q_width = w_query.shape[1]
    q_count = q_width // HD
    slot_count = kv_pool.shape[1]

    outgoing, meta = pack_pages(kv_pool, slot_dest, slot_owner, seq_count)
    places = outgoing.shape[0]
    own_tokens = lax.all_gather(tokens, "tp", axis=1, tiled=True)
    all_tokens = lax.all_gather(own_tokens, "seq", axis=0, tiled=True)
    arrived = lax.all_to_all(outgoing, "seq", split_axis=0, concat_axis=0, tiled=True)
    arrived_meta = lax.all_to_all(meta, "seq", split_axis=1, concat_axis=1, tiled=True)

    queries, key_new, value_new = project_rows(all_tokens, norm_gain, w_query, w_key_value, lengths)
    owner_req = slot_owner[:, 0]
    base_len = lengths[jnp.maximum(owner_req, 0)]
    position = slot_owner[:, 1][:, None] * page_size + jnp.arange(page_size, dtype=jnp.int32)[None, :]
    key_req = jnp.where(position < base_len[:, None], owner_req[:, None], -1)
    payload = attend(
        my_index, seq_count, queries, key_new, value_new, key_req.reshape(1, -1), kv_pool
    )
    payload = lax.all_to_all(
        payload.reshape(seq_count, row_count, -1), "seq", split_axis=0, concat_axis=0, tiled=True
    ).astype(jnp.float32)
    stats = payload[:, :, q_width : q_width + 2 * STAT_PARTS * q_count]
    stats = stats.reshape(seq_count, row_count, 2, STAT_PARTS, q_count)
    stats = stats[:, :, :, 0] + stats[:, :, :, 1] + stats[:, :, :, 2]
    tops, sums = stats[:, :, 0], stats[:, :, 1]
    share = sums * jnp.exp(tops - jnp.max(tops, axis=0, keepdims=True))
    share = share / jnp.sum(share, axis=0, keepdims=True)
    outs = payload[:, :, :q_width].reshape(seq_count, row_count, q_count, HD)
    attended = jnp.sum(outs * share[..., None], axis=0).reshape(row_count, q_width)
    partial_out = jnp.dot(attended.astype(jnp.bfloat16), w_out, preferred_element_type=jnp.float32)
    attn_out = lax.psum_scatter(
        partial_out.astype(jnp.bfloat16), "tp", scatter_dimension=1, tiled=True
    )
    kv_moved = place_pages(
        kv_pool, arrived, arrived_meta, slot_dest, slot_owner, lengths, key_new, value_new
    )
    return (attn_out, kv_moved)


def solution(mesh):
    in_specs = (
        P("seq", "tp"),
        P(),
        P(None, "tp"),
        P(None, None, "tp"),
        P("tp", None),
        P(None, "seq", None, "tp"),
        P("seq", None),
        P("seq"),
        P(),
    )
    out_specs = (P("seq", "tp"), P(None, "seq", None, "tp"))
    return jax.shard_map(local, mesh=mesh, in_specs=in_specs, out_specs=out_specs, check_vma=False)
```

time: 354 us -> 304 us (0.86)
  the two profiles are of different devices: /device:TPU:5 before, /device:TPU:14 now
where the time goes in v1:
time: 304 us
  starting transfers between devices  123 us (40%)
  waiting for transfers between devices  69.6 us (23%)
  blocking collectives  55.1 us (18%)
  Pallas kernels  19.4 us (6%)
  between operations  14.3 us (5%)
  local copies, waits for them, and re-layouts  10.4 us (3%)
  matrix products  9.58 us (3%)
    all_to_all x1, starting transfers between devices, local(): lax.all_to_all(meta, 'seq', split_axis=1, concat_axis=1, tiled=True)  116 us
    all_to_all x1, waiting for transfers between devices, local(): lax.all_to_all(outgoing, 'seq', split_axis=0, concat_axis=0, tiled=True)  69.6 us
    all_gather x1, blocking collectives, local(): all_tokens = lax.all_gather(own_tokens, 'seq', axis=0, tiled=True)  31.6 us
    all_to_all x1, blocking collectives, local(): lax.all_to_all(payload.reshape(seq_count, row_count, -1), 'seq', split_ax...  21.5 us
    pallas_call x1, Pallas kernels, place_pages(): pl.pallas_call(functools.partial(place_body, slot_count, places, page_siz...  10.5 us
    all_to_all x1, starting transfers between devices, local(): lax.all_to_all(outgoing, 'seq', split_axis=0, concat_axis=0, tiled=True)  6.91 us
  transfers between devices with their start and end apart: 3, of which 1 were waited for; matrix products, arithmetic and copies ran while one was open for 5% of the time, Pallas kernels for 5%

profile of v1, /device:TPU:14, one launch (start us, length us, event | category | flops | bytes accessed | tf_op | source)
XLA Modules:
  0.0 303.7 jit_solution(422744246860242297)
XLA Ops:
  7.2 0.8 copy.19
  8.0 0.7 reshape.225.owner_ref
  8.7 5.3 %pack_pages.1 = (bf16[112,2,16,512]{3,2,1,0:T(8,128)(2,1)}, s32[3,112]{1,0:T(4,128)}) custom-call(s32[112]{0:T(128)} %dest_ref.3, s32[224]{0:T(256)} %reshape.225.owner_ref, bf16[2,112,16,512]{3,2,1,0:T(8,128)(2,1)} %pool_ref.3), custom_call_target="tpu_custom_call" | custom-call | tf_op jit(solution)/shard_map/pack_pages/pallas_call | solution.py:100
  13.9 0.8 all_to_all.14
  14.7 0.6 copy.20
  15.3 115.6 %all-to-all-start.1 = ((s32[3,16,7]{2,0,1:T(4,128)}), s32[3,16,7]{2,0,1:T(4,128)S(1)}, u32[]{:S(2)}, u32[]{:S(2)}) async-start(s32[3,16,7]{2,0,1:T(4,128)} %copy.20), calls=%async_computation.2 | async-start | bytes 65536 | tf_op jit(solution)/shard_map/all_to_all | solution.py:314
  130.9 0.8 multiply_bitcast_fusion
  131.7 2.0 all_gather.6
  133.7 31.6 %all-gather = bf16[16,6,2048]{2,1,0:T(8,128)(2,1)S(1)} all-gather(bf16[1,6,2048]{2,1,0:T(8,128)(2,1)S(1)} %bitcast.66), channel_id=1, replica_groups=mesh['seq'=16,'tp'=2] {'seq'}, dimensions={0}, use_global_device_ids=true | all-gather | bytes 417792 | tf_op jit(solution)/shard_map/all_gather | solution.py:312
  165.4 0.1 reshape.244
  165.5 0.1 multiply_reduce_fusion
  165.6 3.1 %convolution_bitcast_fusion = f32[2,96,512]{2,1,0:T(8,128)S(1)} fusion(bf16[2,2048,512]{2,1,0:T(8,128)(2,1)} %param.12, f32[96,2048]{1,0:T(8,128)S(1)} %reshape.244, f32[2048]{0:T(1024)S(1)} %copy-done.5, f32[96]{0:T(128)S(1)} %add_rsqrt_fusion), kind=kOutput, calls=%fused_computation.3 | convolution fusion | flops 403243008 | bytes 5382528 | tf_op jit(solution)/shard_map/rd,cde->cre/dot_general | solution.py:48
  168.8 1.2 gather_fusion
  170.0 1.2 gather_fusion.1
  171.3 3.1 %convolution_bitcast_fusion.1 = f32[12,8,8,128]{3,1,2,0:T(8,128)S(1)} fusion(bf16[2048,1024]{1,0:T(8,128)(2,1)} %param.11, f32[96,2048]{1,0:T(8,128)S(1)} %reshape.244, f32[2048]{0:T(1024)S(1)} %copy-done.5, f32[96]{0:T(128)S(1)} %add_rsqrt_fusion), kind=kOutput, calls=%fused_computation.4 | convolution fusion | flops 403243008 | bytes 5382528 | tf_op jit(solution)/shard_map/dot_general | solution.py:47
  174.3 0.1 copy.22
  174.4 0.1 reshape_squeeze.3
  174.5 0.2 multiply_cosine_fusion
  174.7 0.2 subtract_convert_fusion
  175.0 0.2 subtract_convert_fusion.1
  175.2 0.1 pad_maximum_fusion.1
  175.4 0.1 fusion.3
  175.5 0.1 pad_maximum_fusion
  175.6 0.1 select_n.52.key_req_ref
  175.8 0.0 copy-start.1
  175.8 2.0 copy-done.1
  177.8 3.6 %attend.1 = bf16[96,1152]{1,0:T(8,128)(2,1)S(1)} custom-call(s32[1]{0:T(128)} %bitcast.index_ref, bf16[96,1024]{1,0:T(8,128)(2,1)S(1)} %bitcast.61, bf16[96,512]{1,0:T(8,128)(2,1)S(1)} %get-tuple-element.13.key_new_ref, bf16[96,512]{1,0:T(8,128)(2,1)S(1)} %get-tuple-element.7.value_new_ref, s32[1,1792]{1,0:T(1,128)S(1)} %select_n.52.key_req_ref, ...), custom_call_target="tpu_custom_call" | custom-call | tf_op jit(solution)/shard_map/attend/pallas_call | solution.py:287
  181.5 0.1 reshape.223
  181.5 0.0 all-to-all-done.1
  181.5 21.5 %all_to_all.21 = bf16[16,6,1152]{2,1,0:T(8,128)(2,1)S(1)} all-to-all(bf16[16,6,1152]{2,1,0:T(8,128)(2,1)S(1)} %reshape.223), channel_id=1, replica_groups=mesh['seq'=16,'tp'=2] {'seq'}, dimensions={0} | all-to-all | bytes 442368 | tf_op jit(solution)/shard_map/all_to_all | solution.py:324
  203.0 6.9 %all-to-all-start.2 = ((bf16[112,2,16,512]{3,2,1,0:T(8,128)(2,1)}), bf16[112,2,16,512]{3,2,1,0:T(8,128)(2,1)}, u32[]{:S(2)}, u32[]{:S(2)}) async-start(bf16[112,2,16,512]{3,2,1,0:T(8,128)(2,1)} %get-tuple-element.5), calls=%async_computation.3 | async-start | bytes 7340032 | tf_op jit(solution)/shard_map/all_to_all | solution.py:313
  209.9 0.0 copy-start.4
  209.9 0.0 reduce-scatter.2.cloned.1.call-start
  210.0 0.1 copy.16
  210.1 0.1 slice_reduce_fusion
  210.2 0.2 fusion.8
  210.4 0.1 broadcast_divide_fusion
  210.5 0.1 copy.17
  210.5 0.2 mul.152
  210.7 0.1 mul.153
  210.8 0.3 fusion
  211.1 3.4 %convolution_convert_fusion = bf16[6,2048]{1,0:T(8,128)(2,1)} fusion(bf16[1024,2048]{1,0:T(8,128)(2,1)} %param.13, bf16[6,1024]{1,0:T(8,128)(2,1)S(1)} %fusion), kind=kOutput, calls=%fused_computation.2 | convolution fusion | flops 25178112 | bytes 4231168 | tf_op jit(solution)/shard_map/dot_general | solution.py:335
  214.6 0.0 reduce-scatter.2.cloned.1.call-update
  214.6 0.1 all_to_all.16.meta_ref
  214.7 69.6 %all-to-all-done.2.arrived_ref = bf16[112,2,16,512]{3,2,1,0:T(8,128)(2,1)} async-done(((bf16[112,2,16,512]{3,2,1,0:T(8,128)(2,1)}), bf16[112,2,16,512]{3,2,1,0:T(8,128)(2,1)}, u32[]{:S(2)}, u32[]{:S(2)}) %all-to-all-start.2) | async-done | bytes 3670048 | tf_op jit(solution)/shard_map/all_to_all | solution.py:313
  284.3 2.0 copy-done.2
  286.3 10.5 %place_pages.1 = bf16[2,112,16,512]{3,2,1,0:T(8,128)(2,1)} custom-call(s32[112]{0:T(128)S(1)} %copy-done.4, s32[224]{0:T(256)S(1)} %copy-done.3, s32[3,112]{1,0:T(4,128)S(1)} %all_to_all.16.meta_ref, s32[24]{0:T(128)S(1)} %copy-done, bf16[2,112,16,512]{3,2,1,0:T(8,128)(2,1)S(1)} %copy-done.2, bf16[112,2,16,512]{3,2,1,0:T(8,128)(2,1)} %all-to-all-done.2.arrived_ref, ...), custom_call_target="tpu_custom_call" | custom-call | tf_op jit(solution)/shard_map/place_pages/pallas_call | solution.py:198
  296.8 0.0 reduce-scatter.2.cloned.1.call-done
  (22 shorter events, 0.2 us)
Async XLA Ops:
  7.2 158.5 %copy-start.5 = (f32[2048]{0:T(1024)S(1)}, f32[2048]{0:T(1024)}, u32[]{:S(2)}) copy-start(f32[2048]{0:T(1024)} %param.10) | copy-start | bytes 24580
  15.3 166.2 %all-to-all-start.1 = ((s32[3,16,7]{2,0,1:T(4,128)}), s32[3,16,7]{2,0,1:T(4,128)S(1)}, u32[]{:S(2)}, u32[]{:S(2)}) async-start(s32[3,16,7]{2,0,1:T(4,128)} %copy.20), calls=%async_computation.2 | async-start | bytes 65536 | tf_op jit(solution)/shard_map/all_to_all | solution.py:314
  165.4 3.4 %copy-start = (s32[24]{0:T(128)S(1)}, s32[24]{0:T(128)}, u32[]{:S(2)}) copy-start(s32[24]{0:T(128)} %length_ref.1) | copy-start | bytes 292
  175.8 2.0 copy-start.1
  203.0 81.3 %all-to-all-start.2 = ((bf16[112,2,16,512]{3,2,1,0:T(8,128)(2,1)}), bf16[112,2,16,512]{3,2,1,0:T(8,128)(2,1)}, u32[]{:S(2)}, u32[]{:S(2)}) async-start(bf16[112,2,16,512]{3,2,1,0:T(8,128)(2,1)} %get-tuple-element.5), calls=%async_computation.3 | async-start | bytes 7340032 | tf_op jit(solution)/shard_map/all_to_all | solution.py:313
  209.9 74.3 %copy-start.3 = (s32[224]{0:T(256)S(1)}, s32[224]{0:T(256)}, u32[]{:S(2)}) copy-start(s32[224]{0:T(256)} %reshape.225.owner_ref) | copy-start | bytes 2692
  209.9 74.3 %copy-start.4 = (s32[112]{0:T(128)S(1)}, s32[112]{0:T(128)}, u32[]{:S(2)}) copy-start(s32[112]{0:T(128)} %dest_ref.3) | copy-start | bytes 1348
  209.9 86.9 %reduce-scatter.2.cloned.1.call-start = ((), (), s32[]{:S(2)}) async-start(), calls=%async_computation.4 | async-start | bytes 49152 | tf_op jit(solution)/shard_map/reduce_scatter | solution.py:336
  284.3 2.0 copy-start.2
Sparse Core Ops, SparseCore 0:
  214.7 8.5 reduce-scatter.1

commit v2 on v1

v2 whole, which is shorter than its diff:
```python
import functools

import jax
import jax.numpy as jnp
import numpy as np
from jax import lax
from jax.experimental import pallas as pl
from jax.experimental.pallas import tpu as pltpu
from jax.sharding import PartitionSpec as P

HD = 128
STEPS = 4
STAT_PARTS = 3
CHUNK_ROWS = 8
MOST_VMEM = 60 * 2**20
LANES = 128
QUOTIENT_SHIFT = 20

ROPE_BASE = 1000000.0
NEG_FILL = -1e30
NORM_EPS = 1e-06


def rotate(projected, positions, head_count):
    row_count = projected.shape[0]
    width = projected.shape[1] // head_count
    half_width = width // 2
    heads_view = projected.reshape(row_count, head_count, width)
    frequency = ROPE_BASE ** (-jnp.arange(half_width, dtype=jnp.float32) * 2.0 / width)
    angles = positions.astype(jnp.float32)[:, None] * frequency[None, :]
    cosine = jnp.cos(angles)[:, None, :]
    sine_part = jnp.sin(angles)[:, None, :]
    lower_half = heads_view[:, :, :half_width]
    upper_half = heads_view[:, :, half_width:]
    turned = jnp.concatenate(
        [
            lower_half * cosine - upper_half * sine_part,
            upper_half * cosine + lower_half * sine_part,
        ],
        axis=2,
    )
    return turned.reshape(row_count, head_count * width)


def row_ids(row, row_count):
    inner = row % CHUNK_ROWS
    return (row // CHUNK_ROWS) * row_count + inner, inner < row_count


def project_rows(token_block, row_count, norm_gain, w_query, w_key_value, lengths):
    row, held = row_ids(np.arange(token_block.shape[0], dtype=np.int32), row_count)
    row = np.where(held, row, 0)
    positions = length_of(lengths, jnp.asarray(row // STEPS)) + jnp.asarray(row % STEPS)
    widened = token_block.astype(jnp.float32)
    mean_square = jnp.mean(widened * widened, axis=1, keepdims=True)
    normed = (widened * lax.rsqrt(mean_square + NORM_EPS) * norm_gain[None, :]).astype(jnp.bfloat16)
    queries = jnp.dot(normed, w_query, preferred_element_type=jnp.float32)
    keyval = jnp.einsum("rd,cde->cre", normed, w_key_value, preferred_element_type=jnp.float32)
    queries = rotate(queries, positions, w_query.shape[1] // HD).astype(jnp.bfloat16)
    fresh_key = rotate(keyval[0], positions, w_key_value.shape[2] // HD).astype(jnp.bfloat16)
    fresh_value = keyval[1].astype(jnp.bfloat16)
    return queries, fresh_key, fresh_value


def note_body(row_count, stride, token_ref, dest_ref, owner_ref, out_ref, page_ref):
    width = token_ref.shape[1]
    slot_count = dest_ref.shape[1]
    page_ref[...] = jnp.zeros_like(page_ref)
    page_ref[:row_count, :] = token_ref[...].astype(jnp.float32)
    per_row = width // stride
    values = (dest_ref[...], owner_ref[0:1, :], owner_ref[1:2, :])
    for k, value in enumerate(values):
        for part, digit in enumerate(((value + 1) >> 7, (value + 1) & 127)):
            field = 2 * k + part
            row = row_count + field // per_row
            lane = (field % per_row) * stride
            page_ref[row : row + 1, lane : lane + slot_count] = digit.astype(jnp.float32)
    for target in range(out_ref.shape[0]):
        out_ref[target] = page_ref[...].astype(out_ref.dtype)


def make_notes(tokens, slot_owner, slot_dest, seq_count):
    row_count, width = tokens.shape
    slot_count = slot_dest.shape[0]
    stride = -(-slot_count // LANES) * LANES
    used = row_count + -(-6 // (width // stride))
    rows = -(-used // CHUNK_ROWS) * CHUNK_ROWS
    vmem = pl.BlockSpec(memory_space=pltpu.VMEM)
    return pl.pallas_call(
        functools.partial(note_body, row_count, stride),
        out_shape=jax.ShapeDtypeStruct((seq_count, rows, width), tokens.dtype),
        in_specs=[vmem] * 3,
        out_specs=vmem,
        scratch_shapes=[pltpu.VMEM((rows, width), jnp.float32)],
        name="make_notes",
    )(tokens, slot_dest.reshape(1, -1), slot_owner.T)


def gather_notes(tokens, slot_owner, slot_dest, seq_count):
    inner = 1 << ((seq_count.bit_length() - 1) // 2)
    outer = seq_count // inner
    assert inner * outer == seq_count
    lines = [[o * inner + i for o in range(outer)] for i in range(inner)]
    planes = [[o * inner + i for i in range(inner)] for o in range(outer)]
    note = make_notes(tokens, slot_owner, slot_dest, outer)
    rows, width = note.shape[1:]
    along = lax.all_to_all(
        note, "seq", split_axis=0, concat_axis=0, axis_index_groups=lines, tiled=True
    )
    along = jnp.broadcast_to(along[None], (inner, outer, rows, width))
    across = lax.all_to_all(
        along, "seq", split_axis=0, concat_axis=0, axis_index_groups=planes, tiled=True
    )
    return jnp.swapaxes(across, 0, 1).reshape(seq_count, rows, width)


def read_notes(notes, row_count, slot_count):
    seq_count, rows, width = notes.shape
    stride = -(-slot_count // LANES) * LANES
    fields = notes[:, row_count:].reshape(seq_count, -1)[:, : 6 * stride]
    fields = fields.astype(jnp.float32).astype(jnp.int32).reshape(seq_count, 6, stride)
    fields = fields[:, :, :slot_count]
    return [fields[:, 2 * k] * 128 + fields[:, 2 * k + 1] - 1 for k in range(3)]


PACK_CUTS = 4


def wait_pages(group_ref, page_ref, group, total, sem):
    def many(i, carry):
        pltpu.make_async_copy(group_ref, group_ref, sem).wait()
        return carry

    def one(i, carry):
        pltpu.make_async_copy(page_ref, page_ref, sem).wait()
        return carry

    lax.fori_loop(0, total // group, many, 0)
    lax.fori_loop(0, total % group, one, 0)


def pack_body(
    slot_count, seq_count, capacity, dest_ref, pool_ref, out_ref, held_ref, count_ref, load_sem, send_sem
):
    scale = -(-(1 << QUOTIENT_SHIFT) // slot_count)
    last = seq_count * slot_count - 1
    assert last * (scale * slot_count - (1 << QUOTIENT_SHIFT)) < 1 << QUOTIENT_SHIFT
    assert last * scale < 1 << 31

    edges = [slot_count * cut // PACK_CUTS for cut in range(PACK_CUTS + 1)]
    loads = []
    for cut in range(PACK_CUTS):
        span = pl.ds(edges[cut], edges[cut + 1] - edges[cut])
        load = pltpu.make_async_copy(pool_ref.at[:, span], held_ref.at[:, span], load_sem.at[cut])
        load.start()
        loads.append(load)

    def reset(target, carry):
        count_ref[target] = 0
        return carry

    lax.fori_loop(0, seq_count, reset, 0)

    def send(slot, total):
        dest = dest_ref[slot]

        @pl.when(dest >= 0)
        def _():
            target = (dest * scale) >> QUOTIENT_SHIFT
            rank = count_ref[target]
            count_ref[target] = rank + 1
            pltpu.make_async_copy(
                held_ref.at[:, slot], out_ref.at[target, pl.ds(2 * rank, 2)], send_sem
            ).start()

        return total + (dest >= 0).astype(jnp.int32)

    total = 0
    for cut, load in enumerate(loads):
        load.wait()
        total = lax.fori_loop(edges[cut], edges[cut + 1], send, total)
    wait_pages(out_ref.at[0], out_ref.at[0, pl.ds(0, 2)], capacity, total, send_sem)


def pack_pages(kv_pool, slot_dest, seq_count, capacity):
    slot_count, page_size, width = kv_pool.shape[1:]
    block = (seq_count, 2 * capacity, page_size, width)
    hbm = pl.BlockSpec(memory_space=pltpu.HBM)
    return pl.pallas_call(
        functools.partial(pack_body, slot_count, seq_count, capacity),
        out_shape=jax.ShapeDtypeStruct(block, kv_pool.dtype),
        in_specs=[pl.BlockSpec(memory_space=pltpu.SMEM), hbm],
        out_specs=hbm,
        scratch_shapes=[
            pltpu.VMEM(kv_pool.shape, kv_pool.dtype),
            pltpu.SMEM((seq_count,), jnp.int32),
            pltpu.SemaphoreType.DMA((PACK_CUTS,)),
            pltpu.SemaphoreType.DMA,
        ],
        compiler_params=pltpu.CompilerParams(vmem_limit_bytes=MOST_VMEM),
        name="pack_pages",
    )(slot_dest, kv_pool)


def patched(page, fresh_ref, row_count, req, first):
    entry = lax.broadcasted_iota(jnp.int32, page.shape, 0)
    page = page.astype(jnp.float32)
    for step in range(STEPS):
        row = req * STEPS + step
        at = (row // row_count) * CHUNK_ROWS + row % row_count
        page = jnp.where(entry == first + step, fresh_ref[pl.ds(at, 1), :], page)
    return page.astype(jnp.bfloat16)


KEPT, BLANK, LANDED = 0, 1, 2


def keep_body(row_count, table_ref, pool_ref, key_ref, value_ref, out_ref, mark_ref):
    mark_ref[...] = jnp.zeros_like(mark_ref)

    def fill(slot, carry):
        kind = table_ref[0, slot]
        req = table_ref[2, slot]

        @pl.when(kind == KEPT)
        def _():
            out_ref[0, slot] = pool_ref[0, slot]
            out_ref[1, slot] = pool_ref[1, slot]

        @pl.when(kind == BLANK)
        def _():
            blank = jnp.zeros(out_ref.shape[2:], out_ref.dtype)
            out_ref[0, slot] = blank
            out_ref[1, slot] = blank

        @pl.when((req >= 0) & (kind == KEPT))
        def _():
            first = table_ref[3, slot]
            for which, fresh_ref in ((0, key_ref), (1, value_ref)):
                out_ref[which, slot] = patched(
                    out_ref[which, slot], fresh_ref, row_count, req, first
                )

        return carry

    lax.fori_loop(0, table_ref.shape[1], fill, 0)


MARK = jax.ShapeDtypeStruct((CHUNK_ROWS, LANES), jnp.float32)


def place_kept(row_count, table, kv_pool, key_new, value_new):
    vmem = pl.BlockSpec(memory_space=pltpu.VMEM)
    return pl.pallas_call(
        functools.partial(keep_body, row_count),
        out_shape=(jax.ShapeDtypeStruct(kv_pool.shape, kv_pool.dtype), MARK),
        in_specs=[pl.BlockSpec(memory_space=pltpu.SMEM)] + [vmem] * 3,
        out_specs=(vmem, vmem),
        compiler_params=pltpu.CompilerParams(vmem_limit_bytes=40 * 2**20),
        name="place_kept",
    )(table, kv_pool, key_new, value_new)


def land_body(
    row_count, capacity, table_ref, arrived_ref, key_ref, value_ref, begun_ref, out_ref, mark_ref,
    held_ref, stage_ref, load_sem, sem,
):
    load = pltpu.make_async_copy(arrived_ref, held_ref, load_sem)
    load.start()
    mark_ref[...] = jnp.zeros_like(mark_ref)
    load.wait()

    def send(slot, count):
        landed = table_ref[0, slot] == LANDED
        base = table_ref[1, slot]
        req = table_ref[2, slot]

        @pl.when(landed & (req < 0))
        def _():
            pltpu.make_async_copy(held_ref.at[pl.ds(base, 2)], out_ref.at[:, slot], sem).start()

        @pl.when(landed & (req >= 0))
        def _():
            first = table_ref[3, slot]
            for which, fresh_ref in ((0, key_ref), (1, value_ref)):
                stage_ref[slot, which] = patched(
                    held_ref[base + which], fresh_ref, row_count, req, first
                )
            pltpu.make_async_copy(stage_ref.at[slot], out_ref.at[:, slot], sem).start()

        return count + landed.astype(jnp.int32)

    count = lax.fori_loop(0, table_ref.shape[1], send, 0)
    wait_pages(stage_ref.at[pl.ds(0, capacity)], stage_ref.at[0], capacity, count, sem)


def place_landed(row_count, capacity, table, begun, arrived, key_new, value_new):
    slot_count, page_size, width = begun.shape[1:]
    vmem = pl.BlockSpec(memory_space=pltpu.VMEM)
    hbm = pl.BlockSpec(memory_space=pltpu.HBM)
    arrived = arrived.reshape(-1, page_size, width)
    return pl.pallas_call(
        functools.partial(land_body, row_count, capacity),
        out_shape=(jax.ShapeDtypeStruct(begun.shape, begun.dtype), MARK),
        in_specs=[pl.BlockSpec(memory_space=pltpu.SMEM), hbm, vmem, vmem, hbm],
        out_specs=(hbm, vmem),
        scratch_shapes=[
            pltpu.VMEM(arrived.shape, begun.dtype),
            pltpu.VMEM((slot_count, 2, page_size, width), begun.dtype),
            pltpu.SemaphoreType.DMA,
            pltpu.SemaphoreType.DMA,
        ],
        input_output_aliases={4: 0},
        compiler_params=pltpu.CompilerParams(vmem_limit_bytes=MOST_VMEM),
        name="place_landed",
    )(table, arrived, key_new, value_new, begun)


def split_parts(value):
    parts = []
    for _ in range(STAT_PARTS):
        part = value.astype(jnp.bfloat16).astype(jnp.float32)
        parts.append(part)
        value = value - part
    return parts


def attend_body(
    kv_count, group_size, seq_count, row_count,
    index_ref, mark_ref, query_ref, key_new_ref, value_new_ref, key_req_ref, pool_ref,
    out_ref, whole_ref,
):
    rows = query_ref.shape[0]
    width = kv_count * HD
    slot_count, page_size = pool_ref.shape[1:3]
    q_count = kv_count * group_size
    stack = rows * group_size
    row, held = row_ids(lax.broadcasted_iota(jnp.int32, (stack, 1), 0) % rows, row_count)
    row_req = jnp.where(held, row // STEPS, -2)
    new_row, new_held = row_ids(lax.broadcasted_iota(jnp.int32, (stack, rows), 1), row_count)
    mine = (row_req % seq_count) == index_ref[0]
    new_mask = (new_row // STEPS == row_req) & new_held & (new_row <= row) & mine
    stride = width // CHUNK_ROWS
    lane = lax.broadcasted_iota(jnp.int32, (rows, LANES), 1) % stride
    stats = jnp.zeros((rows, LANES), jnp.float32)
    for head in range(kv_count):
        cols = slice(head * HD, (head + 1) * HD)
        query = jnp.concatenate(
            [
                query_ref[:, (head * group_size + g) * HD : (head * group_size + g + 1) * HD]
                for g in range(group_size)
            ],
            axis=0,
        )
        contract = (((1,), (1,)), ((), ()))
        old_key = pool_ref[0, :, :, cols].reshape(slot_count * page_size, HD)
        old_value = pool_ref[1, :, :, cols].reshape(slot_count * page_size, HD)
        old = lax.dot_general(
            query, old_key, contract, preferred_element_type=jnp.float32
        ) * HD ** (-0.5)
        fresh = lax.dot_general(
            query, key_new_ref[:, cols], contract, preferred_element_type=jnp.float32
        ) * HD ** (-0.5)
        old_mask = key_req_ref[...] == row_req
        old = jnp.where(old_mask, old, NEG_FILL)
        fresh = jnp.where(new_mask, fresh, NEG_FILL)
        top = jnp.maximum(
            jnp.max(old, axis=1, keepdims=True), jnp.max(fresh, axis=1, keepdims=True)
        )
        old = jnp.where(old_mask, jnp.exp(old - top), 0.0)
        fresh = jnp.where(new_mask, jnp.exp(fresh - top), 0.0)
        total = jnp.sum(old, axis=1, keepdims=True) + jnp.sum(fresh, axis=1, keepdims=True)
        summed = jnp.dot(
            old.astype(jnp.bfloat16), old_value, preferred_element_type=jnp.float32
        ) + jnp.dot(
            fresh.astype(jnp.bfloat16), value_new_ref[:, cols], preferred_element_type=jnp.float32
        )
        summed = summed / jnp.where(total > 0.0, total, 1.0)
        parts = split_parts(top) + split_parts(total)
        for g in range(group_size):
            at = head * group_size + g
            own = slice(g * rows, (g + 1) * rows)
            whole_ref[:, at * HD : (at + 1) * HD] = summed[own]
            for k, part in enumerate(parts):
                stats = jnp.where(lane == k * q_count + at, part[own], stats)
    stats = jnp.concatenate([stats] * (width // LANES), axis=1)
    place = lax.broadcasted_iota(jnp.int32, (CHUNK_ROWS, width), 1) // stride
    chunk_row = lax.broadcasted_iota(jnp.int32, (CHUNK_ROWS, width), 0)
    for chunk in range(seq_count):
        span = slice(chunk * CHUNK_ROWS, (chunk + 1) * CHUNK_ROWS)
        line = jnp.sum(jnp.where(place == chunk_row, stats[span], 0.0), axis=0, keepdims=True)
        pieces = [whole_ref[span, g * width : (g + 1) * width] for g in range(group_size)]
        pieces[0] = jnp.where(chunk_row == row_count, line, pieces[0])
        out_ref[chunk] = jnp.concatenate(pieces, axis=0).astype(out_ref.dtype)


def attend(
    my_index, seq_count, row_count, mark, queries, key_new, value_new, key_req, kv_pool
):
    slot_count, page_size, width = kv_pool.shape[1:]
    kv_count = width // HD
    rows, q_width = queries.shape
    group_size = q_width // width
    assert group_size * CHUNK_ROWS == page_size and row_count < CHUNK_ROWS
    assert 2 * STAT_PARTS * kv_count * group_size <= width // CHUNK_ROWS
    smem = pl.BlockSpec(memory_space=pltpu.SMEM)
    vmem = pl.BlockSpec(memory_space=pltpu.VMEM)
    return pl.pallas_call(
        functools.partial(attend_body, kv_count, group_size, seq_count, row_count),
        out_shape=jax.ShapeDtypeStruct((seq_count, page_size, width), jnp.bfloat16),
        in_specs=[smem, pl.BlockSpec(memory_space=pl.ANY)] + [vmem] * 5,
        out_specs=vmem,
        scratch_shapes=[pltpu.VMEM((rows, q_width), jnp.float32)],
        compiler_params=pltpu.CompilerParams(vmem_limit_bytes=48 * 2**20),
        name="attend",
    )(
        my_index.reshape(1).astype(jnp.int32), mark, queries, key_new, value_new, key_req, kv_pool
    )


WEIGHT_CUTS = 4


def combine_body(q_count, row_count, mark_ref, part_ref, weight_ref, out_ref, held_ref, load_sem):
    depth = weight_ref.shape[0] // min(WEIGHT_CUTS, q_count)
    loads = []
    for cut in range(weight_ref.shape[0] // depth):
        span = pl.ds(cut * depth, depth)
        load = pltpu.make_async_copy(weight_ref.at[span], held_ref.at[span], load_sem.at[cut])
        load.start()
        loads.append(load)
    seq_count, page_size, width = part_ref.shape
    stride = width // CHUNK_ROWS
    place = lax.broadcasted_iota(jnp.int32, (CHUNK_ROWS, width), 1) // stride
    chunk_row = lax.broadcasted_iota(jnp.int32, (CHUNK_ROWS, width), 0)
    tops, sums = [], []
    for sender in range(seq_count):
        line = part_ref[sender, :CHUNK_ROWS, :].astype(jnp.float32)[row_count : row_count + 1]
        stats = jnp.where(place == chunk_row, line, 0.0)
        shift = width // 2
        while shift >= stride:
            stats = stats + pltpu.roll(stats, shift, 1)
            shift //= 2
        pieces = [stats[:, k * q_count : (k + 1) * q_count] for k in range(2 * STAT_PARTS)]
        tops.append(sum(pieces[1:STAT_PARTS], pieces[0]))
        sums.append(sum(pieces[STAT_PARTS + 1 :], pieces[STAT_PARTS]))
    peak = functools.reduce(jnp.maximum, tops)
    shares = [total * jnp.exp(top - peak) for top, total in zip(tops, sums)]
    whole = sum(shares[1:], shares[0])
    inverse = 1.0 / jnp.where(whole > 0.0, whole, 1.0)
    shares = [share * inverse for share in shares]
    attended = []
    for head in range(q_count):
        half = head * HD // width
        lane = head * HD - half * width
        acc = jnp.zeros((CHUNK_ROWS, HD), jnp.float32)
        for sender in range(seq_count):
            block = part_ref[sender, half * CHUNK_ROWS : (half + 1) * CHUNK_ROWS, lane : lane + HD]
            acc = acc + block.astype(jnp.float32) * shares[sender][:, head : head + 1]
        attended.append(acc.astype(jnp.bfloat16))
    attended = jnp.concatenate(attended, axis=1)
    total = jnp.zeros(out_ref.shape, jnp.float32)
    for cut, load in enumerate(loads):
        load.wait()
        span = slice(cut * depth, (cut + 1) * depth)
        total = total + jnp.dot(
            attended[:, span], held_ref[span, :], preferred_element_type=jnp.float32
        )
    out_ref[...] = total.astype(out_ref.dtype)


def combine(mark, arrived, w_out, row_count):
    vmem = pl.BlockSpec(memory_space=pltpu.VMEM)
    return pl.pallas_call(
        functools.partial(combine_body, w_out.shape[0] // HD, row_count),
        out_shape=jax.ShapeDtypeStruct((CHUNK_ROWS, w_out.shape[1]), jnp.bfloat16),
        in_specs=[
            pl.BlockSpec(memory_space=pl.ANY), vmem, pl.BlockSpec(memory_space=pltpu.HBM)
        ],
        out_specs=vmem,
        scratch_shapes=[
            pltpu.VMEM(w_out.shape, w_out.dtype),
            pltpu.SemaphoreType.DMA((WEIGHT_CUTS,)),
        ],
        compiler_params=pltpu.CompilerParams(vmem_limit_bytes=MOST_VMEM),
        name="combine",
    )(mark, arrived, w_out)


def length_of(lengths, request):
    hot = request[..., None] == jnp.arange(lengths.shape[0], dtype=jnp.int32)
    return jnp.sum(jnp.where(hot, lengths, 0), axis=-1)


def slot_table(notes, row_count, my_index, capacity, slot_owner, slot_dest, lengths, page_size):
    seq_count = notes.shape[0]
    slot_count = slot_dest.shape[0]
    dest, req, page = read_notes(notes, row_count, slot_count)
    sender = jnp.arange(seq_count, dtype=jnp.int32)[:, None]
    inner = dest - my_index * slot_count
    to_me = (inner >= 0) & (inner < slot_count)
    rank = jnp.cumsum(to_me.astype(jnp.int32), axis=1) - 1
    base = 2 * (sender * capacity + rank)
    match = inner.reshape(1, -1) == jnp.arange(slot_count, dtype=jnp.int32)[:, None]

    def pick(value):
        return jnp.sum(jnp.where(match, value.reshape(1, -1) + 1, 0), axis=1) - 1

    landed_base = pick(base)
    landed = landed_base >= 0
    stays = slot_dest < 0
    kind = jnp.where(landed, LANDED, jnp.where(stays, KEPT, BLANK))
    held_req = jnp.where(landed, pick(req), jnp.where(stays, slot_owner[:, 0], -1))
    held_page = jnp.where(landed, pick(page), slot_owner[:, 1])
    first = length_of(lengths, held_req) - held_page * page_size
    fresh = (held_req >= 0) & (first > -STEPS) & (first < page_size)
    return jnp.stack([kind, landed_base, jnp.where(fresh, held_req, -1), first])


def local(tokens, norm_gain, w_query, w_key_value, w_out, kv_pool, slot_owner, slot_dest, lengths):
    seq_count = lax.axis_size("seq")
    tp_count = lax.axis_size("tp")
    my_index = lax.axis_index("seq")
    row_count, token_width = tokens.shape
    slot_count, page_size = kv_pool.shape[1:3]
    capacity = -(-slot_count // seq_count)

    notes = gather_notes(tokens, slot_owner, slot_dest, seq_count)
    outgoing = pack_pages(kv_pool, slot_dest, seq_count, capacity)
    outgoing, notes = lax.optimization_barrier((outgoing, notes))
    arrived = lax.all_to_all(outgoing, "seq", split_axis=0, concat_axis=0, tiled=True)

    seq_tokens = notes[:, :CHUNK_ROWS].reshape(seq_count * CHUNK_ROWS, token_width)
    all_tokens = lax.all_gather(seq_tokens, "tp", axis=1, tiled=True)
    queries, key_new, value_new = project_rows(
        all_tokens, row_count, norm_gain, w_query, w_key_value, lengths
    )
    table = slot_table(
        notes, row_count, my_index, capacity, slot_owner, slot_dest, lengths, page_size
    )
    key_wide, value_wide = key_new.astype(jnp.float32), value_new.astype(jnp.float32)
    begun, mark = place_kept(row_count, table, kv_pool, key_wide, value_wide)
    owner_req = slot_owner[:, 0]
    base_len = length_of(lengths, owner_req)
    position = slot_owner[:, 1][:, None] * page_size + jnp.arange(page_size, dtype=jnp.int32)[None, :]
    key_req = jnp.where(position < base_len[:, None], owner_req[:, None], -1).reshape(1, -1)
    payload = attend(
        my_index, seq_count, row_count, mark, queries, key_new, value_new, key_req, kv_pool
    )
    payload, arrived = lax.optimization_barrier((payload, arrived))
    partials = lax.all_to_all(payload, "seq", split_axis=0, concat_axis=0, tiled=True)

    kv_moved, mark = place_landed(row_count, capacity, table, begun, arrived, key_wide, value_wide)
    partial_out = combine(mark, partials, w_out, row_count)[:row_count]
    if tp_count == 2:
        half = partial_out.shape[1] // 2
        swap = lax.axis_index("tp") == 0
        low, high = partial_out[:, :half], partial_out[:, half:]
        other = lax.ppermute(jnp.where(swap, high, low), "tp", [(0, 1), (1, 0)])
        own = jnp.where(swap, low, high)
        attn_out = (own.astype(jnp.float32) + other.astype(jnp.float32)).astype(jnp.bfloat16)
    else:
        attn_out = lax.psum_scatter(partial_out, "tp", scatter_dimension=1, tiled=True)
    return (attn_out, kv_moved)


def solution(mesh):
    in_specs = (
        P("seq", "tp"),
        P(),
        P(None, "tp"),
        P(None, None, "tp"),
        P("tp", None),
        P(None, "seq", None, "tp"),
        P("seq", None),
        P("seq"),
        P(),
    )
    out_specs = (P("seq", "tp"), P(None, "seq", None, "tp"))
    return jax.shard_map(local, mesh=mesh, in_specs=in_specs, out_specs=out_specs, check_vma=False)
```

time: 304 us -> 130 us (0.43)
  the two profiles are of different devices: /device:TPU:14 before, /device:TPU:5 now
where the time goes in v2:
time: 130 us; the launch traced here: 128 us
  waiting for transfers between devices  48.6 us (37%)
  Pallas kernels  24.6 us (19%)
  starting transfers between devices  24.6 us (19%)
  blocking collectives  14.8 us (11%)
  other arithmetic  5.42 us (4%)
  local copies, waits for them, and re-layouts  4.94 us (4%)
  matrix products  3.89 us (3%)
    all_to_all x1, waiting for transfers between devices, local(): lax.all_to_all(outgoing, 'seq', split_axis=0, concat_axis=0, tiled=True)  45.9 us
    all_to_all x1, starting transfers between devices, local(): lax.all_to_all(payload, 'seq', split_axis=0, concat_axis=0, tiled=True)  13 us
    all_to_all x1, blocking collectives, gather_notes(): lax.all_to_all(note, 'seq', split_axis=0, concat_axis=0, axis_index_group...  9.18 us
    all_gather x1, blocking collectives, local(): all_tokens = lax.all_gather(seq_tokens, 'tp', axis=1, tiled=True)  5.61 us
    pallas_call x1, Pallas kernels, place_landed(): pl.pallas_call(functools.partial(land_body, row_count, capacity), out_sha...  5.5 us
    pallas_call x1, Pallas kernels, attend(): pl.pallas_call(functools.partial(attend_body, kv_count, group_size, seq_c...  5.36 us
    pallas_call x1, Pallas kernels, place_kept(): pl.pallas_call(functools.partial(keep_body, row_count), out_shape=(jax.Sh...  5.23 us
    all_to_all x1, starting transfers between devices, local(): lax.all_to_all(outgoing, 'seq', split_axis=0, concat_axis=0, tiled=True)  4.44 us
  transfers between devices with their start and end apart: 4, of which 4 were waited for; matrix products, arithmetic and copies ran while one was open for 7% of the time, Pallas kernels for 15%

profile of v2, /device:TPU:5, one launch (start us, length us, event | category | flops | bytes accessed | tf_op | source)
XLA Modules:
  0.0 127.9 jit_solution(4510593799314023131)
XLA Ops:
  0.6 1.4 %make_notes.1 = bf16[4,8,1024]{2,1,0:T(8,128)(2,1)} custom-call(bf16[6,1024]{1,0:T(8,128)(2,1)} %token_ref.1, s32[1,112]{1,0:T(1,128)} %bitcast.73, s32[2,112]{1,0:T(2,128)} %bitcast.72), custom_call_target="tpu_custom_call" | custom-call | tf_op jit(solution)/shard_map/make_notes/pallas_call | solution.py:89
  2.0 9.2 %all_to_all.20 = bf16[4,8,1024]{2,1,0:T(8,128)(2,1)S(1)} all-to-all(bf16[4,8,1024]{2,1,0:T(8,128)(2,1)} %make_notes.1), channel_id=1, replica_groups={{0,8,16,24},{2,10,18,26},{4,12,20,28},{6,14,22,30},{1,9,17,25},{3,11,19..., dimensions={0} | all-to-all | bytes 131072 | tf_op jit(solution)/shard_map/all_to_all | solution.py:107
  11.2 0.7 broadcast_in_dim.88
  11.9 3.7 %all-to-all-start.1 = ((bf16[4,4,8,1024]{3,2,1,0:T(8,128)(2,1)}), bf16[4,4,8,1024]{3,2,1,0:T(8,128)(2,1)S(1)}, u32[]{:S(2)}, u32[]{:S(2)}) async-start(bf16[4,4,8,1024]{3,2,1,0:T(8,128)(2,1)} %broadcast_in_dim.88), calls=%async_computation.1 | async-start | bytes 524288 | tf_op jit(solution)/shard_map/all_to_all | solution.py:111
  15.6 3.1 %pack_pages.1 = bf16[16,14,16,512]{3,2,1,0:T(8,128)(2,1)} custom-call(s32[112]{0:T(128)} %dest_ref.1, bf16[2,112,16,512]{3,2,1,0:T(8,128)(2,1)} %pool_ref.5), custom_call_target="tpu_custom_call" | custom-call | tf_op jit(solution)/shard_map/pack_pages/pallas_call | solution.py:189
  18.7 0.0 copy-start.12
  18.7 0.0 copy-start.11
  18.7 0.9 all-to-all-done.1
  19.7 4.4 %all-to-all-start.2 = ((bf16[16,14,16,512]{3,2,1,0:T(8,128)(2,1)}), bf16[16,14,16,512]{3,2,1,0:T(8,128)(2,1)}, u32[]{:S(2)}, u32[]{:S(2)}) async-start(bf16[16,14,16,512]{3,2,1,0:T(8,128)(2,1)} %pack_pages.1), calls=%async_computation.2 | async-start | bytes 7340032 | tf_op jit(solution)/shard_map/all_to_all | solution.py:531
  24.2 0.1 select_reduce_fusion.4
  24.3 0.3 multiply_cosine_fusion
  24.6 0.1 slice.67
  24.7 0.1 fusion.8
  24.8 0.1 add.169
  24.9 0.3 reduce_window_sum.11
  25.2 0.1 multiply_add_fusion
  25.3 0.1 add.165
  25.3 0.5 broadcast.293
  25.8 0.7 reduce.11
  26.5 0.1 sub.58
  26.6 0.1 add.167
  26.7 0.4 select_reduce_fusion
  27.1 0.1 select_reduce_fusion.3
  27.2 0.1 fusion.7
  27.3 0.1 select_n.93.key_req_ref
  27.4 5.6 %all_gather.3 = bf16[128,2048]{1,0:T(8,128)(2,1)S(1)} all-gather(bf16[128,1024]{1,0:T(8,128)(2,1)S(1)} %bitcast.66), channel_id=1, replica_groups=mesh['seq'=16,'tp'=2] {'tp'}, dimensions={1}, use_global_device_ids=true | all-gather | bytes 786432 | tf_op jit(solution)/shard_map/all_gather | solution.py:534
  33.0 0.2 fusion
  33.2 3.1 %convolution_bitcast_fusion = f32[16,8,8,128]{3,1,2,0:T(8,128)S(1)} fusion(bf16[2048,1024]{1,0:T(8,128)(2,1)} %param.13, bf16[128,2048]{1,0:T(8,128)(2,1)S(1)} %all_gather.3, f32[2048]{0:T(1024)S(1)} %copy-done.7, f32[128]{0:T(128)S(1)} %add_rsqrt_fusion), kind=kOutput, calls=%fused_computation.2 | convolution fusion | flops 537919488 | bytes 5251584 | tf_op jit(solution)/shard_map/dot_general | solution.py:57
  36.4 0.1 copy.18
  36.5 0.3 subtract_convert_fusion
  36.7 0.1 pad_maximum_fusion
  36.9 0.8 convolution_bitcast_fusion.1
  37.8 0.1 reshape_squeeze.3
  37.9 0.3 subtract_convert_fusion.1
  38.2 0.2 pad_maximum_fusion.1
  38.5 2.2 %copy-done = bf16[2,112,16,512]{3,2,1,0:T(8,128)(2,1)S(1)} copy-done((bf16[2,112,16,512]{3,2,1,0:T(8,128)(2,1)S(1)}, bf16[2,112,16,512]{3,2,1,0:T(8,128)(2,1)}, u32[]{:S(2)}) %copy-start) | copy-done | bytes 3670040
  40.7 5.2 %place_kept.1 = (bf16[2,112,16,512]{3,2,1,0:T(8,128)(2,1)}, f32[8,128]{1,0:T(8,128)S(1)}) custom-call(s32[4,112]{1,0:T(4,128)S(1)} %pad_add_fusion.table_ref, bf16[2,112,16,512]{3,2,1,0:T(8,128)(2,1)S(1)} %copy-done, f32[128,512]{1,0:T(8,128)S(1)} %get-tuple-element.34.key_ref, f32[128,512]{1,0:T(8,128)S(1)} %get-tuple-element.25.value_ref), custom_call_target="tpu_custom_call" | custom-call | tf_op jit(solution)/shard_map/place_kept/pallas_call | solution.py:254
  45.9 5.4 %attend.1 = bf16[16,16,512]{2,1,0:T(8,128)(2,1)} custom-call(s32[1]{0:T(128)} %bitcast.13.index_ref, f32[8,128]{1,0:T(8,128)S(1)} %get-tuple-element.11.mark_ref, bf16[128,1024]{1,0:T(8,128)(2,1)S(1)} %bitcast.63, bf16[128,512]{1,0:T(8,128)(2,1)S(1)} %get-tuple-element.33.key_new_ref, bf16[128,512]{1,0:T(8,128)(2,1)S(1)} %get-tuple-element.26.value_new_ref, ...), custom_call_target="tpu_custom_call" | custom-call | tf_op jit(solution)/shard_map/attend/pallas_call | solution.py:408
  51.3 45.9 %all-to-all-done.2 = bf16[16,14,16,512]{3,2,1,0:T(8,128)(2,1)} async-done(((bf16[16,14,16,512]{3,2,1,0:T(8,128)(2,1)}), bf16[16,14,16,512]{3,2,1,0:T(8,128)(2,1)}, u32[]{:S(2)}, u32[]{:S(2)}) %all-to-all-start.2) | async-done | bytes 3670048 | tf_op jit(solution)/shard_map/all_to_all | solution.py:531
  97.1 13.0 %all-to-all-start.3 = ((bf16[16,16,512]{2,1,0:T(8,128)(2,1)}), bf16[16,16,512]{2,1,0:T(8,128)(2,1)S(1)}, u32[]{:S(2)}, u32[]{:S(2)}) async-start(bf16[16,16,512]{2,1,0:T(8,128)(2,1)} %attend.1), calls=%async_computation.3 | async-start | bytes 524288 | tf_op jit(solution)/shard_map/all_to_all | solution.py:551
  110.2 5.5 %place_landed.1 = (bf16[2,112,16,512]{3,2,1,0:T(8,128)(2,1)}, f32[8,128]{1,0:T(8,128)}) custom-call(s32[4,112]{1,0:T(4,128)} %copy-done.4, bf16[224,16,512]{2,1,0:T(8,128)(2,1)} %bitcast.19.arrived_ref, f32[128,512]{1,0:T(8,128)} %copy-done.2, f32[128,512]{1,0:T(8,128)} %copy-done.3, ...), custom_call_target="tpu_custom_call", output_to_operand_aliasing={{0}: (4, {})} | custom-call | tf_op jit(solution)/shard_map/place_landed/pallas_call | solution.py:302
  115.7 1.1 all-to-all-done.3.part_ref
  116.7 0.7 copy-done.6
  117.4 4.0 %combine.1 = bf16[8,2048]{1,0:T(8,128)(2,1)} custom-call(f32[8,128]{1,0:T(8,128)} %get-tuple-element.15.mark_ref, bf16[16,16,512]{2,1,0:T(8,128)(2,1)} %copy-done.6, bf16[1024,2048]{1,0:T(8,128)(2,1)} %weight_ref.1), custom_call_target="tpu_custom_call" | custom-call | tf_op jit(solution)/shard_map/combine/pallas_call | solution.py:474
  121.4 0.7 broadcast_select_fusion
  122.2 3.5 %collective-permute-start = (bf16[6,1024]{1,0:T(8,128)(2,1)S(1)}, bf16[6,1024]{1,0:T(8,128)(2,1)S(1)}, u32[]{:S(2)}, u32[]{:S(2)}) collective-permute-start(bf16[6,1024]{1,0:T(8,128)(2,1)S(1)} %broadcast_select_fusion), channel_id=1, source_target_pairs={{0,1},{1,0},{2,3},{3,2},{4,5},{5,4},{6,7},{7,6},{8,9},{9,8},{10,11... | collective-permute-start | bytes 36872 | tf_op jit(solution)/shard_map/ppermute | solution.py:559
  125.7 0.8 collective-permute-done
  126.6 1.4 %add_convert_fusion.2 = bf16[6,1024]{1,0:T(8,128)(2,1)} fusion(bf16[6,1024]{1,0:T(8,128)(2,1)S(1)} %collective-permute-done, pred[]{:T(512)S(6)} %eq.26, bf16[8,2048]{1,0:T(8,128)(2,1)} %combine.1), kind=kLoop, calls=%fused_computation.27 | loop fusion | flops 30720 | bytes 49153 | tf_op jit(solution)/shard_map/convert_element_type | solution.py:561
  (40 shorter events, 0.3 us)
Async XLA Ops:
  11.9 7.7 %all-to-all-start.1 = ((bf16[4,4,8,1024]{3,2,1,0:T(8,128)(2,1)}), bf16[4,4,8,1024]{3,2,1,0:T(8,128)(2,1)S(1)}, u32[]{:S(2)}, u32[]{:S(2)}) async-start(bf16[4,4,8,1024]{3,2,1,0:T(8,128)(2,1)} %broadcast_in_dim.88), calls=%async_computation.1 | async-start | bytes 524288 | tf_op jit(solution)/shard_map/all_to_all | solution.py:111
  18.7 5.4 %copy-start.10 = (s32[24]{0:T(128)S(1)}, s32[24]{0:T(128)}, u32[]{:S(2)}) copy-start(s32[24]{0:T(128)} %param.19) | copy-start | bytes 292
  18.7 5.4 %copy-start.12 = (s32[128]{0:T(128)S(1)}, s32[128]{0:T(128)}, u32[]{:S(2)}) copy-start(s32[128]{0:T(128)} %constant.64.clone) | copy-start | bytes 1540
  18.7 5.5 %copy-start.11 = (s32[128]{0:T(128)S(1)}, s32[128]{0:T(128)}, u32[]{:S(2)}) copy-start(s32[128]{0:T(128)} %constant.65.clone) | copy-start | bytes 1540
  18.7 5.5 %copy-start.8 = (s32[112,2]{0,1:T(2,128)S(1)}, s32[112,2]{0,1:T(2,128)}, u32[]{:S(2)}) copy-start(s32[112,2]{0,1:T(2,128)} %param.17) | copy-start | bytes 2692
  19.6 7.4 %copy-start.9 = (s32[112]{0:T(128)S(1)}, s32[112]{0:T(128)}, u32[]{:S(2)}) copy-start(s32[112]{0:T(128)} %dest_ref.1) | copy-start | bytes 1348
  19.7 13.6 %copy-start.7 = (f32[2048]{0:T(1024)S(1)}, f32[2048]{0:T(1024)}, u32[]{:S(2)}) copy-start(f32[2048]{0:T(1024)} %param.12) | copy-start | bytes 24580
  19.7 77.5 %all-to-all-start.2 = ((bf16[16,14,16,512]{3,2,1,0:T(8,128)(2,1)}), bf16[16,14,16,512]{3,2,1,0:T(8,128)(2,1)}, u32[]{:S(2)}, u32[]{:S(2)}) async-start(bf16[16,14,16,512]{3,2,1,0:T(8,128)(2,1)} %pack_pages.1), calls=%async_computation.2 | async-start | bytes 7340032 | tf_op jit(solution)/shard_map/all_to_all | solution.py:531
  33.2 3.7 %copy-start.5 = (bf16[2,2048,512]{2,1,0:T(8,128)(2,1)S(1)}, bf16[2,2048,512]{2,1,0:T(8,128)(2,1)}, u32[]{:S(2)}) copy-start(bf16[2,2048,512]{2,1,0:T(8,128)(2,1)} %param.14) | copy-start | bytes 12582916
  37.9 13.4 %copy-start.4 = (s32[4,112]{1,0:T(4,128)}, s32[4,112]{1,0:T(4,128)S(1)}, u32[]{:S(2)}) copy-start(s32[4,112]{1,0:T(4,128)S(1)} %pad_add_fusion.table_ref) | copy-start | bytes 5380
  38.4 12.8 %copy-start.2 = (f32[128,512]{1,0:T(8,128)}, f32[128,512]{1,0:T(8,128)S(1)}, u32[]{:S(2)}) copy-start(f32[128,512]{1,0:T(8,128)S(1)} %get-tuple-element.34.key_ref) | copy-start | bytes 786436
  38.5 12.8 %copy-start.3 = (f32[128,512]{1,0:T(8,128)}, f32[128,512]{1,0:T(8,128)S(1)}, u32[]{:S(2)}) copy-start(f32[128,512]{1,0:T(8,128)S(1)} %get-tuple-element.25.value_ref) | copy-start | bytes 786436
  38.5 2.2 %copy-start = (bf16[2,112,16,512]{3,2,1,0:T(8,128)(2,1)S(1)}, bf16[2,112,16,512]{3,2,1,0:T(8,128)(2,1)}, u32[]{:S(2)}) copy-start(bf16[2,112,16,512]{3,2,1,0:T(8,128)(2,1)} %pool_ref.5) | copy-start | bytes 11010052
  40.7 5.2 %copy-start.1 = (bf16[2,112,16,512]{3,2,1,0:T(8,128)(2,1)S(1)}, bf16[2,112,16,512]{3,2,1,0:T(8,128)(2,1)}, u32[]{:S(2)}) copy-start(bf16[2,112,16,512]{3,2,1,0:T(8,128)(2,1)} %pool_ref.5) | copy-start | bytes 11010052
  97.1 19.6 %all-to-all-start.3 = ((bf16[16,16,512]{2,1,0:T(8,128)(2,1)}), bf16[16,16,512]{2,1,0:T(8,128)(2,1)S(1)}, u32[]{:S(2)}, u32[]{:S(2)}) async-start(bf16[16,16,512]{2,1,0:T(8,128)(2,1)} %attend.1), calls=%async_computation.3 | async-start | bytes 524288 | tf_op jit(solution)/shard_map/all_to_all | solution.py:551
  116.7 0.7 copy-start.6
  122.2 4.4 %collective-permute-start = (bf16[6,1024]{1,0:T(8,128)(2,1)S(1)}, bf16[6,1024]{1,0:T(8,128)(2,1)S(1)}, u32[]{:S(2)}, u32[]{:S(2)}) collective-permute-start(bf16[6,1024]{1,0:T(8,128)(2,1)S(1)} %broadcast_select_fusion), channel_id=1, source_target_pairs={{0,1},{1,0},{2,3},{3,2},{4,5},{5,4},{6,7},{7,6},{8,9},{9,8},{10,11... | collective-permute-start | bytes 36872 | tf_op jit(solution)/shard_map/ppermute | solution.py:559

commit v3 on v2

--- a/solution.py
+++ b/solution.py
@@ -75,11 +75,10 @@
             row = row_count + field // per_row
             lane = (field % per_row) * stride
             page_ref[row : row + 1, lane : lane + slot_count] = digit.astype(jnp.float32)
-    for target in range(out_ref.shape[0]):
-        out_ref[target] = page_ref[...].astype(out_ref.dtype)
-
-
-def make_notes(tokens, slot_owner, slot_dest, seq_count):
+    out_ref[...] = page_ref[...].astype(out_ref.dtype)
+
+
+def make_note(tokens, slot_owner, slot_dest):
     row_count, width = tokens.shape
     slot_count = slot_dest.shape[0]
     stride = -(-slot_count // LANES) * LANES
@@ -88,30 +87,34 @@
     vmem = pl.BlockSpec(memory_space=pltpu.VMEM)
     return pl.pallas_call(
         functools.partial(note_body, row_count, stride),
-        out_shape=jax.ShapeDtypeStruct((seq_count, rows, width), tokens.dtype),
+        out_shape=jax.ShapeDtypeStruct((rows, width), tokens.dtype),
         in_specs=[vmem] * 3,
         out_specs=vmem,
         scratch_shapes=[pltpu.VMEM((rows, width), jnp.float32)],
-        name="make_notes",
+        name="make_note",
     )(tokens, slot_dest.reshape(1, -1), slot_owner.T)
 
 
-def gather_notes(tokens, slot_owner, slot_dest, seq_count):
-    inner = 1 << ((seq_count.bit_length() - 1) // 2)
-    outer = seq_count // inner
-    assert inner * outer == seq_count
-    lines = [[o * inner + i for o in range(outer)] for i in range(inner)]
-    planes = [[o * inner + i for i in range(inner)] for o in range(outer)]
-    note = make_notes(tokens, slot_owner, slot_dest, outer)
-    rows, width = note.shape[1:]
-    along = lax.all_to_all(
-        note, "seq", split_axis=0, concat_axis=0, axis_index_groups=lines, tiled=True
-    )
-    along = jnp.broadcast_to(along[None], (inner, outer, rows, width))
-    across = lax.all_to_all(
-        along, "seq", split_axis=0, concat_axis=0, axis_index_groups=planes, tiled=True
-    )
-    return jnp.swapaxes(across, 0, 1).reshape(seq_count, rows, width)
+def sort_body(inner, index_ref, *refs):
+    part_refs, out_ref = refs[:-1], refs[-1]
+    near, far = index_ref[0] & (inner - 1), index_ref[0] // inner
+    for shift, part_ref in enumerate(part_refs):
+        for step in range(part_ref.shape[0]):
+            out_ref[(far ^ step) * inner + (near ^ shift)] = part_ref[step]
+
+
+def sort_notes(my_index, parts):
+    inner = len(parts)
+    far_count, rows, width = parts[0].shape
+    vmem = pl.BlockSpec(memory_space=pltpu.VMEM)
+    return pl.pallas_call(
+        functools.partial(sort_body, inner),
+        out_shape=jax.ShapeDtypeStruct((far_count * inner, rows, width), parts[0].dtype),
+        in_specs=[pl.BlockSpec(memory_space=pltpu.SMEM)] + [vmem] * inner,
+        out_specs=vmem,
+        compiler_params=pltpu.CompilerParams(vmem_limit_bytes=16 * 2**20),
+        name="sort_notes",
+    )(my_index.reshape(1).astype(jnp.int32), *parts)
 
 
 def read_notes(notes, row_count, slot_count):
@@ -198,6 +201,7 @@
             pltpu.SemaphoreType.DMA,
         ],
         compiler_params=pltpu.CompilerParams(vmem_limit_bytes=MOST_VMEM),
+        cost_estimate=moved(2 * kv_pool.size),
         name="pack_pages",
     )(slot_dest, kv_pool)
 
@@ -215,12 +219,12 @@
 KEPT, BLANK, LANDED = 0, 1, 2
 
 
-def keep_body(row_count, table_ref, pool_ref, key_ref, value_ref, out_ref, mark_ref):
+def keep_body(row_count, table_ref, pool_ref, key_ref, value_ref, after_ref, out_ref, mark_ref):
     mark_ref[...] = jnp.zeros_like(mark_ref)
 
     def fill(slot, carry):
         kind = table_ref[0, slot]
-        req = table_ref[2, slot]
+        req = table_ref[1, slot]
 
         @pl.when(kind == KEPT)
         def _():
@@ -235,7 +239,7 @@
 
         @pl.when((req >= 0) & (kind == KEPT))
         def _():
-            first = table_ref[3, slot]
+            first = table_ref[2, slot]
             for which, fresh_ref in ((0, key_ref), (1, value_ref)):
                 out_ref[which, slot] = patched(
                     out_ref[which, slot], fresh_ref, row_count, req, first
@@ -246,74 +250,80 @@
     lax.fori_loop(0, table_ref.shape[1], fill, 0)
 
 
+def moved(elements, flops=0):
+    return pl.CostEstimate(flops=flops, bytes_accessed=2 * elements, transcendentals=0)
+
+
 MARK = jax.ShapeDtypeStruct((CHUNK_ROWS, LANES), jnp.float32)
 
 
-def place_kept(row_count, table, kv_pool, key_new, value_new):
+def place_kept(row_count, table, kv_pool, key_new, value_new, after):
     vmem = pl.BlockSpec(memory_space=pltpu.VMEM)
     return pl.pallas_call(
         functools.partial(keep_body, row_count),
         out_shape=(jax.ShapeDtypeStruct(kv_pool.shape, kv_pool.dtype), MARK),
-        in_specs=[pl.BlockSpec(memory_space=pltpu.SMEM)] + [vmem] * 3,
+        in_specs=[pl.BlockSpec(memory_space=pltpu.SMEM)]
+        + [vmem] * 3
+        + [pl.BlockSpec(memory_space=pl.ANY)],
         out_specs=(vmem, vmem),
-        compiler_params=pltpu.CompilerParams(vmem_limit_bytes=40 * 2**20),
+        compiler_params=pltpu.CompilerParams(vmem_limit_bytes=24 * 2**20),
+        cost_estimate=moved(3 * kv_pool.size),
         name="place_kept",
-    )(table, kv_pool, key_new, value_new)
+    )(table, kv_pool, key_new, value_new, after)
 
 
 def land_body(
-    row_count, capacity, table_ref, arrived_ref, key_ref, value_ref, begun_ref, out_ref, mark_ref,
-    held_ref, stage_ref, load_sem, sem,
+    row_count, capacity, table_ref, held_ref, key_ref, value_ref, begun_ref, out_ref, mark_ref,
+    stage_ref, sem,
 ):
-    load = pltpu.make_async_copy(arrived_ref, held_ref, load_sem)
-    load.start()
+    places = table_ref.shape[1]
     mark_ref[...] = jnp.zeros_like(mark_ref)
-    load.wait()
-
-    def send(slot, count):
-        landed = table_ref[0, slot] == LANDED
-        base = table_ref[1, slot]
-        req = table_ref[2, slot]
-
-        @pl.when(landed & (req < 0))
+
+    def send(place, count):
+        slot = table_ref[0, place]
+        req = table_ref[1, place]
+
+        @pl.when((slot >= 0) & (req < 0))
         def _():
-            pltpu.make_async_copy(held_ref.at[pl.ds(base, 2)], out_ref.at[:, slot], sem).start()
-
-        @pl.when(landed & (req >= 0))
+            pltpu.make_async_copy(
+                held_ref.at[pl.ds(2 * place, 2)], out_ref.at[:, slot], sem
+            ).start()
+
+        @pl.when((slot >= 0) & (req >= 0))
         def _():
-            first = table_ref[3, slot]
+            first = table_ref[2, place]
             for which, fresh_ref in ((0, key_ref), (1, value_ref)):
                 stage_ref[slot, which] = patched(
-                    held_ref[base + which], fresh_ref, row_count, req, first
+                    held_ref[2 * place + which], fresh_ref, row_count, req, first
                 )
             pltpu.make_async_copy(stage_ref.at[slot], out_ref.at[:, slot], sem).start()
 
-        return count + landed.astype(jnp.int32)
-
-    count = lax.fori_loop(0, table_ref.shape[1], send, 0)
+        return count + (slot >= 0).astype(jnp.int32)
+
+    count = lax.fori_loop(0, places, send, 0)
     wait_pages(stage_ref.at[pl.ds(0, capacity)], stage_ref.at[0], capacity, count, sem)
 
 
-def place_landed(row_count, capacity, table, begun, arrived, key_new, value_new):
+def place_landed(row_count, table, begun, arrived, key_new, value_new):
     slot_count, page_size, width = begun.shape[1:]
+    capacity = arrived.shape[1] // 2
     vmem = pl.BlockSpec(memory_space=pltpu.VMEM)
     hbm = pl.BlockSpec(memory_space=pltpu.HBM)
     arrived = arrived.reshape(-1, page_size, width)
     return pl.pallas_call(
         functools.partial(land_body, row_count, capacity),
         out_shape=(jax.ShapeDtypeStruct(begun.shape, begun.dtype), MARK),
-        in_specs=[pl.BlockSpec(memory_space=pltpu.SMEM), hbm, vmem, vmem, hbm],
+        in_specs=[pl.BlockSpec(memory_space=pltpu.SMEM), vmem, vmem, vmem, hbm],
         out_specs=(hbm, vmem),
         scratch_shapes=[
-            pltpu.VMEM(arrived.shape, begun.dtype),
             pltpu.VMEM((slot_count, 2, page_size, width), begun.dtype),
-            pltpu.SemaphoreType.DMA,
             pltpu.SemaphoreType.DMA,
         ],
         input_output_aliases={4: 0},
-        compiler_params=pltpu.CompilerParams(vmem_limit_bytes=MOST_VMEM),
+        compiler_params=pltpu.CompilerParams(vmem_limit_bytes=32 * 2**20),
+        cost_estimate=moved(3 * begun.size),
         name="place_landed",
-    )(table, arrived, key_new, value_new, begun)
+    )(table, pltpu.with_memory_space_constraint(arrived, pltpu.VMEM), key_new, value_new, begun)
 
 
 def split_parts(value):
@@ -327,9 +337,9 @@
 
 def attend_body(
     kv_count, group_size, seq_count, row_count,
-    index_ref, mark_ref, query_ref, key_new_ref, value_new_ref, key_req_ref, pool_ref,
-    out_ref, whole_ref,
+    index_ref, query_ref, key_new_ref, value_new_ref, key_req_ref, pool_ref, *rest,
 ):
+    out_refs, whole_ref, chunk_ref = rest[:-2], rest[-2], rest[-1]
     rows = query_ref.shape[0]
     width = kv_count * HD
     slot_count, page_size = pool_ref.shape[1:3]
@@ -391,11 +401,16 @@
         line = jnp.sum(jnp.where(place == chunk_row, stats[span], 0.0), axis=0, keepdims=True)
         pieces = [whole_ref[span, g * width : (g + 1) * width] for g in range(group_size)]
         pieces[0] = jnp.where(chunk_row == row_count, line, pieces[0])
-        out_ref[chunk] = jnp.concatenate(pieces, axis=0).astype(out_ref.dtype)
+        chunk_ref[chunk] = jnp.concatenate(pieces, axis=0).astype(chunk_ref.dtype)
+    inner = len(out_refs)
+    own = index_ref[0] & (inner - 1)
+    for shift, out_ref in enumerate(out_refs):
+        for far in range(seq_count // inner):
+            out_ref[far] = chunk_ref[far * inner + (own ^ shift)]
 
 
 def attend(
-    my_index, seq_count, row_count, mark, queries, key_new, value_new, key_req, kv_pool
+    my_index, seq_count, inner, row_count, queries, key_new, value_new, key_req, kv_pool
 ):
     slot_count, page_size, width = kv_pool.shape[1:]
     kv_count = width // HD
@@ -407,84 +422,171 @@
     vmem = pl.BlockSpec(memory_space=pltpu.VMEM)
     return pl.pallas_call(
         functools.partial(attend_body, kv_count, group_size, seq_count, row_count),
-        out_shape=jax.ShapeDtypeStruct((seq_count, page_size, width), jnp.bfloat16),
-        in_specs=[smem, pl.BlockSpec(memory_space=pl.ANY)] + [vmem] * 5,
-        out_specs=vmem,
-        scratch_shapes=[pltpu.VMEM((rows, q_width), jnp.float32)],
-        compiler_params=pltpu.CompilerParams(vmem_limit_bytes=48 * 2**20),
+        out_shape=(jax.ShapeDtypeStruct((seq_count // inner, page_size, width), jnp.bfloat16),)
+        * inner,
+        in_specs=[smem] + [vmem] * 5,
+        out_specs=(vmem,) * inner,
+        scratch_shapes=[
+            pltpu.VMEM((rows, q_width), jnp.float32),
+            pltpu.VMEM((seq_count, page_size, width), jnp.bfloat16),
+        ],
+        compiler_params=pltpu.CompilerParams(vmem_limit_bytes=36 * 2**20),
+        cost_estimate=moved(2 * kv_pool.size, 4 * rows * q_width * slot_count * page_size),
         name="attend",
     )(
-        my_index.reshape(1).astype(jnp.int32), mark, queries, key_new, value_new, key_req, kv_pool
+        my_index.reshape(1).astype(jnp.int32), queries, key_new, value_new, key_req, kv_pool
     )
 
 
-WEIGHT_CUTS = 4
-
-
-def combine_body(q_count, row_count, mark_ref, part_ref, weight_ref, out_ref, held_ref, load_sem):
-    depth = weight_ref.shape[0] // min(WEIGHT_CUTS, q_count)
-    loads = []
-    for cut in range(weight_ref.shape[0] // depth):
-        span = pl.ds(cut * depth, depth)
-        load = pltpu.make_async_copy(weight_ref.at[span], held_ref.at[span], load_sem.at[cut])
-        load.start()
-        loads.append(load)
-    seq_count, page_size, width = part_ref.shape
+def merge_units(units, q_count, row_count):
+    width = units[0].shape[1]
     stride = width // CHUNK_ROWS
     place = lax.broadcasted_iota(jnp.int32, (CHUNK_ROWS, width), 1) // stride
     chunk_row = lax.broadcasted_iota(jnp.int32, (CHUNK_ROWS, width), 0)
     tops, sums = [], []
-    for sender in range(seq_count):
-        line = part_ref[sender, :CHUNK_ROWS, :].astype(jnp.float32)[row_count : row_count + 1]
-        stats = jnp.where(place == chunk_row, line, 0.0)
+    for unit in units:
+        stats = jnp.where(place == chunk_row, unit[row_count : row_count + 1], 0.0)
         shift = width // 2
         while shift >= stride:
             stats = stats + pltpu.roll(stats, shift, 1)
             shift //= 2
-        pieces = [stats[:, k * q_count : (k + 1) * q_count] for k in range(2 * STAT_PARTS)]
+        stats = stats[:, :LANES]
+        pieces = [stats] + [
+            pltpu.roll(stats, LANES - k * q_count, 1) for k in range(1, 2 * STAT_PARTS)
+        ]
         tops.append(sum(pieces[1:STAT_PARTS], pieces[0]))
         sums.append(sum(pieces[STAT_PARTS + 1 :], pieces[STAT_PARTS]))
+    lane = lax.broadcasted_iota(jnp.int32, (CHUNK_ROWS, LANES), 1)
+    tops = [jnp.where(lane < q_count, top, 0.0) for top in tops]
+    sums = [jnp.where(lane < q_count, total, 0.0) for total in sums]
     peak = functools.reduce(jnp.maximum, tops)
     shares = [total * jnp.exp(top - peak) for top, total in zip(tops, sums)]
     whole = sum(shares[1:], shares[0])
     inverse = 1.0 / jnp.where(whole > 0.0, whole, 1.0)
     shares = [share * inverse for share in shares]
-    attended = []
+    heads = []
     for head in range(q_count):
         half = head * HD // width
-        lane = head * HD - half * width
+        at = head * HD - half * width
         acc = jnp.zeros((CHUNK_ROWS, HD), jnp.float32)
-        for sender in range(seq_count):
-            block = part_ref[sender, half * CHUNK_ROWS : (half + 1) * CHUNK_ROWS, lane : lane + HD]
-            acc = acc + block.astype(jnp.float32) * shares[sender][:, head : head + 1]
-        attended.append(acc.astype(jnp.bfloat16))
-    attended = jnp.concatenate(attended, axis=1)
-    total = jnp.zeros(out_ref.shape, jnp.float32)
-    for cut, load in enumerate(loads):
-        load.wait()
-        span = slice(cut * depth, (cut + 1) * depth)
-        total = total + jnp.dot(
-            attended[:, span], held_ref[span, :], preferred_element_type=jnp.float32
-        )
-    out_ref[...] = total.astype(out_ref.dtype)
-
-
-def combine(mark, arrived, w_out, row_count):
-    vmem = pl.BlockSpec(memory_space=pltpu.VMEM)
-    return pl.pallas_call(
-        functools.partial(combine_body, w_out.shape[0] // HD, row_count),
-        out_shape=jax.ShapeDtypeStruct((CHUNK_ROWS, w_out.shape[1]), jnp.bfloat16),
+        for unit, share in zip(units, shares):
+            block = unit[half * CHUNK_ROWS : (half + 1) * CHUNK_ROWS, at : at + HD]
+            acc = acc + block * share[:, head : head + 1]
+        heads.append(acc)
+    return heads, peak, whole
+
+
+def merge_body(q_count, row_count, index_ref, mark_ref, weight_ref, *rest):
+    rest, near_ref, held_ref, load_sem = rest[:-3], rest[-3], rest[-2], rest[-1]
+    load = pltpu.make_async_copy(weight_ref, near_ref, load_sem)
+    load.start()
+    far_count = rest[0].shape[0]
+    part_refs, out_refs = rest[:-far_count], rest[-far_count:]
+    width = held_ref.shape[2]
+    stride = width // CHUNK_ROWS
+    place = lax.broadcasted_iota(jnp.int32, (CHUNK_ROWS, width), 1) // stride
+    chunk_row = lax.broadcasted_iota(jnp.int32, (CHUNK_ROWS, width), 0)
+    for far in range(far_count):
+        units = [part_ref[far].astype(jnp.float32) for part_ref in part_refs]
+        heads, peak, whole = merge_units(units, q_count, row_count)
+        stats = jnp.zeros((CHUNK_ROWS, LANES), jnp.float32)
+        for k, part in enumerate(split_parts(peak) + split_parts(whole)):
+            stats = stats + (pltpu.roll(part, k * q_count, 1) if k else part)
+        shift = stride
+        while shift < LANES:
+            stats = stats + pltpu.roll(stats, shift, 1)
+            shift *= 2
+        stats = jnp.concatenate([stats] * (width // LANES), axis=1)
+        line = jnp.sum(jnp.where(place == chunk_row, stats, 0.0), axis=0, keepdims=True)
+        numerators = jnp.concatenate(heads, axis=1)
+        pieces = [
+            numerators[:, g * width : (g + 1) * width]
+            for g in range(numerators.shape[1] // width)
+        ]
+        pieces[0] = jnp.where(chunk_row == row_count, line, pieces[0])
+        held_ref[far] = jnp.concatenate(pieces, axis=0).astype(held_ref.dtype)
+    own = index_ref[0] // len(part_refs)
+    for shift, out_ref in enumerate(out_refs):
+        out_ref[...] = held_ref[own ^ shift]
+    load.wait()
+
+
+def merge(my_index, mark, w_out, parts, q_count, row_count):
+    far_count, page_size, width = parts[0].shape
+    vmem = pl.BlockSpec(memory_space=pltpu.VMEM)
+    unit = jax.ShapeDtypeStruct((page_size, width), jnp.bfloat16)
+    return pl.pallas_call(
+        functools.partial(merge_body, q_count, row_count),
+        out_shape=(unit,) * far_count + (pltpu.VMEM(w_out.shape, w_out.dtype),),
         in_specs=[
-            pl.BlockSpec(memory_space=pl.ANY), vmem, pl.BlockSpec(memory_space=pltpu.HBM)
+            pl.BlockSpec(memory_space=pltpu.SMEM),
+            pl.BlockSpec(memory_space=pl.ANY),
+            pl.BlockSpec(memory_space=pltpu.HBM),
+        ]
+        + [vmem] * len(parts),
+        out_specs=(vmem,) * (far_count + 1),
+        scratch_shapes=[
+            pltpu.VMEM((far_count, page_size, width), jnp.bfloat16),
+            pltpu.SemaphoreType.DMA,
         ],
+        compiler_params=pltpu.CompilerParams(vmem_limit_bytes=24 * 2**20),
+        cost_estimate=moved(3 * 2**20),
+        name="merge",
+    )(my_index.reshape(1).astype(jnp.int32), mark, w_out, *parts)
+
+
+def combine_body(q_count, row_count, tp_count, index_ref, *refs):
+    part_refs, weight_ref, out_refs = refs[: -1 - tp_count], refs[-1 - tp_count], refs[-tp_count:]
+    units = [part_ref[...].astype(jnp.float32) for part_ref in part_refs]
+    heads, _, _ = merge_units(units, q_count, row_count)
+    attended = jnp.concatenate([head.astype(jnp.bfloat16) for head in heads], axis=1)
+    total = jnp.dot(attended, weight_ref[...], preferred_element_type=jnp.float32)
+    width = total.shape[1] // tp_count
+    blocks = [total[:, k * width : (k + 1) * width] for k in range(tp_count)]
+    for shift, out_ref in enumerate(out_refs):
+        chosen = blocks[0]
+        for k in range(1, tp_count):
+            chosen = jnp.where((index_ref[0] ^ shift) == k, blocks[k], chosen)
+        out_ref[...] = chosen.astype(out_ref.dtype)
+
+
+def combine(tp_index, tp_count, parts, w_near, row_count):
+    vmem = pl.BlockSpec(memory_space=pltpu.VMEM)
+    block = jax.ShapeDtypeStruct((CHUNK_ROWS, w_near.shape[1] // tp_count), jnp.bfloat16)
+    return pl.pallas_call(
+        functools.partial(combine_body, w_near.shape[0] // HD, row_count, tp_count),
+        out_shape=(block,) * tp_count,
+        in_specs=[pl.BlockSpec(memory_space=pltpu.SMEM)] + [vmem] * (len(parts) + 1),
+        out_specs=(vmem,) * tp_count,
+        compiler_params=pltpu.CompilerParams(vmem_limit_bytes=24 * 2**20),
+        cost_estimate=moved(2 * w_near.size),
+        name="combine",
+    )(tp_index.reshape(1).astype(jnp.int32), *parts, w_near)
+
+
+def close_body(mark_ref, *refs):
+    part_refs, out_ref = refs[:-1], refs[-1]
+    total = part_refs[0][...].astype(jnp.float32)
+    for part_ref in part_refs[1:]:
+        total = total + part_ref[...].astype(jnp.float32)
+    out_ref[...] = total[: out_ref.shape[0]].astype(out_ref.dtype)
+
+
+def close(mark, parts, row_count):
+    vmem = pl.BlockSpec(memory_space=pltpu.VMEM)
+    return pl.pallas_call(
+        close_body,
+        out_shape=jax.ShapeDtypeStruct((row_count, parts[0].shape[1]), jnp.bfloat16),
+        in_specs=[pl.BlockSpec(memory_space=pl.ANY)] + [vmem] * len(parts),
         out_specs=vmem,
-        scratch_shapes=[
-            pltpu.VMEM(w_out.shape, w_out.dtype),
-            pltpu.SemaphoreType.DMA((WEIGHT_CUTS,)),
-        ],
-        compiler_params=pltpu.CompilerParams(vmem_limit_bytes=MOST_VMEM),
-        name="combine",
-    )(mark, arrived, w_out)
+        compiler_params=pltpu.CompilerParams(vmem_limit_bytes=16 * 2**20),
+        name="close",
+    )(mark, *parts)
+
+
+def swap_all(parts, step, count, axis="seq"):
+    pairs = [[(i, i ^ (k * step)) for i in range(count)] for k in range(len(parts))]
+    return [parts[0]] + [lax.ppermute(parts[k], axis, pairs[k]) for k in range(1, len(parts))]
 
 
 def length_of(lengths, request):
@@ -492,29 +594,33 @@
     return jnp.sum(jnp.where(hot, lengths, 0), axis=-1)
 
 
-def slot_table(notes, row_count, my_index, capacity, slot_owner, slot_dest, lengths, page_size):
+def slot_tables(notes, row_count, my_index, capacity, slot_owner, slot_dest, lengths, page_size):
     seq_count = notes.shape[0]
     slot_count = slot_dest.shape[0]
     dest, req, page = read_notes(notes, row_count, slot_count)
-    sender = jnp.arange(seq_count, dtype=jnp.int32)[:, None]
     inner = dest - my_index * slot_count
     to_me = (inner >= 0) & (inner < slot_count)
     rank = jnp.cumsum(to_me.astype(jnp.int32), axis=1) - 1
-    base = 2 * (sender * capacity + rank)
-    match = inner.reshape(1, -1) == jnp.arange(slot_count, dtype=jnp.int32)[:, None]
+    match = to_me[:, None, :] & (
+        rank[:, None, :] == jnp.arange(capacity, dtype=jnp.int32)[None, :, None]
+    )
 
     def pick(value):
-        return jnp.sum(jnp.where(match, value.reshape(1, -1) + 1, 0), axis=1) - 1
-
-    landed_base = pick(base)
-    landed = landed_base >= 0
+        return jnp.sum(jnp.where(match, value[:, None, :] + 1, 0), axis=2).reshape(-1) - 1
+
+    def fresh(request, held_page):
+        first = length_of(lengths, request) - held_page * page_size
+        hit = (request >= 0) & (first > -STEPS) & (first < page_size)
+        return jnp.where(hit, request, -1), first
+
+    slot = pick(inner)
+    by_place = jnp.stack([slot, *fresh(pick(req), pick(page))])
+    landed = jnp.any(slot[None, :] == jnp.arange(slot_count, dtype=jnp.int32)[:, None], axis=1)
     stays = slot_dest < 0
     kind = jnp.where(landed, LANDED, jnp.where(stays, KEPT, BLANK))
-    held_req = jnp.where(landed, pick(req), jnp.where(stays, slot_owner[:, 0], -1))
-    held_page = jnp.where(landed, pick(page), slot_owner[:, 1])
-    first = length_of(lengths, held_req) - held_page * page_size
-    fresh = (held_req >= 0) & (first > -STEPS) & (first < page_size)
-    return jnp.stack([kind, landed_base, jnp.where(fresh, held_req, -1), first])
+    held_req = jnp.where(kind == KEPT, slot_owner[:, 0], -1)
+    by_slot = jnp.stack([kind, *fresh(held_req, slot_owner[:, 1])])
+    return by_slot, by_place
 
 
 def local(tokens, norm_gain, w_query, w_key_value, w_out, kv_pool, slot_owner, slot_dest, lengths):
@@ -525,9 +631,12 @@
     slot_count, page_size = kv_pool.shape[1:3]
     capacity = -(-slot_count // seq_count)
 
-    notes = gather_notes(tokens, slot_owner, slot_dest, seq_count)
+    inner = 1 << ((seq_count.bit_length() - 1) // 2)
+    note = make_note(tokens, slot_owner, slot_dest)
+    along = swap_all([note] * (seq_count // inner), inner, seq_count)
     outgoing = pack_pages(kv_pool, slot_dest, seq_count, capacity)
-    outgoing, notes = lax.optimization_barrier((outgoing, notes))
+    outgoing, along, lengths = lax.optimization_barrier((outgoing, along, lengths))
+    notes = sort_notes(my_index, swap_all([jnp.stack(along)] * inner, 1, seq_count))
     arrived = lax.all_to_all(outgoing, "seq", split_axis=0, concat_axis=0, tiled=True)
 
     seq_tokens = notes[:, :CHUNK_ROWS].reshape(seq_count * CHUNK_ROWS, token_width)
@@ -535,32 +644,25 @@
     queries, key_new, value_new = project_rows(
         all_tokens, row_count, norm_gain, w_query, w_key_value, lengths
     )
-    table = slot_table(
+    by_slot, by_place = slot_tables(
         notes, row_count, my_index, capacity, slot_owner, slot_dest, lengths, page_size
     )
     key_wide, value_wide = key_new.astype(jnp.float32), value_new.astype(jnp.float32)
-    begun, mark = place_kept(row_count, table, kv_pool, key_wide, value_wide)
     owner_req = slot_owner[:, 0]
     base_len = length_of(lengths, owner_req)
     position = slot_owner[:, 1][:, None] * page_size + jnp.arange(page_size, dtype=jnp.int32)[None, :]
     key_req = jnp.where(position < base_len[:, None], owner_req[:, None], -1).reshape(1, -1)
     payload = attend(
-        my_index, seq_count, row_count, mark, queries, key_new, value_new, key_req, kv_pool
+        my_index, seq_count, inner, row_count, queries, key_new, value_new, key_req, kv_pool
     )
-    payload, arrived = lax.optimization_barrier((payload, arrived))
-    partials = lax.all_to_all(payload, "seq", split_axis=0, concat_axis=0, tiled=True)
-
-    kv_moved, mark = place_landed(row_count, capacity, table, begun, arrived, key_wide, value_wide)
-    partial_out = combine(mark, partials, w_out, row_count)[:row_count]
-    if tp_count == 2:
-        half = partial_out.shape[1] // 2
-        swap = lax.axis_index("tp") == 0
-        low, high = partial_out[:, :half], partial_out[:, half:]
-        other = lax.ppermute(jnp.where(swap, high, low), "tp", [(0, 1), (1, 0)])
-        own = jnp.where(swap, low, high)
-        attn_out = (own.astype(jnp.float32) + other.astype(jnp.float32)).astype(jnp.bfloat16)
-    else:
-        attn_out = lax.psum_scatter(partial_out, "tp", scatter_dimension=1, tiled=True)
+    begun, mark = place_kept(row_count, by_slot, kv_pool, key_wide, value_wide, payload[0])
+    near = swap_all(payload, 1, seq_count)
+    *merged, w_near = merge(my_index, mark, w_out, near, w_query.shape[1] // HD, row_count)
+    far = swap_all(merged, inner, seq_count)
+    columns = combine(lax.axis_index("tp"), tp_count, far, w_near, row_count)
+    columns = swap_all(columns, 1, tp_count, "tp")
+    kv_moved, mark = place_landed(row_count, by_place, begun, arrived, key_wide, value_wide)
+    attn_out = close(mark, columns, row_count)
     return (attn_out, kv_moved)
 
 

time: 130 us -> 109 us (0.84); the launches traced: 128 us -> 110 us
  waiting for transfers between devices: 48.6 us -> 26.8 us
  starting transfers between devices: 24.6 us -> 39.5 us
  blocking collectives: 14.8 us -> 6.78 us
  Pallas kernels: 24.6 us -> 21.4 us
  other arithmetic: 5.42 us -> 2.8 us
  local copies, waits for them, and re-layouts: 4.94 us -> 7.37 us
    all_to_all x1, waiting for transfers between devices: 45.9 us -> 0.01 us  [local(): lax.all_to_all(outgoing, 'seq', split_axis=0, concat_axis=0, tiled=True)]
    ppermute x1 -> x13, starting transfers between devices: 3.52 us -> 32.4 us  [swap_all(): lax.ppermute(parts[k], axis, pairs[k])]
    ppermute x1 -> x13, waiting for transfers between devices: 0.84 us -> 26.8 us  [swap_all(): lax.ppermute(parts[k], axis, pairs[k])]
    all_to_all x2 -> x0, starting transfers between devices: 16.7 us -> none  [the longest x1 13 us: local(): lax.all_to_all(payload, 'seq', split_axis=0, concat_axis=0, tiled=True)]
    all_to_all x1 -> x0, blocking collectives: 9.18 us -> none  [gather_notes(): lax.all_to_all(note, 'seq', split_axis=0, concat_axis=0, axis_index_group...]
    unnamed x29 -> x27, local copies, waits for them, and re-layouts: 3.09 us -> 6.4 us
    all_to_all x1, starting transfers between devices: 4.44 us -> 7.17 us  [local(): lax.all_to_all(outgoing, 'seq', split_axis=0, concat_axis=0, tiled=True)]
    all_to_all x2 -> x0, waiting for transfers between devices: 1.95 us -> none  [the longest x1 1.07 us: local(): lax.all_to_all(payload, 'seq', split_axis=0, concat_axis=0, tiled=True)]
  transfers between devices with their start and end apart: 4 -> 14, of which waited for: 4 -> 6; matrix products, arithmetic and copies ran while one was open for 7% -> 7% of each run, Pallas kernels for 15% -> 18%
where the time goes in v3:
time: 109 us; the launch traced here: 110 us
  starting transfers between devices  39.5 us (36%)
  waiting for transfers between devices  26.8 us (25%)
  Pallas kernels  21.4 us (20%)
  local copies, waits for them, and re-layouts  7.37 us (7%)
  blocking collectives  6.78 us (6%)
  matrix products  3.88 us (4%)
  other arithmetic  2.8 us (3%)
    ppermute x13, starting transfers between devices, swap_all(): lax.ppermute(parts[k], axis, pairs[k])  32.4 us
    ppermute x13, waiting for transfers between devices, swap_all(): lax.ppermute(parts[k], axis, pairs[k])  26.8 us
    all_to_all x1, starting transfers between devices, local(): lax.all_to_all(outgoing, 'seq', split_axis=0, concat_axis=0, tiled=True)  7.17 us
    all_gather x1, blocking collectives, local(): all_tokens = lax.all_gather(seq_tokens, 'tp', axis=1, tiled=True)  6.78 us
    unnamed x27, local copies, waits for them, and re-layouts  6.4 us
    pallas_call x1, Pallas kernels, place_kept(): pl.pallas_call(functools.partial(keep_body, row_count), out_shape=(jax.Sh...  5.37 us
    pallas_call x1, Pallas kernels, place_landed(): pl.pallas_call(functools.partial(land_body, row_count, capacity), out_sha...  4.73 us
    pallas_call x1, Pallas kernels, attend(): pl.pallas_call(functools.partial(attend_body, kv_count, group_size, seq_c...  4.67 us
  transfers between devices with their start and end apart: 14, of which 6 were waited for; matrix products, arithmetic and copies ran while one was open for 7% of the time, Pallas kernels for 18%

profile of v3, /device:TPU:5, one launch (start us, length us, event | category | flops | bytes accessed | tf_op | source)
XLA Modules:
  0.0 109.6 jit_solution(4826071531650665970)
XLA Ops:
  0.6 1.4 %make_note.1 = bf16[8,1024]{1,0:T(8,128)(2,1)} custom-call(bf16[6,1024]{1,0:T(8,128)(2,1)} %token_ref.1, s32[1,112]{1,0:T(1,128)} %bitcast.74, s32[2,112]{1,0:T(2,128)} %bitcast.73), custom_call_target="tpu_custom_call" | custom-call | tf_op jit(solution)/shard_map/make_note/pallas_call | solution.py:88
  2.0 3.3 %collective-permute-start.2 = (bf16[8,1024]{1,0:T(8,128)(2,1)}, bf16[8,1024]{1,0:T(8,128)(2,1)S(1)}, u32[]{:S(2)}, u32[]{:S(2)}) collective-permute-start(bf16[8,1024]{1,0:T(8,128)(2,1)} %make_note.1), channel_id=1, source_target_pairs={{0,24},{2,26},{4,28},{6,30},{8,16},{10,18},{12,20},{14,22},{16,8},... | collective-permute-start | bytes 49160 | tf_op jit(solution)/shard_map/ppermute | solution.py:589
  5.3 0.3 collective-permute-start
  5.6 2.7 %pack_pages.1 = bf16[16,14,16,512]{3,2,1,0:T(8,128)(2,1)} custom-call(s32[112]{0:T(128)} %dest_ref.1, bf16[2,112,16,512]{3,2,1,0:T(8,128)(2,1)} %pool_ref.5), custom_call_target="tpu_custom_call" | custom-call | bytes 7340032 | tf_op jit(solution)/shard_map/pack_pages/pallas_call | solution.py:192
  8.4 0.6 collective-permute-done.1
  9.0 7.2 %all-to-all-start = ((bf16[16,14,16,512]{3,2,1,0:T(8,128)(2,1)}), bf16[16,14,16,512]{3,2,1,0:T(8,128)(2,1)}, u32[]{:S(2)}, u32[]{:S(2)}) async-start(bf16[16,14,16,512]{3,2,1,0:T(8,128)(2,1)} %pack_pages.1), calls=%async_computation | async-start | bytes 7340032 | tf_op jit(solution)/shard_map/all_to_all | solution.py:640
  16.2 1.2 %collective-permute-start.5 = (bf16[4,8,1024]{2,1,0:T(8,128)(2,1)S(1)}, bf16[4,8,1024]{2,1,0:T(8,128)(2,1)S(1)}, u32[]{:S(2)}, u32[]{:S(2)}) collective-permute-start(bf16[4,8,1024]{2,1,0:T(8,128)(2,1)S(1)} %pad_maximum_fusion.2.refs_0_), channel_id=1, source_target_pairs={{0,6},{2,4},{4,2},{6,0},{8,14},{10,12},{12,10},{14,8},{16,22},{18,... | collective-permute-start | bytes 196616 | tf_op jit(solution)/shard_map/ppermute | solution.py:589
  17.5 1.2 %collective-permute-start.4 = (bf16[4,8,1024]{2,1,0:T(8,128)(2,1)S(1)}, bf16[4,8,1024]{2,1,0:T(8,128)(2,1)S(1)}, u32[]{:S(2)}, u32[]{:S(2)}) collective-permute-start(bf16[4,8,1024]{2,1,0:T(8,128)(2,1)S(1)} %pad_maximum_fusion.2.refs_0_), channel_id=1, source_target_pairs={{0,4},{2,6},{4,0},{6,2},{8,12},{10,14},{12,8},{14,10},{16,20},{18,... | collective-permute-start | bytes 196616 | tf_op jit(solution)/shard_map/ppermute | solution.py:589
  18.7 0.3 collective-permute-start.3
  19.0 0.3 multiply_cosine_fusion
  19.4 8.6 %collective-permute-done.5.refs_3_ = bf16[4,8,1024]{2,1,0:T(8,128)(2,1)S(1)} collective-permute-done((bf16[4,8,1024]{2,1,0:T(8,128)(2,1)S(1)}, bf16[4,8,1024]{2,1,0:T(8,128)(2,1)S(1)}, u32[]{:S(2)}, u32[]{:S(2)}) %collective-permute-start.5) | collective-permute-done | bytes 65568 | tf_op jit(solution)/shard_map/ppermute | solution.py:589
  27.9 6.9 %collective-permute-done.4.refs_2_ = bf16[4,8,1024]{2,1,0:T(8,128)(2,1)S(1)} collective-permute-done((bf16[4,8,1024]{2,1,0:T(8,128)(2,1)S(1)}, bf16[4,8,1024]{2,1,0:T(8,128)(2,1)S(1)}, u32[]{:S(2)}, u32[]{:S(2)}) %collective-permute-start.4) | collective-permute-done | bytes 65568 | tf_op jit(solution)/shard_map/ppermute | solution.py:589
  35.1 0.3 reduce_window_sum.14
  35.4 0.4 select_reduce_fusion.2
  35.9 0.1 sub.74
  36.0 0.1 sub.73
  36.4 0.1 mul.162
  36.5 0.1 fusion.8
  36.6 0.1 select_reduce_fusion.3
  36.7 0.1 fusion.9
  36.8 0.1 select_n.77.key_req_ref
  36.9 6.8 %all_gather.3 = bf16[128,2048]{1,0:T(8,128)(2,1)S(1)} all-gather(bf16[128,1024]{1,0:T(8,128)(2,1)S(1)} %bitcast.59), channel_id=1, replica_groups=mesh['seq'=16,'tp'=2] {'tp'}, dimensions={1}, use_global_device_ids=true | all-gather | bytes 786432 | tf_op jit(solution)/shard_map/all_gather | solution.py:643
  43.7 0.2 fusion
  43.9 3.1 %convolution_bitcast_fusion = f32[16,8,8,128]{3,1,2,0:T(8,128)S(1)} fusion(bf16[2048,1024]{1,0:T(8,128)(2,1)} %param.13, bf16[128,2048]{1,0:T(8,128)(2,1)S(1)} %all_gather.3, f32[2048]{0:T(1024)S(1)} %copy-done.6, f32[128]{0:T(128)S(1)} %add_rsqrt_fusion), kind=kOutput, calls=%fused_computation.2 | convolution fusion | flops 537919488 | bytes 5251584 | tf_op jit(solution)/shard_map/dot_general | solution.py:57
  47.0 0.1 copy.22
  47.2 0.3 subtract_convert_fusion
  47.5 0.1 pad_maximum_fusion
  47.7 0.8 convolution_bitcast_fusion.1
  48.5 0.1 reshape_squeeze.3
  48.6 0.3 subtract_convert_fusion.1
  48.9 0.2 pad_maximum_fusion.1
  49.2 2.0 %copy-done = bf16[2,112,16,512]{3,2,1,0:T(8,128)(2,1)S(1)} copy-done((bf16[2,112,16,512]{3,2,1,0:T(8,128)(2,1)S(1)}, bf16[2,112,16,512]{3,2,1,0:T(8,128)(2,1)}, u32[]{:S(2)}) %copy-start) | copy-done | bytes 3670040
  51.2 4.7 %attend.1 = (bf16[4,16,512]{2,1,0:T(8,128)(2,1)S(1)}, bf16[4,16,512]{2,1,0:T(8,128)(2,1)S(1)}, bf16[4,16,512]{2,1,0:T(8,128)(2,1)S(1)}, bf16[4,16,512]{2,1,0:T(8,128)(2,1)S(1)}) custom-call(s32[1]{0:T(128)} %bitcast.index_ref, bf16[128,1024]{1,0:T(8,128)(2,1)S(1)} %bitcast.60, bf16[128,512]{1,0:T(8,128)(2,1)S(1)} %get-tuple-element.62.key_new_ref, ...), custom_call_target="tpu_custom_call" | custom-call | flops 939524096 | bytes 7340032 | tf_op jit(solution)/shard_map/attend/pallas_call | solution.py:423
  55.9 2.3 %collective-permute-start.6 = (bf16[4,16,512]{2,1,0:T(8,128)(2,1)S(1)}, bf16[4,16,512]{2,1,0:T(8,128)(2,1)S(1)}, u32[]{:S(2)}, u32[]{:S(2)}) collective-permute-start(bf16[4,16,512]{2,1,0:T(8,128)(2,1)S(1)} %get-tuple-element.33), channel_id=1, source_target_pairs={{0,2},{2,0},{4,6},{6,4},{8,10},{10,8},{12,14},{14,12},{16,18},{18,... | collective-permute-start | bytes 196616 | tf_op jit(solution)/shard_map/ppermute | solution.py:589
  58.2 2.2 %collective-permute-start.7 = (bf16[4,16,512]{2,1,0:T(8,128)(2,1)S(1)}, bf16[4,16,512]{2,1,0:T(8,128)(2,1)S(1)}, u32[]{:S(2)}, u32[]{:S(2)}) collective-permute-start(bf16[4,16,512]{2,1,0:T(8,128)(2,1)S(1)} %get-tuple-element.34), channel_id=1, source_target_pairs={{0,4},{2,6},{4,0},{6,2},{8,12},{10,14},{12,8},{14,10},{16,20},{18,... | collective-permute-start | bytes 196616 | tf_op jit(solution)/shard_map/ppermute | solution.py:589
  60.4 5.4 %place_kept.1 = (bf16[2,112,16,512]{3,2,1,0:T(8,128)(2,1)}, f32[8,128]{1,0:T(8,128)S(1)}) custom-call(s32[3,112]{1,0:T(4,128)S(1)} %pad_add_fusion.1.table_ref, bf16[2,112,16,512]{3,2,1,0:T(8,128)(2,1)S(1)} %copy-done, f32[128,512]{1,0:T(8,128)S(1)} %get-tuple-element.63.key_ref, f32[128,512]{1,0:T(8,128)S(1)} %get-tuple-element.50.value_ref, ...), custom_call_target="tpu_custom_call" | custom-call | bytes 11010048 | tf_op jit(solution)/shard_map/place_kept/pallas_call | solution.py:262
  65.7 0.4 collective-permute-done.6.rest_1_
  66.1 5.5 %collective-permute-done.8.rest_3_ = bf16[4,16,512]{2,1,0:T(8,128)(2,1)S(1)} collective-permute-done((bf16[4,16,512]{2,1,0:T(8,128)(2,1)S(1)}, bf16[4,16,512]{2,1,0:T(8,128)(2,1)S(1)}, u32[]{:S(2)}, u32[]{:S(2)}) %collective-permute-start.8) | collective-permute-done | bytes 65568 | tf_op jit(solution)/shard_map/ppermute | solution.py:589
  71.6 1.0 merge.1
  72.6 2.0 %copy-done.2 = bf16[1024,2048]{1,0:T(8,128)(2,1)} copy-done((bf16[1024,2048]{1,0:T(8,128)(2,1)}, bf16[1024,2048]{1,0:T(8,128)(2,1)S(1)}, u32[]{:S(2)}) %copy-start.2) | copy-done | bytes 4194328
  74.6 18.5 %collective-permute-start.10 = (bf16[16,512]{1,0:T(8,128)(2,1)S(1)}, bf16[16,512]{1,0:T(8,128)(2,1)S(1)}, u32[]{:S(2)}, u32[]{:S(2)}) collective-permute-start(bf16[16,512]{1,0:T(8,128)(2,1)S(1)} %get-tuple-element.38), channel_id=1, source_target_pairs={{0,16},{2,18},{4,20},{6,22},{8,24},{10,26},{12,28},{14,30},{16,0},... | collective-permute-start | bytes 49160 | tf_op jit(solution)/shard_map/ppermute | solution.py:589
  93.0 1.2 %collective-permute-start.11 = (bf16[16,512]{1,0:T(8,128)(2,1)S(1)}, bf16[16,512]{1,0:T(8,128)(2,1)S(1)}, u32[]{:S(2)}, u32[]{:S(2)}) collective-permute-start(bf16[16,512]{1,0:T(8,128)(2,1)S(1)} %get-tuple-element.39), channel_id=1, source_target_pairs={{0,24},{2,26},{4,28},{6,30},{8,16},{10,18},{12,20},{14,22},{16,8},... | collective-permute-start | bytes 49160 | tf_op jit(solution)/shard_map/ppermute | solution.py:589
  94.3 4.9 %collective-permute-done.10.refs_2_ = bf16[16,512]{1,0:T(8,128)(2,1)S(1)} collective-permute-done((bf16[16,512]{1,0:T(8,128)(2,1)S(1)}, bf16[16,512]{1,0:T(8,128)(2,1)S(1)}, u32[]{:S(2)}, u32[]{:S(2)}) %collective-permute-start.10) | collective-permute-done | bytes 16416 | tf_op jit(solution)/shard_map/ppermute | solution.py:589
  99.2 2.2 %copy-done.3 = bf16[1024,2048]{1,0:T(8,128)(2,1)S(1)} copy-done((bf16[1024,2048]{1,0:T(8,128)(2,1)S(1)}, bf16[1024,2048]{1,0:T(8,128)(2,1)}, u32[]{:S(2)}) %copy-start.3) | copy-done | bytes 4194328
  101.4 0.9 combine.1
  102.3 1.9 %collective-permute-start.12 = (bf16[8,1024]{1,0:T(8,128)(2,1)S(1)}, bf16[8,1024]{1,0:T(8,128)(2,1)S(1)}, u32[]{:S(2)}, u32[]{:S(2)}) collective-permute-start(bf16[8,1024]{1,0:T(8,128)(2,1)S(1)} %get-tuple-element.42), channel_id=1, source_target_pairs={{0,1},{1,0},{2,3},{3,2},{4,5},{5,4},{6,7},{7,6},{8,9},{9,8},{10,11... | collective-permute-start | bytes 49160 | tf_op jit(solution)/shard_map/ppermute | solution.py:589
  104.3 4.7 %place_landed.1 = (bf16[2,112,16,512]{3,2,1,0:T(8,128)(2,1)}, f32[8,128]{1,0:T(8,128)S(1)}) custom-call(s32[3,112]{1,0:T(4,128)S(1)} %pad_add_fusion.table_ref, bf16[224,16,512]{2,1,0:T(8,128)(2,1)} %bitcast.11.held_ref, f32[128,512]{1,0:T(8,128)S(1)} %get-tuple-element.63.key_ref, ...), custom_call_target="tpu_custom_call", output_to_operand_aliasing={{0}: (4, {})} | custom-call | bytes 11010048 | tf_op jit(solution)/shard_map/place_landed/pallas_call | solution.py:313
  109.0 0.6 close.1
  (65 shorter events, 1.0 us)
Async XLA Ops:
  2.0 6.4 %collective-permute-start.2 = (bf16[8,1024]{1,0:T(8,128)(2,1)}, bf16[8,1024]{1,0:T(8,128)(2,1)S(1)}, u32[]{:S(2)}, u32[]{:S(2)}) collective-permute-start(bf16[8,1024]{1,0:T(8,128)(2,1)} %make_note.1), channel_id=1, source_target_pairs={{0,24},{2,26},{4,28},{6,30},{8,16},{10,18},{12,20},{14,22},{16,8},... | collective-permute-start | bytes 49160 | tf_op jit(solution)/shard_map/ppermute | solution.py:589
  5.3 3.7 %collective-permute-start.1 = (bf16[8,1024]{1,0:T(8,128)(2,1)}, bf16[8,1024]{1,0:T(8,128)(2,1)S(1)}, u32[]{:S(2)}, u32[]{:S(2)}) collective-permute-start(bf16[8,1024]{1,0:T(8,128)(2,1)} %make_note.1), channel_id=1, source_target_pairs={{0,16},{2,18},{4,20},{6,22},{8,24},{10,26},{12,28},{14,30},{16,0},... | collective-permute-start | bytes 49160 | tf_op jit(solution)/shard_map/ppermute | solution.py:589
  5.3 3.7 %collective-permute-start = (bf16[8,1024]{1,0:T(8,128)(2,1)}, bf16[8,1024]{1,0:T(8,128)(2,1)S(1)}, u32[]{:S(2)}, u32[]{:S(2)}) collective-permute-start(bf16[8,1024]{1,0:T(8,128)(2,1)} %make_note.1), channel_id=1, source_target_pairs={{0,8},{2,10},{4,12},{6,14},{8,0},{10,2},{12,4},{14,6},{16,24},{18,... | collective-permute-start | bytes 49160 | tf_op jit(solution)/shard_map/ppermute | solution.py:589
  8.3 7.8 %copy-start.7 = (s32[112,2]{0,1:T(2,128)S(1)}, s32[112,2]{0,1:T(2,128)}, u32[]{:S(2)}) copy-start(s32[112,2]{0,1:T(2,128)} %param.17) | copy-start | bytes 2692
  8.3 7.9 %copy-start.5 = (bf16[8,1024]{1,0:T(8,128)(2,1)S(1)}, bf16[8,1024]{1,0:T(8,128)(2,1)}, u32[]{:S(2)}) copy-start(bf16[8,1024]{1,0:T(8,128)(2,1)} %make_note.1) | copy-start | bytes 49156
  8.4 10.6 %copy-start.9 = (s32[24]{0:T(128)S(1)}, s32[24]{0:T(128)}, u32[]{:S(2)}) copy-start(s32[24]{0:T(128)} %param.19) | copy-start | bytes 292
  8.4 10.6 %copy-start.11 = (s32[128]{0:T(128)S(1)}, s32[128]{0:T(128)}, u32[]{:S(2)}) copy-start(s32[128]{0:T(128)} %constant.63.clone) | copy-start | bytes 1540
  8.4 10.7 %copy-start.10 = (s32[128]{0:T(128)S(1)}, s32[128]{0:T(128)}, u32[]{:S(2)}) copy-start(s32[128]{0:T(128)} %constant.64.clone) | copy-start | bytes 1540
  8.4 28.2 %copy-start.8 = (s32[112]{0:T(128)S(1)}, s32[112]{0:T(128)}, u32[]{:S(2)}) copy-start(s32[112]{0:T(128)} %dest_ref.1) | copy-start | bytes 1348
  8.4 35.5 %copy-start.6 = (f32[2048]{0:T(1024)S(1)}, f32[2048]{0:T(1024)}, u32[]{:S(2)}) copy-start(f32[2048]{0:T(1024)} %param.12) | copy-start | bytes 24580
  9.0 95.2 %all-to-all-start = ((bf16[16,14,16,512]{3,2,1,0:T(8,128)(2,1)}), bf16[16,14,16,512]{3,2,1,0:T(8,128)(2,1)}, u32[]{:S(2)}, u32[]{:S(2)}) async-start(bf16[16,14,16,512]{3,2,1,0:T(8,128)(2,1)} %pack_pages.1), calls=%async_computation | async-start | bytes 7340032 | tf_op jit(solution)/shard_map/all_to_all | solution.py:640
  16.2 11.7 %collective-permute-start.5 = (bf16[4,8,1024]{2,1,0:T(8,128)(2,1)S(1)}, bf16[4,8,1024]{2,1,0:T(8,128)(2,1)S(1)}, u32[]{:S(2)}, u32[]{:S(2)}) collective-permute-start(bf16[4,8,1024]{2,1,0:T(8,128)(2,1)S(1)} %pad_maximum_fusion.2.refs_0_), channel_id=1, source_target_pairs={{0,6},{2,4},{4,2},{6,0},{8,14},{10,12},{12,10},{14,8},{16,22},{18,... | collective-permute-start | bytes 196616 | tf_op jit(solution)/shard_map/ppermute | solution.py:589
  17.5 17.4 %collective-permute-start.4 = (bf16[4,8,1024]{2,1,0:T(8,128)(2,1)S(1)}, bf16[4,8,1024]{2,1,0:T(8,128)(2,1)S(1)}, u32[]{:S(2)}, u32[]{:S(2)}) collective-permute-start(bf16[4,8,1024]{2,1,0:T(8,128)(2,1)S(1)} %pad_maximum_fusion.2.refs_0_), channel_id=1, source_target_pairs={{0,4},{2,6},{4,0},{6,2},{8,12},{10,14},{12,8},{14,10},{16,20},{18,... | collective-permute-start | bytes 196616 | tf_op jit(solution)/shard_map/ppermute | solution.py:589
  18.7 16.2 %collective-permute-start.3 = (bf16[4,8,1024]{2,1,0:T(8,128)(2,1)S(1)}, bf16[4,8,1024]{2,1,0:T(8,128)(2,1)S(1)}, u32[]{:S(2)}, u32[]{:S(2)}) collective-permute-start(bf16[4,8,1024]{2,1,0:T(8,128)(2,1)S(1)} %pad_maximum_fusion.2.refs_0_), channel_id=1, source_target_pairs={{0,2},{2,0},{4,6},{6,4},{8,10},{10,8},{12,14},{14,12},{16,18},{18,... | collective-permute-start | bytes 196616 | tf_op jit(solution)/shard_map/ppermute | solution.py:589
  43.9 3.8 %copy-start.4 = (bf16[2,2048,512]{2,1,0:T(8,128)(2,1)S(1)}, bf16[2,2048,512]{2,1,0:T(8,128)(2,1)}, u32[]{:S(2)}) copy-start(bf16[2,2048,512]{2,1,0:T(8,128)(2,1)} %param.14) | copy-start | bytes 12582916
  49.2 2.0 %copy-start = (bf16[2,112,16,512]{3,2,1,0:T(8,128)(2,1)S(1)}, bf16[2,112,16,512]{3,2,1,0:T(8,128)(2,1)}, u32[]{:S(2)}) copy-start(bf16[2,112,16,512]{3,2,1,0:T(8,128)(2,1)} %pool_ref.5) | copy-start | bytes 11010052
  51.2 20.4 %copy-start.1 = (bf16[1024,2048]{1,0:T(8,128)(2,1)S(1)}, bf16[1024,2048]{1,0:T(8,128)(2,1)}, u32[]{:S(2)}) copy-start(bf16[1024,2048]{1,0:T(8,128)(2,1)} %weight_ref.1) | copy-start | bytes 12582916
  55.9 10.2 %collective-permute-start.6 = (bf16[4,16,512]{2,1,0:T(8,128)(2,1)S(1)}, bf16[4,16,512]{2,1,0:T(8,128)(2,1)S(1)}, u32[]{:S(2)}, u32[]{:S(2)}) collective-permute-start(bf16[4,16,512]{2,1,0:T(8,128)(2,1)S(1)} %get-tuple-element.33), channel_id=1, source_target_pairs={{0,2},{2,0},{4,6},{6,4},{8,10},{10,8},{12,14},{14,12},{16,18},{18,... | collective-permute-start | bytes 196616 | tf_op jit(solution)/shard_map/ppermute | solution.py:589
  58.2 8.0 %collective-permute-start.7 = (bf16[4,16,512]{2,1,0:T(8,128)(2,1)S(1)}, bf16[4,16,512]{2,1,0:T(8,128)(2,1)S(1)}, u32[]{:S(2)}, u32[]{:S(2)}) collective-permute-start(bf16[4,16,512]{2,1,0:T(8,128)(2,1)S(1)} %get-tuple-element.34), channel_id=1, source_target_pairs={{0,4},{2,6},{4,0},{6,2},{8,12},{10,14},{12,8},{14,10},{16,20},{18,... | collective-permute-start | bytes 196616 | tf_op jit(solution)/shard_map/ppermute | solution.py:589
  60.3 11.3 %collective-permute-start.8 = (bf16[4,16,512]{2,1,0:T(8,128)(2,1)S(1)}, bf16[4,16,512]{2,1,0:T(8,128)(2,1)S(1)}, u32[]{:S(2)}, u32[]{:S(2)}) collective-permute-start(bf16[4,16,512]{2,1,0:T(8,128)(2,1)S(1)} %get-tuple-element.35), channel_id=1, source_target_pairs={{0,6},{2,4},{4,2},{6,0},{8,14},{10,12},{12,10},{14,8},{16,22},{18,... | collective-permute-start | bytes 196616 | tf_op jit(solution)/shard_map/ppermute | solution.py:589
  72.6 2.0 %copy-start.2 = (bf16[1024,2048]{1,0:T(8,128)(2,1)}, bf16[1024,2048]{1,0:T(8,128)(2,1)S(1)}, u32[]{:S(2)}) copy-start(bf16[1024,2048]{1,0:T(8,128)(2,1)S(1)} %get-tuple-element.40.refs_4_) | copy-start | bytes 12582916
  74.6 19.7 %collective-permute-start.9 = (bf16[16,512]{1,0:T(8,128)(2,1)S(1)}, bf16[16,512]{1,0:T(8,128)(2,1)S(1)}, u32[]{:S(2)}, u32[]{:S(2)}) collective-permute-start(bf16[16,512]{1,0:T(8,128)(2,1)S(1)} %get-tuple-element.37), channel_id=1, source_target_pairs={{0,8},{2,10},{4,12},{6,14},{8,0},{10,2},{12,4},{14,6},{16,24},{18,... | collective-permute-start | bytes 49160 | tf_op jit(solution)/shard_map/ppermute | solution.py:589
  74.6 24.7 %collective-permute-start.10 = (bf16[16,512]{1,0:T(8,128)(2,1)S(1)}, bf16[16,512]{1,0:T(8,128)(2,1)S(1)}, u32[]{:S(2)}, u32[]{:S(2)}) collective-permute-start(bf16[16,512]{1,0:T(8,128)(2,1)S(1)} %get-tuple-element.38), channel_id=1, source_target_pairs={{0,16},{2,18},{4,20},{6,22},{8,24},{10,26},{12,28},{14,30},{16,0},... | collective-permute-start | bytes 49160 | tf_op jit(solution)/shard_map/ppermute | solution.py:589
  93.0 6.2 %collective-permute-start.11 = (bf16[16,512]{1,0:T(8,128)(2,1)S(1)}, bf16[16,512]{1,0:T(8,128)(2,1)S(1)}, u32[]{:S(2)}, u32[]{:S(2)}) collective-permute-start(bf16[16,512]{1,0:T(8,128)(2,1)S(1)} %get-tuple-element.39), channel_id=1, source_target_pairs={{0,24},{2,26},{4,28},{6,30},{8,16},{10,18},{12,20},{14,22},{16,8},... | collective-permute-start | bytes 49160 | tf_op jit(solution)/shard_map/ppermute | solution.py:589
  99.2 2.2 %copy-start.3 = (bf16[1024,2048]{1,0:T(8,128)(2,1)S(1)}, bf16[1024,2048]{1,0:T(8,128)(2,1)}, u32[]{:S(2)}) copy-start(bf16[1024,2048]{1,0:T(8,128)(2,1)} %copy-done.2) | copy-start | bytes 12582916
  102.3 6.7 %collective-permute-start.12 = (bf16[8,1024]{1,0:T(8,128)(2,1)S(1)}, bf16[8,1024]{1,0:T(8,128)(2,1)S(1)}, u32[]{:S(2)}, u32[]{:S(2)}) collective-permute-start(bf16[8,1024]{1,0:T(8,128)(2,1)S(1)} %get-tuple-element.42), channel_id=1, source_target_pairs={{0,1},{1,0},{2,3},{3,2},{4,5},{5,4},{6,7},{7,6},{8,9},{9,8},{10,11... | collective-permute-start | bytes 49160 | tf_op jit(solution)/shard_map/ppermute | solution.py:589

commit v4 on v3

--- a/solution.py
+++ b/solution.py
@@ -103,7 +103,7 @@
             out_ref[(far ^ step) * inner + (near ^ shift)] = part_ref[step]
 
 
-def sort_notes(my_index, parts):
+def sort_notes(my_place, parts):
     inner = len(parts)
     far_count, rows, width = parts[0].shape
     vmem = pl.BlockSpec(memory_space=pltpu.VMEM)
@@ -114,7 +114,7 @@
         out_specs=vmem,
         compiler_params=pltpu.CompilerParams(vmem_limit_bytes=16 * 2**20),
         name="sort_notes",
-    )(my_index.reshape(1).astype(jnp.int32), *parts)
+    )(my_place, *parts)
 
 
 def read_notes(notes, row_count, slot_count):
@@ -219,7 +219,7 @@
 KEPT, BLANK, LANDED = 0, 1, 2
 
 
-def keep_body(row_count, table_ref, pool_ref, key_ref, value_ref, after_ref, out_ref, mark_ref):
+def keep_body(row_count, table_ref, pool_ref, key_ref, value_ref, after_ref, ready_ref, out_ref, mark_ref):
     mark_ref[...] = jnp.zeros_like(mark_ref)
 
     def fill(slot, carry):
@@ -257,51 +257,64 @@
 MARK = jax.ShapeDtypeStruct((CHUNK_ROWS, LANES), jnp.float32)
 
 
-def place_kept(row_count, table, kv_pool, key_new, value_new, after):
+def place_kept(row_count, table, kv_pool, key_new, value_new, after, ready):
     vmem = pl.BlockSpec(memory_space=pltpu.VMEM)
     return pl.pallas_call(
         functools.partial(keep_body, row_count),
         out_shape=(jax.ShapeDtypeStruct(kv_pool.shape, kv_pool.dtype), MARK),
         in_specs=[pl.BlockSpec(memory_space=pltpu.SMEM)]
         + [vmem] * 3
-        + [pl.BlockSpec(memory_space=pl.ANY)],
+        + [pl.BlockSpec(memory_space=pl.ANY)] * 2,
         out_specs=(vmem, vmem),
         compiler_params=pltpu.CompilerParams(vmem_limit_bytes=24 * 2**20),
         cost_estimate=moved(3 * kv_pool.size),
         name="place_kept",
-    )(table, kv_pool, key_new, value_new, after)
+    )(table, kv_pool, key_new, value_new, after, ready)
+
+
+LAND_CUTS = 7
 
 
 def land_body(
-    row_count, capacity, table_ref, held_ref, key_ref, value_ref, begun_ref, out_ref, mark_ref,
-    stage_ref, sem,
+    row_count, capacity, table_ref, arrived_ref, key_ref, value_ref, begun_ref, out_ref, mark_ref,
+    held_ref, load_sem, sem,
 ):
     places = table_ref.shape[1]
+    edges = [places * cut // LAND_CUTS for cut in range(LAND_CUTS + 1)]
+    loads = []
+    for cut in range(LAND_CUTS):
+        span = pl.ds(2 * edges[cut], 2 * (edges[cut + 1] - edges[cut]))
+        load = pltpu.make_async_copy(arrived_ref.at[span], held_ref.at[span], load_sem.at[cut])
+        load.start()
+        loads.append(load)
     mark_ref[...] = jnp.zeros_like(mark_ref)
 
     def send(place, count):
         slot = table_ref[0, place]
         req = table_ref[1, place]
 
-        @pl.when((slot >= 0) & (req < 0))
+        @pl.when(slot >= 0)
         def _():
+            @pl.when(req >= 0)
+            def _():
+                first = table_ref[2, place]
+                for which, fresh_ref in ((0, key_ref), (1, value_ref)):
+                    held_ref[2 * place + which] = patched(
+                        held_ref[2 * place + which], fresh_ref, row_count, req, first
+                    )
+
             pltpu.make_async_copy(
                 held_ref.at[pl.ds(2 * place, 2)], out_ref.at[:, slot], sem
             ).start()
 
-        @pl.when((slot >= 0) & (req >= 0))
-        def _():
-            first = table_ref[2, place]
-            for which, fresh_ref in ((0, key_ref), (1, value_ref)):
-                stage_ref[slot, which] = patched(
-                    held_ref[2 * place + which], fresh_ref, row_count, req, first
-                )
-            pltpu.make_async_copy(stage_ref.at[slot], out_ref.at[:, slot], sem).start()
-
         return count + (slot >= 0).astype(jnp.int32)
 
-    count = lax.fori_loop(0, places, send, 0)
-    wait_pages(stage_ref.at[pl.ds(0, capacity)], stage_ref.at[0], capacity, count, sem)
+    count = 0
+    for cut, load in enumerate(loads):
+        load.wait()
+        count = lax.fori_loop(edges[cut], edges[cut + 1], send, count)
+    group = held_ref.at[pl.ds(0, 2 * capacity)]
+    wait_pages(group, held_ref.at[pl.ds(0, 2)], capacity, count, sem)
 
 
 def place_landed(row_count, table, begun, arrived, key_new, value_new):
@@ -313,17 +326,18 @@
     return pl.pallas_call(
         functools.partial(land_body, row_count, capacity),
         out_shape=(jax.ShapeDtypeStruct(begun.shape, begun.dtype), MARK),
-        in_specs=[pl.BlockSpec(memory_space=pltpu.SMEM), vmem, vmem, vmem, hbm],
+        in_specs=[pl.BlockSpec(memory_space=pltpu.SMEM), hbm, vmem, vmem, hbm],
         out_specs=(hbm, vmem),
         scratch_shapes=[
-            pltpu.VMEM((slot_count, 2, page_size, width), begun.dtype),
+            pltpu.VMEM(arrived.shape, begun.dtype),
+            pltpu.SemaphoreType.DMA((LAND_CUTS,)),
             pltpu.SemaphoreType.DMA,
         ],
         input_output_aliases={4: 0},
         compiler_params=pltpu.CompilerParams(vmem_limit_bytes=32 * 2**20),
         cost_estimate=moved(3 * begun.size),
         name="place_landed",
-    )(table, pltpu.with_memory_space_constraint(arrived, pltpu.VMEM), key_new, value_new, begun)
+    )(table, arrived, key_new, value_new, begun)
 
 
 def split_parts(value):
@@ -410,7 +424,7 @@
 
 
 def attend(
-    my_index, seq_count, inner, row_count, queries, key_new, value_new, key_req, kv_pool
+    my_place, seq_count, inner, row_count, queries, key_new, value_new, key_req, kv_pool
 ):
     slot_count, page_size, width = kv_pool.shape[1:]
     kv_count = width // HD
@@ -430,11 +444,11 @@
             pltpu.VMEM((rows, q_width), jnp.float32),
             pltpu.VMEM((seq_count, page_size, width), jnp.bfloat16),
         ],
-        compiler_params=pltpu.CompilerParams(vmem_limit_bytes=36 * 2**20),
+        compiler_params=pltpu.CompilerParams(vmem_limit_bytes=48 * 2**20),
         cost_estimate=moved(2 * kv_pool.size, 4 * rows * q_width * slot_count * page_size),
         name="attend",
     )(
-        my_index.reshape(1).astype(jnp.int32), queries, key_new, value_new, key_req, kv_pool
+        my_place, queries, key_new, value_new, key_req, kv_pool
     )
 
 
@@ -511,7 +525,7 @@
     load.wait()
 
 
-def merge(my_index, mark, w_out, parts, q_count, row_count):
+def merge(my_place, mark, w_out, parts, q_count, row_count):
     far_count, page_size, width = parts[0].shape
     vmem = pl.BlockSpec(memory_space=pltpu.VMEM)
     unit = jax.ShapeDtypeStruct((page_size, width), jnp.bfloat16)
@@ -532,7 +546,7 @@
         compiler_params=pltpu.CompilerParams(vmem_limit_bytes=24 * 2**20),
         cost_estimate=moved(3 * 2**20),
         name="merge",
-    )(my_index.reshape(1).astype(jnp.int32), mark, w_out, *parts)
+    )(my_place, mark, w_out, *parts)
 
 
 def combine_body(q_count, row_count, tp_count, index_ref, *refs):
@@ -546,11 +560,11 @@
     for shift, out_ref in enumerate(out_refs):
         chosen = blocks[0]
         for k in range(1, tp_count):
-            chosen = jnp.where((index_ref[0] ^ shift) == k, blocks[k], chosen)
+            chosen = jnp.where((index_ref[1] ^ shift) == k, blocks[k], chosen)
         out_ref[...] = chosen.astype(out_ref.dtype)
 
 
-def combine(tp_index, tp_count, parts, w_near, row_count):
+def combine(my_place, tp_count, parts, w_near, row_count):
     vmem = pl.BlockSpec(memory_space=pltpu.VMEM)
     block = jax.ShapeDtypeStruct((CHUNK_ROWS, w_near.shape[1] // tp_count), jnp.bfloat16)
     return pl.pallas_call(
@@ -561,7 +575,7 @@
         compiler_params=pltpu.CompilerParams(vmem_limit_bytes=24 * 2**20),
         cost_estimate=moved(2 * w_near.size),
         name="combine",
-    )(tp_index.reshape(1).astype(jnp.int32), *parts, w_near)
+    )(my_place, *parts, w_near)
 
 
 def close_body(mark_ref, *refs):
@@ -627,6 +641,7 @@
     seq_count = lax.axis_size("seq")
     tp_count = lax.axis_size("tp")
     my_index = lax.axis_index("seq")
+    my_place = jnp.stack([my_index, lax.axis_index("tp")]).astype(jnp.int32)
     row_count, token_width = tokens.shape
     slot_count, page_size = kv_pool.shape[1:3]
     capacity = -(-slot_count // seq_count)
@@ -636,7 +651,7 @@
     along = swap_all([note] * (seq_count // inner), inner, seq_count)
     outgoing = pack_pages(kv_pool, slot_dest, seq_count, capacity)
     outgoing, along, lengths = lax.optimization_barrier((outgoing, along, lengths))
-    notes = sort_notes(my_index, swap_all([jnp.stack(along)] * inner, 1, seq_count))
+    notes = sort_notes(my_place, swap_all([jnp.stack(along)] * inner, 1, seq_count))
     arrived = lax.all_to_all(outgoing, "seq", split_axis=0, concat_axis=0, tiled=True)
 
     seq_tokens = notes[:, :CHUNK_ROWS].reshape(seq_count * CHUNK_ROWS, token_width)
@@ -653,13 +668,13 @@
     position = slot_owner[:, 1][:, None] * page_size + jnp.arange(page_size, dtype=jnp.int32)[None, :]
     key_req = jnp.where(position < base_len[:, None], owner_req[:, None], -1).reshape(1, -1)
     payload = attend(
-        my_index, seq_count, inner, row_count, queries, key_new, value_new, key_req, kv_pool
+        my_place, seq_count, inner, row_count, queries, key_new, value_new, key_req, kv_pool
     )
-    begun, mark = place_kept(row_count, by_slot, kv_pool, key_wide, value_wide, payload[0])
+    begun, mark = place_kept(row_count, by_slot, kv_pool, key_wide, value_wide, payload[0], by_place)
     near = swap_all(payload, 1, seq_count)
-    *merged, w_near = merge(my_index, mark, w_out, near, w_query.shape[1] // HD, row_count)
+    *merged, w_near = merge(my_place, mark, w_out, near, w_query.shape[1] // HD, row_count)
     far = swap_all(merged, inner, seq_count)
-    columns = combine(lax.axis_index("tp"), tp_count, far, w_near, row_count)
+    columns = combine(my_place, tp_count, far, w_near, row_count)
     columns = swap_all(columns, 1, tp_count, "tp")
     kv_moved, mark = place_landed(row_count, by_place, begun, arrived, key_wide, value_wide)
     attn_out = close(mark, columns, row_count)

time: 109 us -> 106 us (0.972)
  local copies, waits for them, and re-layouts: 7.37 us -> 3.22 us
  Pallas kernels: 21.4 us -> 23.4 us
  waiting for transfers between devices: 26.8 us -> 25.5 us
    unnamed x27 -> x23, local copies, waits for them, and re-layouts: 6.4 us -> 2.24 us
    ppermute x13, waiting for transfers between devices: 26.8 us -> 25.5 us  [swap_all(): lax.ppermute(parts[k], axis, pairs[k])]
    pallas_call x1, Pallas kernels: 4.73 us -> 3.51 us  [place_landed(): pl.pallas_call(functools.partial(land_body, row_count, capacity), out_sha...]
    all_to_all x1, starting transfers between devices: 7.17 us -> 6.01 us  [local(): lax.all_to_all(outgoing, 'seq', split_axis=0, concat_axis=0, tiled=True)]
  transfers between devices with their start and end apart: 14 -> 14, of which waited for: 6 -> 4; matrix products, arithmetic and copies ran while one was open for 7% -> 7% of each run, Pallas kernels for 18% -> 20%
where the time goes in v4:
time: 106 us
  starting transfers between devices  39.2 us (37%)
  waiting for transfers between devices  25.5 us (24%)
  Pallas kernels  23.4 us (22%)
  blocking collectives  6.96 us (7%)
  matrix products  3.85 us (4%)
  local copies, waits for them, and re-layouts  3.22 us (3%)
  other arithmetic  2.87 us (3%)
  between operations  1.08 us (1%)
    ppermute x13, starting transfers between devices, swap_all(): lax.ppermute(parts[k], axis, pairs[k])  33.2 us
    ppermute x13, waiting for transfers between devices, swap_all(): lax.ppermute(parts[k], axis, pairs[k])  25.5 us
    all_gather x1, blocking collectives, local(): all_tokens = lax.all_gather(seq_tokens, 'tp', axis=1, tiled=True)  6.96 us
    all_to_all x1, starting transfers between devices, local(): lax.all_to_all(outgoing, 'seq', split_axis=0, concat_axis=0, tiled=True)  6.01 us
    pallas_call x1, Pallas kernels, attend(): pl.pallas_call(functools.partial(attend_body, kv_count, group_size, seq_c...  5.46 us
    pallas_call x1, Pallas kernels, place_kept(): pl.pallas_call(functools.partial(keep_body, row_count), out_shape=(jax.Sh...  5.2 us
    pallas_call x1, Pallas kernels, pack_pages(): pl.pallas_call(functools.partial(pack_body, slot_count, seq_count, capaci...  3.74 us
    pallas_call x1, Pallas kernels, place_landed(): pl.pallas_call(functools.partial(land_body, row_count, capacity), out_sha...  3.51 us
  transfers between devices with their start and end apart: 14, of which 4 were waited for; matrix products, arithmetic and copies ran while one was open for 7% of the time, Pallas kernels for 20%

profile of v4, /device:TPU:5, one launch (start us, length us, event | category | flops | bytes accessed | tf_op | source)
XLA Modules:
  0.0 106.1 jit_solution(13591354904245930407)
XLA Ops:
  0.6 1.4 %make_note.1 = bf16[8,1024]{1,0:T(8,128)(2,1)} custom-call(bf16[6,1024]{1,0:T(8,128)(2,1)} %token_ref.1, s32[1,112]{1,0:T(1,128)} %bitcast.74, s32[2,112]{1,0:T(2,128)} %bitcast.73), custom_call_target="tpu_custom_call" | custom-call | tf_op jit(solution)/shard_map/make_note/pallas_call | solution.py:88
  2.0 3.3 %collective-permute-start.2 = (bf16[8,1024]{1,0:T(8,128)(2,1)}, bf16[8,1024]{1,0:T(8,128)(2,1)S(1)}, u32[]{:S(2)}, u32[]{:S(2)}) collective-permute-start(bf16[8,1024]{1,0:T(8,128)(2,1)} %make_note.1), channel_id=1, source_target_pairs={{0,24},{2,26},{4,28},{6,30},{8,16},{10,18},{12,20},{14,22},{16,8},... | collective-permute-start | bytes 49160 | tf_op jit(solution)/shard_map/ppermute | solution.py:603
  5.3 0.3 collective-permute-start
  5.7 3.7 %pack_pages.1 = bf16[16,14,16,512]{3,2,1,0:T(8,128)(2,1)} custom-call(s32[112]{0:T(128)} %dest_ref.1, bf16[2,112,16,512]{3,2,1,0:T(8,128)(2,1)} %pool_ref.5), custom_call_target="tpu_custom_call" | custom-call | bytes 7340032 | tf_op jit(solution)/shard_map/pack_pages/pallas_call | solution.py:192
  9.5 6.0 %all-to-all-start = ((bf16[16,14,16,512]{3,2,1,0:T(8,128)(2,1)}), bf16[16,14,16,512]{3,2,1,0:T(8,128)(2,1)}, u32[]{:S(2)}, u32[]{:S(2)}) async-start(bf16[16,14,16,512]{3,2,1,0:T(8,128)(2,1)} %pack_pages.1), calls=%async_computation | async-start | bytes 7340032 | tf_op jit(solution)/shard_map/all_to_all | solution.py:655
  15.6 1.2 %collective-permute-start.5 = (bf16[4,8,1024]{2,1,0:T(8,128)(2,1)S(1)}, bf16[4,8,1024]{2,1,0:T(8,128)(2,1)S(1)}, u32[]{:S(2)}, u32[]{:S(2)}) collective-permute-start(bf16[4,8,1024]{2,1,0:T(8,128)(2,1)S(1)} %pad_maximum_fusion.2.refs_0_), channel_id=1, source_target_pairs={{0,6},{2,4},{4,2},{6,0},{8,14},{10,12},{12,10},{14,8},{16,22},{18,... | collective-permute-start | bytes 196616 | tf_op jit(solution)/shard_map/ppermute | solution.py:603
  16.9 1.2 %collective-permute-start.4 = (bf16[4,8,1024]{2,1,0:T(8,128)(2,1)S(1)}, bf16[4,8,1024]{2,1,0:T(8,128)(2,1)S(1)}, u32[]{:S(2)}, u32[]{:S(2)}) collective-permute-start(bf16[4,8,1024]{2,1,0:T(8,128)(2,1)S(1)} %pad_maximum_fusion.2.refs_0_), channel_id=1, source_target_pairs={{0,4},{2,6},{4,0},{6,2},{8,12},{10,14},{12,8},{14,10},{16,20},{18,... | collective-permute-start | bytes 196616 | tf_op jit(solution)/shard_map/ppermute | solution.py:603
  18.0 0.3 collective-permute-start.3
  18.3 0.1 select_reduce_fusion.5
  18.4 0.3 multiply_cosine_fusion
  18.7 8.6 %collective-permute-done.5.refs_3_ = bf16[4,8,1024]{2,1,0:T(8,128)(2,1)S(1)} collective-permute-done((bf16[4,8,1024]{2,1,0:T(8,128)(2,1)S(1)}, bf16[4,8,1024]{2,1,0:T(8,128)(2,1)S(1)}, u32[]{:S(2)}, u32[]{:S(2)}) %collective-permute-start.5) | collective-permute-done | bytes 65568 | tf_op jit(solution)/shard_map/ppermute | solution.py:603
  27.3 6.9 %collective-permute-done.4.refs_2_ = bf16[4,8,1024]{2,1,0:T(8,128)(2,1)S(1)} collective-permute-done((bf16[4,8,1024]{2,1,0:T(8,128)(2,1)S(1)}, bf16[4,8,1024]{2,1,0:T(8,128)(2,1)S(1)}, u32[]{:S(2)}, u32[]{:S(2)}) %collective-permute-start.4) | collective-permute-done | bytes 65568 | tf_op jit(solution)/shard_map/ppermute | solution.py:603
  34.2 0.6 sort_notes.1
  35.0 0.3 reduce_window_sum.14
  35.3 0.4 select_reduce_fusion.2
  35.9 0.1 sub.78
  36.0 0.1 sub.71
  36.2 0.1 sub.73
  36.4 0.1 mul.162
  36.5 0.1 fusion.8
  36.6 0.1 select_reduce_fusion.3
  36.7 0.1 fusion.9
  36.9 0.1 select_n.77.key_req_ref
  36.9 7.0 %all_gather.3 = bf16[128,2048]{1,0:T(8,128)(2,1)S(1)} all-gather(bf16[128,1024]{1,0:T(8,128)(2,1)S(1)} %bitcast.59), channel_id=1, replica_groups=mesh['seq'=16,'tp'=2] {'tp'}, dimensions={1}, use_global_device_ids=true | all-gather | bytes 786432 | tf_op jit(solution)/shard_map/all_gather | solution.py:658
  43.9 0.2 fusion
  44.1 3.1 %convolution_bitcast_fusion = f32[16,8,8,128]{3,1,2,0:T(8,128)S(1)} fusion(bf16[2048,1024]{1,0:T(8,128)(2,1)} %param.13, bf16[128,2048]{1,0:T(8,128)(2,1)S(1)} %all_gather.3, f32[2048]{0:T(1024)S(1)} %copy-done.4, f32[128]{0:T(128)S(1)} %add_rsqrt_fusion), kind=kOutput, calls=%fused_computation.2 | convolution fusion | flops 537919488 | bytes 5251584 | tf_op jit(solution)/shard_map/dot_general | solution.py:57
  47.2 0.1 copy.22
  47.3 0.3 subtract_convert_fusion
  47.6 0.1 pad_maximum_fusion
  47.8 0.8 convolution_bitcast_fusion.1
  48.6 0.1 reshape_squeeze.3
  48.7 0.3 subtract_convert_fusion.1
  49.1 0.2 pad_maximum_fusion.1
  49.3 2.0 %copy-done = bf16[2,112,16,512]{3,2,1,0:T(8,128)(2,1)S(1)} copy-done((bf16[2,112,16,512]{3,2,1,0:T(8,128)(2,1)S(1)}, bf16[2,112,16,512]{3,2,1,0:T(8,128)(2,1)}, u32[]{:S(2)}) %copy-start) | copy-done | bytes 3670040
  51.4 5.5 %attend.1 = (bf16[4,16,512]{2,1,0:T(8,128)(2,1)S(1)}, bf16[4,16,512]{2,1,0:T(8,128)(2,1)S(1)}, bf16[4,16,512]{2,1,0:T(8,128)(2,1)S(1)}, bf16[4,16,512]{2,1,0:T(8,128)(2,1)S(1)}) custom-call(s32[2]{0:T(128)S(1)} %pad_add_fusion.2.index_ref, bf16[128,1024]{1,0:T(8,128)(2,1)S(1)} %bitcast.60, bf16[128,512]{1,0:T(8,128)(2,1)S(1)} %get-tuple-element.62.key_new_ref, ...), custom_call_target="tpu_custom_call" | custom-call | flops 939524096 | bytes 7340032 | tf_op jit(solution)/shard_map/attend/pallas_call | solution.py:437
  56.8 2.3 %collective-permute-start.6 = (bf16[4,16,512]{2,1,0:T(8,128)(2,1)S(1)}, bf16[4,16,512]{2,1,0:T(8,128)(2,1)S(1)}, u32[]{:S(2)}, u32[]{:S(2)}) collective-permute-start(bf16[4,16,512]{2,1,0:T(8,128)(2,1)S(1)} %get-tuple-element.33), channel_id=1, source_target_pairs={{0,2},{2,0},{4,6},{6,4},{8,10},{10,8},{12,14},{14,12},{16,18},{18,... | collective-permute-start | bytes 196616 | tf_op jit(solution)/shard_map/ppermute | solution.py:603
  59.1 2.2 %collective-permute-start.7 = (bf16[4,16,512]{2,1,0:T(8,128)(2,1)S(1)}, bf16[4,16,512]{2,1,0:T(8,128)(2,1)S(1)}, u32[]{:S(2)}, u32[]{:S(2)}) collective-permute-start(bf16[4,16,512]{2,1,0:T(8,128)(2,1)S(1)} %get-tuple-element.34), channel_id=1, source_target_pairs={{0,4},{2,6},{4,0},{6,2},{8,12},{10,14},{12,8},{14,10},{16,20},{18,... | collective-permute-start | bytes 196616 | tf_op jit(solution)/shard_map/ppermute | solution.py:603
  61.4 5.2 %place_kept.1 = (bf16[2,112,16,512]{3,2,1,0:T(8,128)(2,1)}, f32[8,128]{1,0:T(8,128)S(1)}) custom-call(s32[3,112]{1,0:T(4,128)S(1)} %pad_add_fusion.1.table_ref, bf16[2,112,16,512]{3,2,1,0:T(8,128)(2,1)S(1)} %copy-done, f32[128,512]{1,0:T(8,128)S(1)} %get-tuple-element.63.key_ref, f32[128,512]{1,0:T(8,128)S(1)} %get-tuple-element.50.value_ref, ...), custom_call_target="tpu_custom_call" | custom-call | bytes 11010048 | tf_op jit(solution)/shard_map/place_kept/pallas_call | solution.py:262
  66.6 4.4 %collective-permute-done.8.rest_3_ = bf16[4,16,512]{2,1,0:T(8,128)(2,1)S(1)} collective-permute-done((bf16[4,16,512]{2,1,0:T(8,128)(2,1)S(1)}, bf16[4,16,512]{2,1,0:T(8,128)(2,1)S(1)}, u32[]{:S(2)}, u32[]{:S(2)}) %collective-permute-start.8) | collective-permute-done | bytes 65568 | tf_op jit(solution)/shard_map/ppermute | solution.py:603
  71.0 1.5 %merge.1 = (bf16[16,512]{1,0:T(8,128)(2,1)S(1)}, bf16[16,512]{1,0:T(8,128)(2,1)S(1)}, bf16[16,512]{1,0:T(8,128)(2,1)S(1)}, bf16[16,512]{1,0:T(8,128)(2,1)S(1)}, bf16[1024,2048]{1,0:T(8,128)(2,1)S(1)}) custom-call(s32[2]{0:T(128)S(1)} %pad_add_fusion.2.index_ref, f32[8,128]{1,0:T(8,128)S(1)} %get-tuple-element.32.mark_ref, bf16[1024,2048]{1,0:T(8,128)(2,1)S(1)} %copy-done.1, ...), custom_call_target="tpu_custom_call" | custom-call | bytes 6291456 | tf_op jit(solution)/shard_map/merge/pallas_call | solution.py:532
  72.5 1.2 %collective-permute-start.9 = (bf16[16,512]{1,0:T(8,128)(2,1)S(1)}, bf16[16,512]{1,0:T(8,128)(2,1)S(1)}, u32[]{:S(2)}, u32[]{:S(2)}) collective-permute-start(bf16[16,512]{1,0:T(8,128)(2,1)S(1)} %get-tuple-element.37), channel_id=1, source_target_pairs={{0,8},{2,10},{4,12},{6,14},{8,0},{10,2},{12,4},{14,6},{16,24},{18,... | collective-permute-start | bytes 49160 | tf_op jit(solution)/shard_map/ppermute | solution.py:603
  73.7 18.2 %collective-permute-start.10 = (bf16[16,512]{1,0:T(8,128)(2,1)S(1)}, bf16[16,512]{1,0:T(8,128)(2,1)S(1)}, u32[]{:S(2)}, u32[]{:S(2)}) collective-permute-start(bf16[16,512]{1,0:T(8,128)(2,1)S(1)} %get-tuple-element.38), channel_id=1, source_target_pairs={{0,16},{2,18},{4,20},{6,22},{8,24},{10,26},{12,28},{14,30},{16,0},... | collective-permute-start | bytes 49160 | tf_op jit(solution)/shard_map/ppermute | solution.py:603
  91.9 1.1 %collective-permute-start.11 = (bf16[16,512]{1,0:T(8,128)(2,1)S(1)}, bf16[16,512]{1,0:T(8,128)(2,1)S(1)}, u32[]{:S(2)}, u32[]{:S(2)}) collective-permute-start(bf16[16,512]{1,0:T(8,128)(2,1)S(1)} %get-tuple-element.39), channel_id=1, source_target_pairs={{0,24},{2,26},{4,28},{6,30},{8,16},{10,18},{12,20},{14,22},{16,8},... | collective-permute-start | bytes 49160 | tf_op jit(solution)/shard_map/ppermute | solution.py:603
  93.0 5.6 %collective-permute-done.10.refs_2_ = bf16[16,512]{1,0:T(8,128)(2,1)S(1)} collective-permute-done((bf16[16,512]{1,0:T(8,128)(2,1)S(1)}, bf16[16,512]{1,0:T(8,128)(2,1)S(1)}, u32[]{:S(2)}, u32[]{:S(2)}) %collective-permute-start.10) | collective-permute-done | bytes 16416 | tf_op jit(solution)/shard_map/ppermute | solution.py:603
  98.6 1.4 %combine.1 = (bf16[8,1024]{1,0:T(8,128)(2,1)S(1)}, bf16[8,1024]{1,0:T(8,128)(2,1)S(1)}) custom-call(s32[2]{0:T(128)S(1)} %pad_add_fusion.2.index_ref, bf16[16,512]{1,0:T(8,128)(2,1)S(1)} %get-tuple-element.36.refs_0_, bf16[16,512]{1,0:T(8,128)(2,1)S(1)} %collective-permute-done.9.refs_1_, bf16[16,512]{1,0:T(8,128)(2,1)S(1)} %collective-permute-done.10.refs_2_, ...), custom_call_target="tpu_custom_call" | custom-call | bytes 8388608 | tf_op jit(solution)/shard_map/combine/pallas_call | solution.py:570
  100.0 1.9 %collective-permute-start.12 = (bf16[8,1024]{1,0:T(8,128)(2,1)S(1)}, bf16[8,1024]{1,0:T(8,128)(2,1)S(1)}, u32[]{:S(2)}, u32[]{:S(2)}) collective-permute-start(bf16[8,1024]{1,0:T(8,128)(2,1)S(1)} %get-tuple-element.42), channel_id=1, source_target_pairs={{0,1},{1,0},{2,3},{3,2},{4,5},{5,4},{6,7},{7,6},{8,9},{9,8},{10,11... | collective-permute-start | bytes 49160 | tf_op jit(solution)/shard_map/ppermute | solution.py:603
  101.9 3.5 %place_landed.1 = (bf16[2,112,16,512]{3,2,1,0:T(8,128)(2,1)}, f32[8,128]{1,0:T(8,128)S(1)}) custom-call(s32[3,112]{1,0:T(4,128)S(1)} %pad_add_fusion.ready_ref.table_ref, bf16[224,16,512]{2,1,0:T(8,128)(2,1)} %bitcast.12.arrived_ref, f32[128,512]{1,0:T(8,128)S(1)} %get-tuple-element.63.key_ref, ...), custom_call_target="tpu_custom_call", output_to_operand_aliasing={{0}: (4, {})} | custom-call | bytes 11010048 | tf_op jit(solution)/shard_map/place_landed/pallas_call | solution.py:326
  105.5 0.6 close.1
  (62 shorter events, 0.9 us)
Async XLA Ops:
  2.0 7.5 %collective-permute-start.2 = (bf16[8,1024]{1,0:T(8,128)(2,1)}, bf16[8,1024]{1,0:T(8,128)(2,1)S(1)}, u32[]{:S(2)}, u32[]{:S(2)}) collective-permute-start(bf16[8,1024]{1,0:T(8,128)(2,1)} %make_note.1), channel_id=1, source_target_pairs={{0,24},{2,26},{4,28},{6,30},{8,16},{10,18},{12,20},{14,22},{16,8},... | collective-permute-start | bytes 49160 | tf_op jit(solution)/shard_map/ppermute | solution.py:603
  5.3 4.2 %collective-permute-start.1 = (bf16[8,1024]{1,0:T(8,128)(2,1)}, bf16[8,1024]{1,0:T(8,128)(2,1)S(1)}, u32[]{:S(2)}, u32[]{:S(2)}) collective-permute-start(bf16[8,1024]{1,0:T(8,128)(2,1)} %make_note.1), channel_id=1, source_target_pairs={{0,16},{2,18},{4,20},{6,22},{8,24},{10,26},{12,28},{14,30},{16,0},... | collective-permute-start | bytes 49160 | tf_op jit(solution)/shard_map/ppermute | solution.py:603
  5.3 4.2 %collective-permute-start = (bf16[8,1024]{1,0:T(8,128)(2,1)}, bf16[8,1024]{1,0:T(8,128)(2,1)S(1)}, u32[]{:S(2)}, u32[]{:S(2)}) collective-permute-start(bf16[8,1024]{1,0:T(8,128)(2,1)} %make_note.1), channel_id=1, source_target_pairs={{0,8},{2,10},{4,12},{6,14},{8,0},{10,2},{12,4},{14,6},{16,24},{18,... | collective-permute-start | bytes 49160 | tf_op jit(solution)/shard_map/ppermute | solution.py:603
  9.4 6.1 %copy-start.5 = (s32[112,2]{0,1:T(2,128)S(1)}, s32[112,2]{0,1:T(2,128)}, u32[]{:S(2)}) copy-start(s32[112,2]{0,1:T(2,128)} %param.17) | copy-start | bytes 2692
  9.4 6.1 %copy-start.3 = (bf16[8,1024]{1,0:T(8,128)(2,1)S(1)}, bf16[8,1024]{1,0:T(8,128)(2,1)}, u32[]{:S(2)}) copy-start(bf16[8,1024]{1,0:T(8,128)(2,1)} %make_note.1) | copy-start | bytes 49156
  9.5 8.9 %copy-start.7 = (s32[24]{0:T(128)S(1)}, s32[24]{0:T(128)}, u32[]{:S(2)}) copy-start(s32[24]{0:T(128)} %param.19) | copy-start | bytes 292
  9.5 8.9 %copy-start.9 = (s32[128]{0:T(128)S(1)}, s32[128]{0:T(128)}, u32[]{:S(2)}) copy-start(s32[128]{0:T(128)} %constant.63.clone) | copy-start | bytes 1540
  9.5 8.9 %copy-start.8 = (s32[128]{0:T(128)S(1)}, s32[128]{0:T(128)}, u32[]{:S(2)}) copy-start(s32[128]{0:T(128)} %constant.64.clone) | copy-start | bytes 1540
  9.5 27.1 %copy-start.6 = (s32[112]{0:T(128)S(1)}, s32[112]{0:T(128)}, u32[]{:S(2)}) copy-start(s32[112]{0:T(128)} %dest_ref.1) | copy-start | bytes 1348
  9.5 34.6 %copy-start.4 = (f32[2048]{0:T(1024)S(1)}, f32[2048]{0:T(1024)}, u32[]{:S(2)}) copy-start(f32[2048]{0:T(1024)} %param.12) | copy-start | bytes 24580
  9.5 92.4 %all-to-all-start = ((bf16[16,14,16,512]{3,2,1,0:T(8,128)(2,1)}), bf16[16,14,16,512]{3,2,1,0:T(8,128)(2,1)}, u32[]{:S(2)}, u32[]{:S(2)}) async-start(bf16[16,14,16,512]{3,2,1,0:T(8,128)(2,1)} %pack_pages.1), calls=%async_computation | async-start | bytes 7340032 | tf_op jit(solution)/shard_map/all_to_all | solution.py:655
  15.6 11.7 %collective-permute-start.5 = (bf16[4,8,1024]{2,1,0:T(8,128)(2,1)S(1)}, bf16[4,8,1024]{2,1,0:T(8,128)(2,1)S(1)}, u32[]{:S(2)}, u32[]{:S(2)}) collective-permute-start(bf16[4,8,1024]{2,1,0:T(8,128)(2,1)S(1)} %pad_maximum_fusion.2.refs_0_), channel_id=1, source_target_pairs={{0,6},{2,4},{4,2},{6,0},{8,14},{10,12},{12,10},{14,8},{16,22},{18,... | collective-permute-start | bytes 196616 | tf_op jit(solution)/shard_map/ppermute | solution.py:603
  16.9 17.4 %collective-permute-start.4 = (bf16[4,8,1024]{2,1,0:T(8,128)(2,1)S(1)}, bf16[4,8,1024]{2,1,0:T(8,128)(2,1)S(1)}, u32[]{:S(2)}, u32[]{:S(2)}) collective-permute-start(bf16[4,8,1024]{2,1,0:T(8,128)(2,1)S(1)} %pad_maximum_fusion.2.refs_0_), channel_id=1, source_target_pairs={{0,4},{2,6},{4,0},{6,2},{8,12},{10,14},{12,8},{14,10},{16,20},{18,... | collective-permute-start | bytes 196616 | tf_op jit(solution)/shard_map/ppermute | solution.py:603
  18.0 16.2 %collective-permute-start.3 = (bf16[4,8,1024]{2,1,0:T(8,128)(2,1)S(1)}, bf16[4,8,1024]{2,1,0:T(8,128)(2,1)S(1)}, u32[]{:S(2)}, u32[]{:S(2)}) collective-permute-start(bf16[4,8,1024]{2,1,0:T(8,128)(2,1)S(1)} %pad_maximum_fusion.2.refs_0_), channel_id=1, source_target_pairs={{0,2},{2,0},{4,6},{6,4},{8,10},{10,8},{12,14},{14,12},{16,18},{18,... | collective-permute-start | bytes 196616 | tf_op jit(solution)/shard_map/ppermute | solution.py:603
  44.1 3.7 %copy-start.2 = (bf16[2,2048,512]{2,1,0:T(8,128)(2,1)S(1)}, bf16[2,2048,512]{2,1,0:T(8,128)(2,1)}, u32[]{:S(2)}) copy-start(bf16[2,2048,512]{2,1,0:T(8,128)(2,1)} %param.14) | copy-start | bytes 12582916
  49.3 2.0 %copy-start = (bf16[2,112,16,512]{3,2,1,0:T(8,128)(2,1)S(1)}, bf16[2,112,16,512]{3,2,1,0:T(8,128)(2,1)}, u32[]{:S(2)}) copy-start(bf16[2,112,16,512]{3,2,1,0:T(8,128)(2,1)} %pool_ref.5) | copy-start | bytes 11010052
  51.4 19.6 %copy-start.1 = (bf16[1024,2048]{1,0:T(8,128)(2,1)S(1)}, bf16[1024,2048]{1,0:T(8,128)(2,1)}, u32[]{:S(2)}) copy-start(bf16[1024,2048]{1,0:T(8,128)(2,1)} %weight_ref.1) | copy-start | bytes 12582916
  56.8 9.7 %collective-permute-start.6 = (bf16[4,16,512]{2,1,0:T(8,128)(2,1)S(1)}, bf16[4,16,512]{2,1,0:T(8,128)(2,1)S(1)}, u32[]{:S(2)}, u32[]{:S(2)}) collective-permute-start(bf16[4,16,512]{2,1,0:T(8,128)(2,1)S(1)} %get-tuple-element.33), channel_id=1, source_target_pairs={{0,2},{2,0},{4,6},{6,4},{8,10},{10,8},{12,14},{14,12},{16,18},{18,... | collective-permute-start | bytes 196616 | tf_op jit(solution)/shard_map/ppermute | solution.py:603
  59.1 7.5 %collective-permute-start.7 = (bf16[4,16,512]{2,1,0:T(8,128)(2,1)S(1)}, bf16[4,16,512]{2,1,0:T(8,128)(2,1)S(1)}, u32[]{:S(2)}, u32[]{:S(2)}) collective-permute-start(bf16[4,16,512]{2,1,0:T(8,128)(2,1)S(1)} %get-tuple-element.34), channel_id=1, source_target_pairs={{0,4},{2,6},{4,0},{6,2},{8,12},{10,14},{12,8},{14,10},{16,20},{18,... | collective-permute-start | bytes 196616 | tf_op jit(solution)/shard_map/ppermute | solution.py:603
  61.3 9.7 %collective-permute-start.8 = (bf16[4,16,512]{2,1,0:T(8,128)(2,1)S(1)}, bf16[4,16,512]{2,1,0:T(8,128)(2,1)S(1)}, u32[]{:S(2)}, u32[]{:S(2)}) collective-permute-start(bf16[4,16,512]{2,1,0:T(8,128)(2,1)S(1)} %get-tuple-element.35), channel_id=1, source_target_pairs={{0,6},{2,4},{4,2},{6,0},{8,14},{10,12},{12,10},{14,8},{16,22},{18,... | collective-permute-start | bytes 196616 | tf_op jit(solution)/shard_map/ppermute | solution.py:603
  72.5 20.5 %collective-permute-start.9 = (bf16[16,512]{1,0:T(8,128)(2,1)S(1)}, bf16[16,512]{1,0:T(8,128)(2,1)S(1)}, u32[]{:S(2)}, u32[]{:S(2)}) collective-permute-start(bf16[16,512]{1,0:T(8,128)(2,1)S(1)} %get-tuple-element.37), channel_id=1, source_target_pairs={{0,8},{2,10},{4,12},{6,14},{8,0},{10,2},{12,4},{14,6},{16,24},{18,... | collective-permute-start | bytes 49160 | tf_op jit(solution)/shard_map/ppermute | solution.py:603
  73.7 24.9 %collective-permute-start.10 = (bf16[16,512]{1,0:T(8,128)(2,1)S(1)}, bf16[16,512]{1,0:T(8,128)(2,1)S(1)}, u32[]{:S(2)}, u32[]{:S(2)}) collective-permute-start(bf16[16,512]{1,0:T(8,128)(2,1)S(1)} %get-tuple-element.38), channel_id=1, source_target_pairs={{0,16},{2,18},{4,20},{6,22},{8,24},{10,26},{12,28},{14,30},{16,0},... | collective-permute-start | bytes 49160 | tf_op jit(solution)/shard_map/ppermute | solution.py:603
  91.9 6.7 %collective-permute-start.11 = (bf16[16,512]{1,0:T(8,128)(2,1)S(1)}, bf16[16,512]{1,0:T(8,128)(2,1)S(1)}, u32[]{:S(2)}, u32[]{:S(2)}) collective-permute-start(bf16[16,512]{1,0:T(8,128)(2,1)S(1)} %get-tuple-element.39), channel_id=1, source_target_pairs={{0,24},{2,26},{4,28},{6,30},{8,16},{10,18},{12,20},{14,22},{16,8},... | collective-permute-start | bytes 49160 | tf_op jit(solution)/shard_map/ppermute | solution.py:603
  100.0 5.5 %collective-permute-start.12 = (bf16[8,1024]{1,0:T(8,128)(2,1)S(1)}, bf16[8,1024]{1,0:T(8,128)(2,1)S(1)}, u32[]{:S(2)}, u32[]{:S(2)}) collective-permute-start(bf16[8,1024]{1,0:T(8,128)(2,1)S(1)} %get-tuple-element.42), channel_id=1, source_target_pairs={{0,1},{1,0},{2,3},{3,2},{4,5},{5,4},{6,7},{7,6},{8,9},{9,8},{10,11... | collective-permute-start | bytes 49160 | tf_op jit(solution)/shard_map/ppermute | solution.py:603

commit v5 on v4

--- a/solution.py
+++ b/solution.py
@@ -181,7 +181,7 @@
     total = 0
     for cut, load in enumerate(loads):
         load.wait()
-        total = lax.fori_loop(edges[cut], edges[cut + 1], send, total)
+        total = lax.fori_loop(edges[cut], edges[cut + 1], send, total, unroll=4)
     wait_pages(out_ref.at[0], out_ref.at[0, pl.ds(0, 2)], capacity, total, send_sem)
 
 
@@ -272,49 +272,59 @@
     )(table, kv_pool, key_new, value_new, after, ready)
 
 
-LAND_CUTS = 7
-
-
 def land_body(
     row_count, capacity, table_ref, arrived_ref, key_ref, value_ref, begun_ref, out_ref, mark_ref,
     held_ref, load_sem, sem,
 ):
     places = table_ref.shape[1]
-    edges = [places * cut // LAND_CUTS for cut in range(LAND_CUTS + 1)]
-    loads = []
-    for cut in range(LAND_CUTS):
-        span = pl.ds(2 * edges[cut], 2 * (edges[cut + 1] - edges[cut]))
-        load = pltpu.make_async_copy(arrived_ref.at[span], held_ref.at[span], load_sem.at[cut])
-        load.start()
-        loads.append(load)
+    senders = places // capacity
+
+    def load_of(sender):
+        span = pl.ds(2 * capacity * sender, 2 * capacity)
+        return pltpu.make_async_copy(
+            arrived_ref.at[span], held_ref.at[span], load_sem.at[sender]
+        )
+
+    for sender in range(senders):
+
+        @pl.when(table_ref[5, sender * capacity] > 0)
+        def _(sender=sender):
+            load_of(sender).start()
+
     mark_ref[...] = jnp.zeros_like(mark_ref)
-
-    def send(place, count):
-        slot = table_ref[0, place]
+    for sender in range(senders):
+
+        @pl.when(table_ref[5, sender * capacity] > 0)
+        def _(sender=sender):
+            load_of(sender).wait()
+            for place in range(sender * capacity, (sender + 1) * capacity):
+                plain = table_ref[0, place]
+
+                @pl.when(plain >= 0)
+                def _(place=place, plain=plain):
+                    pltpu.make_async_copy(
+                        held_ref.at[pl.ds(2 * place, 2)], out_ref.at[:, plain], sem
+                    ).start()
+
+    def patch(place, carry):
         req = table_ref[1, place]
 
-        @pl.when(slot >= 0)
+        @pl.when(req >= 0)
         def _():
-            @pl.when(req >= 0)
-            def _():
-                first = table_ref[2, place]
-                for which, fresh_ref in ((0, key_ref), (1, value_ref)):
-                    held_ref[2 * place + which] = patched(
-                        held_ref[2 * place + which], fresh_ref, row_count, req, first
-                    )
-
+            first = table_ref[2, place]
+            for which, fresh_ref in ((0, key_ref), (1, value_ref)):
+                held_ref[2 * place + which] = patched(
+                    held_ref[2 * place + which], fresh_ref, row_count, req, first
+                )
             pltpu.make_async_copy(
-                held_ref.at[pl.ds(2 * place, 2)], out_ref.at[:, slot], sem
+                held_ref.at[pl.ds(2 * place, 2)], out_ref.at[:, table_ref[3, place]], sem
             ).start()
 
-        return count + (slot >= 0).astype(jnp.int32)
-
-    count = 0
-    for cut, load in enumerate(loads):
-        load.wait()
-        count = lax.fori_loop(edges[cut], edges[cut + 1], send, count)
+        return carry
+
+    lax.fori_loop(0, places, patch, 0, unroll=4)
     group = held_ref.at[pl.ds(0, 2 * capacity)]
-    wait_pages(group, held_ref.at[pl.ds(0, 2)], capacity, count, sem)
+    wait_pages(group, held_ref.at[pl.ds(0, 2)], capacity, table_ref[4, 0], sem)
 
 
 def place_landed(row_count, table, begun, arrived, key_new, value_new):
@@ -330,7 +340,7 @@
         out_specs=(hbm, vmem),
         scratch_shapes=[
             pltpu.VMEM(arrived.shape, begun.dtype),
-            pltpu.SemaphoreType.DMA((LAND_CUTS,)),
+            pltpu.SemaphoreType.DMA((arrived.shape[0] // (2 * capacity),)),
             pltpu.SemaphoreType.DMA,
         ],
         input_output_aliases={4: 0},
@@ -628,7 +638,11 @@
         return jnp.where(hit, request, -1), first
 
     slot = pick(inner)
-    by_place = jnp.stack([slot, *fresh(pick(req), pick(page))])
+    new_req, first = fresh(pick(req), pick(page))
+    count = jnp.broadcast_to(jnp.sum((slot >= 0).astype(jnp.int32)), slot.shape)
+    sends = jnp.repeat(jnp.sum(to_me.astype(jnp.int32), axis=1), capacity)
+    plain = jnp.where(new_req < 0, slot, -1)
+    by_place = jnp.stack([plain, new_req, first, slot, count, sends])
     landed = jnp.any(slot[None, :] == jnp.arange(slot_count, dtype=jnp.int32)[:, None], axis=1)
     stays = slot_dest < 0
     kind = jnp.where(landed, LANDED, jnp.where(stays, KEPT, BLANK))

time: 106 us -> 106 us (level)
  waiting for transfers between devices: 25.5 us -> 22.2 us
  local copies, waits for them, and re-layouts: 3.22 us -> 6.08 us
    ppermute x13, waiting for transfers between devices: 25.5 us -> 22.2 us  [swap_all(): lax.ppermute(parts[k], axis, pairs[k])]
    unnamed x23 -> x25, local copies, waits for them, and re-layouts: 2.24 us -> 4.28 us
  transfers between devices with their start and end apart: 14 -> 14, of which waited for: 4 -> 5; matrix products, arithmetic and copies ran while one was open for 7% -> 9% of each run, Pallas kernels for 20% -> 19%
where the time goes in v5:
time: 106 us
  starting transfers between devices  39.4 us (37%)
  Pallas kernels  22.6 us (21%)
  waiting for transfers between devices  22.2 us (21%)
  blocking collectives  6.96 us (7%)
  local copies, waits for them, and re-layouts  6.08 us (6%)
  matrix products  3.85 us (4%)
  other arithmetic  3.81 us (4%)
    ppermute x13, starting transfers between devices, swap_all(): lax.ppermute(parts[k], axis, pairs[k])  33.2 us
    ppermute x13, waiting for transfers between devices, swap_all(): lax.ppermute(parts[k], axis, pairs[k])  22.2 us
    all_gather x1, blocking collectives, local(): all_tokens = lax.all_gather(seq_tokens, 'tp', axis=1, tiled=True)  6.96 us
    all_to_all x1, starting transfers between devices, local(): lax.all_to_all(outgoing, 'seq', split_axis=0, concat_axis=0, tiled=True)  6.2 us
    pallas_call x1, Pallas kernels, attend(): pl.pallas_call(functools.partial(attend_body, kv_count, group_size, seq_c...  5.46 us
    pallas_call x1, Pallas kernels, place_kept(): pl.pallas_call(functools.partial(keep_body, row_count), out_shape=(jax.Sh...  5.23 us
    unnamed x25, local copies, waits for them, and re-layouts  4.28 us
    pallas_call x1, Pallas kernels, place_landed(): pl.pallas_call(functools.partial(land_body, row_count, capacity), out_sha...  3.69 us
  transfers between devices with their start and end apart: 14, of which 5 were waited for; matrix products, arithmetic and copies ran while one was open for 9% of the time, Pallas kernels for 19%

profile of v5, /device:TPU:5, one launch (start us, length us, event | category | flops | bytes accessed | tf_op | source)
XLA Modules:
  0.0 105.9 jit_solution(793650149058744663)
XLA Ops:
  0.6 1.4 %make_note.1 = bf16[8,1024]{1,0:T(8,128)(2,1)} custom-call(bf16[6,1024]{1,0:T(8,128)(2,1)} %token_ref.1, s32[1,112]{1,0:T(1,128)} %bitcast.74, s32[2,112]{1,0:T(2,128)} %bitcast.73), custom_call_target="tpu_custom_call" | custom-call | tf_op jit(solution)/shard_map/make_note/pallas_call | solution.py:88
  2.0 3.3 %collective-permute-start.2 = (bf16[8,1024]{1,0:T(8,128)(2,1)}, bf16[8,1024]{1,0:T(8,128)(2,1)S(1)}, u32[]{:S(2)}, u32[]{:S(2)}) collective-permute-start(bf16[8,1024]{1,0:T(8,128)(2,1)} %make_note.1), channel_id=1, source_target_pairs={{0,24},{2,26},{4,28},{6,30},{8,16},{10,18},{12,20},{14,22},{16,8},... | collective-permute-start | bytes 49160 | tf_op jit(solution)/shard_map/ppermute | solution.py:613
  5.3 0.3 collective-permute-start
  5.6 2.7 %pack_pages.1 = bf16[16,14,16,512]{3,2,1,0:T(8,128)(2,1)} custom-call(s32[112]{0:T(128)} %dest_ref.1, bf16[2,112,16,512]{3,2,1,0:T(8,128)(2,1)} %pool_ref.5), custom_call_target="tpu_custom_call" | custom-call | bytes 7340032 | tf_op jit(solution)/shard_map/pack_pages/pallas_call | solution.py:192
  8.4 0.6 collective-permute-done.1
  9.0 6.2 %all-to-all-start = ((bf16[16,14,16,512]{3,2,1,0:T(8,128)(2,1)}), bf16[16,14,16,512]{3,2,1,0:T(8,128)(2,1)}, u32[]{:S(2)}, u32[]{:S(2)}) async-start(bf16[16,14,16,512]{3,2,1,0:T(8,128)(2,1)} %pack_pages.1), calls=%async_computation | async-start | bytes 7340032 | tf_op jit(solution)/shard_map/all_to_all | solution.py:669
  15.3 1.2 %collective-permute-start.5 = (bf16[4,8,1024]{2,1,0:T(8,128)(2,1)S(1)}, bf16[4,8,1024]{2,1,0:T(8,128)(2,1)S(1)}, u32[]{:S(2)}, u32[]{:S(2)}) collective-permute-start(bf16[4,8,1024]{2,1,0:T(8,128)(2,1)S(1)} %pad_maximum_fusion.2.refs_0_), channel_id=1, source_target_pairs={{0,6},{2,4},{4,2},{6,0},{8,14},{10,12},{12,10},{14,8},{16,22},{18,... | collective-permute-start | bytes 196616 | tf_op jit(solution)/shard_map/ppermute | solution.py:613
  16.6 1.2 %collective-permute-start.4 = (bf16[4,8,1024]{2,1,0:T(8,128)(2,1)S(1)}, bf16[4,8,1024]{2,1,0:T(8,128)(2,1)S(1)}, u32[]{:S(2)}, u32[]{:S(2)}) collective-permute-start(bf16[4,8,1024]{2,1,0:T(8,128)(2,1)S(1)} %pad_maximum_fusion.2.refs_0_), channel_id=1, source_target_pairs={{0,4},{2,6},{4,0},{6,2},{8,12},{10,14},{12,8},{14,10},{16,20},{18,... | collective-permute-start | bytes 196616 | tf_op jit(solution)/shard_map/ppermute | solution.py:613
  17.8 0.3 collective-permute-start.3
  18.1 0.3 multiply_cosine_fusion
  18.5 8.5 %collective-permute-done.5.refs_3_ = bf16[4,8,1024]{2,1,0:T(8,128)(2,1)S(1)} collective-permute-done((bf16[4,8,1024]{2,1,0:T(8,128)(2,1)S(1)}, bf16[4,8,1024]{2,1,0:T(8,128)(2,1)S(1)}, u32[]{:S(2)}, u32[]{:S(2)}) %collective-permute-start.5) | collective-permute-done | bytes 65568 | tf_op jit(solution)/shard_map/ppermute | solution.py:613
  26.9 6.9 %collective-permute-done.4.refs_2_ = bf16[4,8,1024]{2,1,0:T(8,128)(2,1)S(1)} collective-permute-done((bf16[4,8,1024]{2,1,0:T(8,128)(2,1)S(1)}, bf16[4,8,1024]{2,1,0:T(8,128)(2,1)S(1)}, u32[]{:S(2)}, u32[]{:S(2)}) %collective-permute-start.4) | collective-permute-done | bytes 65568 | tf_op jit(solution)/shard_map/ppermute | solution.py:613
  33.9 0.6 sort_notes.1
  34.6 0.4 slice_add_fusion.1
  35.0 0.3 reduce_window_sum.14
  35.3 0.4 select_reduce_fusion.1
  35.7 0.6 convert_reduce_fusion.1
  37.0 0.1 stack_reshape.3
  37.2 0.1 fusion.8
  37.4 0.1 select_reduce_fusion.3
  37.5 0.1 fusion.9
  37.7 7.0 %all_gather.3 = bf16[128,2048]{1,0:T(8,128)(2,1)S(1)} all-gather(bf16[128,1024]{1,0:T(8,128)(2,1)S(1)} %bitcast.59), channel_id=1, replica_groups=mesh['seq'=16,'tp'=2] {'tp'}, dimensions={1}, use_global_device_ids=true | all-gather | bytes 786432 | tf_op jit(solution)/shard_map/all_gather | solution.py:672
  44.7 0.2 fusion
  44.9 3.1 %convolution_bitcast_fusion = f32[16,8,8,128]{3,1,2,0:T(8,128)S(1)} fusion(bf16[2048,1024]{1,0:T(8,128)(2,1)} %param.13, bf16[128,2048]{1,0:T(8,128)(2,1)S(1)} %all_gather.3, f32[2048]{0:T(1024)S(1)} %copy-done.5, f32[128]{0:T(128)S(1)} %add_rsqrt_fusion), kind=kOutput, calls=%fused_computation.2 | convolution fusion | flops 537919488 | bytes 5251584 | tf_op jit(solution)/shard_map/dot_general | solution.py:57
  48.0 0.1 copy.22
  48.1 0.3 subtract_convert_fusion
  48.4 0.1 pad_maximum_fusion
  48.6 0.8 convolution_bitcast_fusion.1
  49.4 0.1 reshape_squeeze.3
  49.5 0.3 subtract_convert_fusion.1
  49.8 0.2 pad_maximum_fusion.1
  50.1 2.0 %copy-done = bf16[2,112,16,512]{3,2,1,0:T(8,128)(2,1)S(1)} copy-done((bf16[2,112,16,512]{3,2,1,0:T(8,128)(2,1)S(1)}, bf16[2,112,16,512]{3,2,1,0:T(8,128)(2,1)}, u32[]{:S(2)}) %copy-start) | copy-done | bytes 3670040
  52.1 5.5 %attend.1 = (bf16[4,16,512]{2,1,0:T(8,128)(2,1)S(1)}, bf16[4,16,512]{2,1,0:T(8,128)(2,1)S(1)}, bf16[4,16,512]{2,1,0:T(8,128)(2,1)S(1)}, bf16[4,16,512]{2,1,0:T(8,128)(2,1)S(1)}) custom-call(s32[2]{0:T(128)S(1)} %pad_add_fusion.1.index_ref, bf16[128,1024]{1,0:T(8,128)(2,1)S(1)} %bitcast.60, bf16[128,512]{1,0:T(8,128)(2,1)S(1)} %get-tuple-element.64.key_new_ref, ...), custom_call_target="tpu_custom_call" | custom-call | flops 939524096 | bytes 7340032 | tf_op jit(solution)/shard_map/attend/pallas_call | solution.py:447
  57.6 2.3 %collective-permute-start.6 = (bf16[4,16,512]{2,1,0:T(8,128)(2,1)S(1)}, bf16[4,16,512]{2,1,0:T(8,128)(2,1)S(1)}, u32[]{:S(2)}, u32[]{:S(2)}) collective-permute-start(bf16[4,16,512]{2,1,0:T(8,128)(2,1)S(1)} %get-tuple-element.33), channel_id=1, source_target_pairs={{0,2},{2,0},{4,6},{6,4},{8,10},{10,8},{12,14},{14,12},{16,18},{18,... | collective-permute-start | bytes 196616 | tf_op jit(solution)/shard_map/ppermute | solution.py:613
  59.8 2.2 %collective-permute-start.7 = (bf16[4,16,512]{2,1,0:T(8,128)(2,1)S(1)}, bf16[4,16,512]{2,1,0:T(8,128)(2,1)S(1)}, u32[]{:S(2)}, u32[]{:S(2)}) collective-permute-start(bf16[4,16,512]{2,1,0:T(8,128)(2,1)S(1)} %get-tuple-element.34), channel_id=1, source_target_pairs={{0,4},{2,6},{4,0},{6,2},{8,12},{10,14},{12,8},{14,10},{16,20},{18,... | collective-permute-start | bytes 196616 | tf_op jit(solution)/shard_map/ppermute | solution.py:613
  62.0 0.6 stack_broadcast_in_dim.3
  62.8 2.0 %copy-done.1 = bf16[2,112,16,512]{3,2,1,0:T(8,128)(2,1)S(1)} copy-done((bf16[2,112,16,512]{3,2,1,0:T(8,128)(2,1)S(1)}, bf16[2,112,16,512]{3,2,1,0:T(8,128)(2,1)}, u32[]{:S(2)}) %copy-start.1) | copy-done | bytes 3670040
  64.8 5.2 %place_kept.1 = (bf16[2,112,16,512]{3,2,1,0:T(8,128)(2,1)}, f32[8,128]{1,0:T(8,128)S(1)}) custom-call(s32[3,112]{1,0:T(4,128)S(1)} %pad_add_fusion.table_ref, bf16[2,112,16,512]{3,2,1,0:T(8,128)(2,1)S(1)} %copy-done.1, f32[128,512]{1,0:T(8,128)S(1)} %get-tuple-element.65.key_ref, f32[128,512]{1,0:T(8,128)S(1)} %get-tuple-element.50.value_ref, ...), custom_call_target="tpu_custom_call" | custom-call | bytes 11010048 | tf_op jit(solution)/shard_map/place_kept/pallas_call | solution.py:262
  70.0 0.6 collective-permute-done.8.rest_3_
  70.6 1.5 %merge.1 = (bf16[16,512]{1,0:T(8,128)(2,1)S(1)}, bf16[16,512]{1,0:T(8,128)(2,1)S(1)}, bf16[16,512]{1,0:T(8,128)(2,1)S(1)}, bf16[16,512]{1,0:T(8,128)(2,1)S(1)}, bf16[1024,2048]{1,0:T(8,128)(2,1)S(1)}) custom-call(s32[2]{0:T(128)S(1)} %pad_add_fusion.1.index_ref, f32[8,128]{1,0:T(8,128)S(1)} %get-tuple-element.32.mark_ref, bf16[1024,2048]{1,0:T(8,128)(2,1)S(1)} %copy-done.2, ...), custom_call_target="tpu_custom_call" | custom-call | bytes 6291456 | tf_op jit(solution)/shard_map/merge/pallas_call | solution.py:542
  72.2 1.2 %collective-permute-start.9 = (bf16[16,512]{1,0:T(8,128)(2,1)S(1)}, bf16[16,512]{1,0:T(8,128)(2,1)S(1)}, u32[]{:S(2)}, u32[]{:S(2)}) collective-permute-start(bf16[16,512]{1,0:T(8,128)(2,1)S(1)} %get-tuple-element.37), channel_id=1, source_target_pairs={{0,8},{2,10},{4,12},{6,14},{8,0},{10,2},{12,4},{14,6},{16,24},{18,... | collective-permute-start | bytes 49160 | tf_op jit(solution)/shard_map/ppermute | solution.py:613
  73.4 18.1 %collective-permute-start.10 = (bf16[16,512]{1,0:T(8,128)(2,1)S(1)}, bf16[16,512]{1,0:T(8,128)(2,1)S(1)}, u32[]{:S(2)}, u32[]{:S(2)}) collective-permute-start(bf16[16,512]{1,0:T(8,128)(2,1)S(1)} %get-tuple-element.38), channel_id=1, source_target_pairs={{0,16},{2,18},{4,20},{6,22},{8,24},{10,26},{12,28},{14,30},{16,0},... | collective-permute-start | bytes 49160 | tf_op jit(solution)/shard_map/ppermute | solution.py:613
  91.5 1.1 %collective-permute-start.11 = (bf16[16,512]{1,0:T(8,128)(2,1)S(1)}, bf16[16,512]{1,0:T(8,128)(2,1)S(1)}, u32[]{:S(2)}, u32[]{:S(2)}) collective-permute-start(bf16[16,512]{1,0:T(8,128)(2,1)S(1)} %get-tuple-element.39), channel_id=1, source_target_pairs={{0,24},{2,26},{4,28},{6,30},{8,16},{10,18},{12,20},{14,22},{16,8},... | collective-permute-start | bytes 49160 | tf_op jit(solution)/shard_map/ppermute | solution.py:613
  92.6 5.6 %collective-permute-done.10.refs_2_ = bf16[16,512]{1,0:T(8,128)(2,1)S(1)} collective-permute-done((bf16[16,512]{1,0:T(8,128)(2,1)S(1)}, bf16[16,512]{1,0:T(8,128)(2,1)S(1)}, u32[]{:S(2)}, u32[]{:S(2)}) %collective-permute-start.10) | collective-permute-done | bytes 16416 | tf_op jit(solution)/shard_map/ppermute | solution.py:613
  98.2 1.4 %combine.1 = (bf16[8,1024]{1,0:T(8,128)(2,1)S(1)}, bf16[8,1024]{1,0:T(8,128)(2,1)S(1)}) custom-call(s32[2]{0:T(128)S(1)} %pad_add_fusion.1.index_ref, bf16[16,512]{1,0:T(8,128)(2,1)S(1)} %get-tuple-element.36.refs_0_, bf16[16,512]{1,0:T(8,128)(2,1)S(1)} %collective-permute-done.9.refs_1_, bf16[16,512]{1,0:T(8,128)(2,1)S(1)} %collective-permute-done.10.refs_2_, ...), custom_call_target="tpu_custom_call" | custom-call | bytes 8388608 | tf_op jit(solution)/shard_map/combine/pallas_call | solution.py:580
  99.6 1.9 %collective-permute-start.12 = (bf16[8,1024]{1,0:T(8,128)(2,1)S(1)}, bf16[8,1024]{1,0:T(8,128)(2,1)S(1)}, u32[]{:S(2)}, u32[]{:S(2)}) collective-permute-start(bf16[8,1024]{1,0:T(8,128)(2,1)S(1)} %get-tuple-element.42), channel_id=1, source_target_pairs={{0,1},{1,0},{2,3},{3,2},{4,5},{5,4},{6,7},{7,6},{8,9},{9,8},{10,11... | collective-permute-start | bytes 49160 | tf_op jit(solution)/shard_map/ppermute | solution.py:613
  101.6 3.7 %place_landed.1 = (bf16[2,112,16,512]{3,2,1,0:T(8,128)(2,1)}, f32[8,128]{1,0:T(8,128)S(1)}) custom-call(s32[6,112]{1,0:T(8,128)S(1)} %stack.49.ready_ref.table_ref, bf16[224,16,512]{2,1,0:T(8,128)(2,1)} %bitcast.12.arrived_ref, f32[128,512]{1,0:T(8,128)S(1)} %get-tuple-element.65.key_ref, ...), custom_call_target="tpu_custom_call", output_to_operand_aliasing={{0}: (4, {})} | custom-call | bytes 11010048 | tf_op jit(solution)/shard_map/place_landed/pallas_call | solution.py:336
  105.3 0.6 close.1
  (66 shorter events, 1.5 us)
Async XLA Ops:
  2.0 6.4 %collective-permute-start.2 = (bf16[8,1024]{1,0:T(8,128)(2,1)}, bf16[8,1024]{1,0:T(8,128)(2,1)S(1)}, u32[]{:S(2)}, u32[]{:S(2)}) collective-permute-start(bf16[8,1024]{1,0:T(8,128)(2,1)} %make_note.1), channel_id=1, source_target_pairs={{0,24},{2,26},{4,28},{6,30},{8,16},{10,18},{12,20},{14,22},{16,8},... | collective-permute-start | bytes 49160 | tf_op jit(solution)/shard_map/ppermute | solution.py:613
  5.3 3.7 %collective-permute-start.1 = (bf16[8,1024]{1,0:T(8,128)(2,1)}, bf16[8,1024]{1,0:T(8,128)(2,1)S(1)}, u32[]{:S(2)}, u32[]{:S(2)}) collective-permute-start(bf16[8,1024]{1,0:T(8,128)(2,1)} %make_note.1), channel_id=1, source_target_pairs={{0,16},{2,18},{4,20},{6,22},{8,24},{10,26},{12,28},{14,30},{16,0},... | collective-permute-start | bytes 49160 | tf_op jit(solution)/shard_map/ppermute | solution.py:613
  5.3 3.7 %collective-permute-start = (bf16[8,1024]{1,0:T(8,128)(2,1)}, bf16[8,1024]{1,0:T(8,128)(2,1)S(1)}, u32[]{:S(2)}, u32[]{:S(2)}) collective-permute-start(bf16[8,1024]{1,0:T(8,128)(2,1)} %make_note.1), channel_id=1, source_target_pairs={{0,8},{2,10},{4,12},{6,14},{8,0},{10,2},{12,4},{14,6},{16,24},{18,... | collective-permute-start | bytes 49160 | tf_op jit(solution)/shard_map/ppermute | solution.py:613
  8.3 7.0 %copy-start.6 = (s32[112,2]{0,1:T(2,128)S(1)}, s32[112,2]{0,1:T(2,128)}, u32[]{:S(2)}) copy-start(s32[112,2]{0,1:T(2,128)} %param.17) | copy-start | bytes 2692
  8.3 7.0 %copy-start.4 = (bf16[8,1024]{1,0:T(8,128)(2,1)S(1)}, bf16[8,1024]{1,0:T(8,128)(2,1)}, u32[]{:S(2)}) copy-start(bf16[8,1024]{1,0:T(8,128)(2,1)} %make_note.1) | copy-start | bytes 49156
  8.3 9.7 %copy-start.8 = (s32[24]{0:T(128)S(1)}, s32[24]{0:T(128)}, u32[]{:S(2)}) copy-start(s32[24]{0:T(128)} %param.19) | copy-start | bytes 292
  8.4 9.7 %copy-start.10 = (s32[128]{0:T(128)S(1)}, s32[128]{0:T(128)}, u32[]{:S(2)}) copy-start(s32[128]{0:T(128)} %constant.63.clone) | copy-start | bytes 1540
  8.4 9.8 %copy-start.9 = (s32[128]{0:T(128)S(1)}, s32[128]{0:T(128)}, u32[]{:S(2)}) copy-start(s32[128]{0:T(128)} %constant.64.clone) | copy-start | bytes 1540
  8.4 29.0 %copy-start.7 = (s32[112]{0:T(128)S(1)}, s32[112]{0:T(128)}, u32[]{:S(2)}) copy-start(s32[112]{0:T(128)} %dest_ref.1) | copy-start | bytes 1348
  8.4 36.5 %copy-start.5 = (f32[2048]{0:T(1024)S(1)}, f32[2048]{0:T(1024)}, u32[]{:S(2)}) copy-start(f32[2048]{0:T(1024)} %param.12) | copy-start | bytes 24580
  9.0 92.6 %all-to-all-start = ((bf16[16,14,16,512]{3,2,1,0:T(8,128)(2,1)}), bf16[16,14,16,512]{3,2,1,0:T(8,128)(2,1)}, u32[]{:S(2)}, u32[]{:S(2)}) async-start(bf16[16,14,16,512]{3,2,1,0:T(8,128)(2,1)} %pack_pages.1), calls=%async_computation | async-start | bytes 7340032 | tf_op jit(solution)/shard_map/all_to_all | solution.py:669
  15.3 11.6 %collective-permute-start.5 = (bf16[4,8,1024]{2,1,0:T(8,128)(2,1)S(1)}, bf16[4,8,1024]{2,1,0:T(8,128)(2,1)S(1)}, u32[]{:S(2)}, u32[]{:S(2)}) collective-permute-start(bf16[4,8,1024]{2,1,0:T(8,128)(2,1)S(1)} %pad_maximum_fusion.2.refs_0_), channel_id=1, source_target_pairs={{0,6},{2,4},{4,2},{6,0},{8,14},{10,12},{12,10},{14,8},{16,22},{18,... | collective-permute-start | bytes 196616 | tf_op jit(solution)/shard_map/ppermute | solution.py:613
  16.6 17.3 %collective-permute-start.4 = (bf16[4,8,1024]{2,1,0:T(8,128)(2,1)S(1)}, bf16[4,8,1024]{2,1,0:T(8,128)(2,1)S(1)}, u32[]{:S(2)}, u32[]{:S(2)}) collective-permute-start(bf16[4,8,1024]{2,1,0:T(8,128)(2,1)S(1)} %pad_maximum_fusion.2.refs_0_), channel_id=1, source_target_pairs={{0,4},{2,6},{4,0},{6,2},{8,12},{10,14},{12,8},{14,10},{16,20},{18,... | collective-permute-start | bytes 196616 | tf_op jit(solution)/shard_map/ppermute | solution.py:613
  17.8 16.1 %collective-permute-start.3 = (bf16[4,8,1024]{2,1,0:T(8,128)(2,1)S(1)}, bf16[4,8,1024]{2,1,0:T(8,128)(2,1)S(1)}, u32[]{:S(2)}, u32[]{:S(2)}) collective-permute-start(bf16[4,8,1024]{2,1,0:T(8,128)(2,1)S(1)} %pad_maximum_fusion.2.refs_0_), channel_id=1, source_target_pairs={{0,2},{2,0},{4,6},{6,4},{8,10},{10,8},{12,14},{14,12},{16,18},{18,... | collective-permute-start | bytes 196616 | tf_op jit(solution)/shard_map/ppermute | solution.py:613
  44.9 3.7 %copy-start.3 = (bf16[2,2048,512]{2,1,0:T(8,128)(2,1)S(1)}, bf16[2,2048,512]{2,1,0:T(8,128)(2,1)}, u32[]{:S(2)}) copy-start(bf16[2,2048,512]{2,1,0:T(8,128)(2,1)} %param.14) | copy-start | bytes 12582916
  50.1 2.0 %copy-start = (bf16[2,112,16,512]{3,2,1,0:T(8,128)(2,1)S(1)}, bf16[2,112,16,512]{3,2,1,0:T(8,128)(2,1)}, u32[]{:S(2)}) copy-start(bf16[2,112,16,512]{3,2,1,0:T(8,128)(2,1)} %pool_ref.5) | copy-start | bytes 11010052
  57.6 12.5 %collective-permute-start.6 = (bf16[4,16,512]{2,1,0:T(8,128)(2,1)S(1)}, bf16[4,16,512]{2,1,0:T(8,128)(2,1)S(1)}, u32[]{:S(2)}, u32[]{:S(2)}) collective-permute-start(bf16[4,16,512]{2,1,0:T(8,128)(2,1)S(1)} %get-tuple-element.33), channel_id=1, source_target_pairs={{0,2},{2,0},{4,6},{6,4},{8,10},{10,8},{12,14},{14,12},{16,18},{18,... | collective-permute-start | bytes 196616 | tf_op jit(solution)/shard_map/ppermute | solution.py:613
  59.8 10.2 %collective-permute-start.7 = (bf16[4,16,512]{2,1,0:T(8,128)(2,1)S(1)}, bf16[4,16,512]{2,1,0:T(8,128)(2,1)S(1)}, u32[]{:S(2)}, u32[]{:S(2)}) collective-permute-start(bf16[4,16,512]{2,1,0:T(8,128)(2,1)S(1)} %get-tuple-element.34), channel_id=1, source_target_pairs={{0,4},{2,6},{4,0},{6,2},{8,12},{10,14},{12,8},{14,10},{16,20},{18,... | collective-permute-start | bytes 196616 | tf_op jit(solution)/shard_map/ppermute | solution.py:613
  62.0 8.6 %collective-permute-start.8 = (bf16[4,16,512]{2,1,0:T(8,128)(2,1)S(1)}, bf16[4,16,512]{2,1,0:T(8,128)(2,1)S(1)}, u32[]{:S(2)}, u32[]{:S(2)}) collective-permute-start(bf16[4,16,512]{2,1,0:T(8,128)(2,1)S(1)} %get-tuple-element.35), channel_id=1, source_target_pairs={{0,6},{2,4},{4,2},{6,0},{8,14},{10,12},{12,10},{14,8},{16,22},{18,... | collective-permute-start | bytes 196616 | tf_op jit(solution)/shard_map/ppermute | solution.py:613
  62.7 2.0 %copy-start.1 = (bf16[2,112,16,512]{3,2,1,0:T(8,128)(2,1)S(1)}, bf16[2,112,16,512]{3,2,1,0:T(8,128)(2,1)}, u32[]{:S(2)}) copy-start(bf16[2,112,16,512]{3,2,1,0:T(8,128)(2,1)} %pool_ref.5) | copy-start | bytes 11010052
  64.8 5.8 %copy-start.2 = (bf16[1024,2048]{1,0:T(8,128)(2,1)S(1)}, bf16[1024,2048]{1,0:T(8,128)(2,1)}, u32[]{:S(2)}) copy-start(bf16[1024,2048]{1,0:T(8,128)(2,1)} %weight_ref.1) | copy-start | bytes 12582916
  72.2 20.5 %collective-permute-start.9 = (bf16[16,512]{1,0:T(8,128)(2,1)S(1)}, bf16[16,512]{1,0:T(8,128)(2,1)S(1)}, u32[]{:S(2)}, u32[]{:S(2)}) collective-permute-start(bf16[16,512]{1,0:T(8,128)(2,1)S(1)} %get-tuple-element.37), channel_id=1, source_target_pairs={{0,8},{2,10},{4,12},{6,14},{8,0},{10,2},{12,4},{14,6},{16,24},{18,... | collective-permute-start | bytes 49160 | tf_op jit(solution)/shard_map/ppermute | solution.py:613
  73.4 24.8 %collective-permute-start.10 = (bf16[16,512]{1,0:T(8,128)(2,1)S(1)}, bf16[16,512]{1,0:T(8,128)(2,1)S(1)}, u32[]{:S(2)}, u32[]{:S(2)}) collective-permute-start(bf16[16,512]{1,0:T(8,128)(2,1)S(1)} %get-tuple-element.38), channel_id=1, source_target_pairs={{0,16},{2,18},{4,20},{6,22},{8,24},{10,26},{12,28},{14,30},{16,0},... | collective-permute-start | bytes 49160 | tf_op jit(solution)/shard_map/ppermute | solution.py:613
  91.5 6.7 %collective-permute-start.11 = (bf16[16,512]{1,0:T(8,128)(2,1)S(1)}, bf16[16,512]{1,0:T(8,128)(2,1)S(1)}, u32[]{:S(2)}, u32[]{:S(2)}) collective-permute-start(bf16[16,512]{1,0:T(8,128)(2,1)S(1)} %get-tuple-element.39), channel_id=1, source_target_pairs={{0,24},{2,26},{4,28},{6,30},{8,16},{10,18},{12,20},{14,22},{16,8},... | collective-permute-start | bytes 49160 | tf_op jit(solution)/shard_map/ppermute | solution.py:613
  99.6 5.6 %collective-permute-start.12 = (bf16[8,1024]{1,0:T(8,128)(2,1)S(1)}, bf16[8,1024]{1,0:T(8,128)(2,1)S(1)}, u32[]{:S(2)}, u32[]{:S(2)}) collective-permute-start(bf16[8,1024]{1,0:T(8,128)(2,1)S(1)} %get-tuple-element.42), channel_id=1, source_target_pairs={{0,1},{1,0},{2,3},{3,2},{4,5},{5,4},{6,7},{7,6},{8,9},{9,8},{10,11... | collective-permute-start | bytes 49160 | tf_op jit(solution)/shard_map/ppermute | solution.py:613
